TPU v7x, 32 devices: a whole 2x2x4 slice. The times are simulated.
32 devices in a mesh: dp: 4 (over y, x), fsdp: 8 (over z, core).
Axes of the slice: x: 2, y: 2, z: 4, core: 2. Of those that a mesh axis runs over, the one named last changes fastest.
Arguments:
- mlp_input: bfloat16 [256, 4096], P('dp', 'fsdp'), may hold values from -6 to 6
- residual_in: bfloat16 [256, 4096], P(('dp', 'fsdp')), may hold values from -6 to 6
- gate_weight: bfloat16 [4096, 14336], P(None, 'fsdp'), may hold values from -0.09375 to 0.09375
- up_weight: bfloat16 [4096, 14336], P(None, 'fsdp'), may hold values from -0.09375 to 0.09375
- down_weight: bfloat16 [14336, 4096], P('fsdp'), may hold values from -0.046875 to 0.046875
- span_index: bfloat16 [16384, 4096], P(('dp', 'fsdp')), may hold values from -6 to 6
- positive_keys: bfloat16 [256, 4096], P(('dp', 'fsdp')), may hold values from -6 to 6
- request_rows: int32 [32, 32, 32], P(None, ('dp', 'fsdp')), may hold values from 0 to 511, as said below
- request_counts: int32 [32, 32], P(None, ('dp', 'fsdp')), may hold values from 0 to 32, as said below
- negative_slots: int32 [256, 64], P(('dp', 'fsdp')), may hold values from 0 to 1023, as said below
Outputs:
- query_loss: float32 [256], P(('dp', 'fsdp'))
- input_grad: bfloat16 [256, 4096], P('dp', 'fsdp')
- gate_grad: bfloat16 [4096, 14336], P('dp', 'fsdp')
- up_grad: bfloat16 [4096, 14336], P('dp', 'fsdp')
- down_grad: bfloat16 [14336, 4096], P('fsdp', 'dp')
Inputs may be any that keep to these rules, and one draw needn't show every extreme that they name: `request_rows`: entry [r, o, s] is a local row of shard o; it is read only where s < request_counts[r, o]. `request_counts`: for each requesting device r the counts over the 32 shards sum to 512, and some shard gets exactly 32. `negative_slots`: rows q of device r = q // 8; an entry o * 32 + s names slot s of shard o with s < request_counts[r, o]; the 512 entries of a device use each such slot exactly once.
All inputs are finite; a program needn't handle non-finite values.
Results may differ from a plain program's by a relative error of at most 0.017.
Values may be sent and summed in bfloat16 or wider, within the bound.
No kernel may reach another device: no remote copies, remote signals or barrier semaphores. Data moves between devices by JAX's collectives and lax.ppermute only.
A program may use at most 192 MiB of HBM per device.

v0:
```python
import jax
import jax.numpy as jnp
from jax import lax
from jax.sharding import PartitionSpec as P

inverse_temp = 50.0
eps = 1e-06
contract_first = (((0,), (0,)), ((), ()))
contract_last = (((1,), (1,)), ((), ()))


def silu_grad(gate_act):
    sigmoid_gate = jax.nn.sigmoid(gate_act)
    return sigmoid_gate * (1.0 + gate_act * (1.0 - sigmoid_gate))


def contrast(unit_rows, row_norm, key_block):
    key_unit = key_block / jnp.sqrt(jnp.sum(key_block * key_block, axis=-1, keepdims=True) + eps)
    scores = inverse_temp * jnp.einsum(
        "qd,qnd->qn", unit_rows, key_unit, precision=lax.Precision.HIGHEST
    )
    weights = jnp.exp(scores)
    exp_total = jnp.sum(weights, axis=-1)
    query_loss = jnp.log(exp_total) - scores[:, 0]
    column = lax.broadcasted_iota(jnp.int32, scores.shape, 1)
    coeffs = weights / exp_total[:, None] - (column == 0).astype(scores.dtype)
    pull_term = inverse_temp * jnp.einsum(
        "qn,qnd->qd", coeffs, key_unit, precision=lax.Precision.HIGHEST
    )
    inner_term = jnp.sum(coeffs * scores, axis=-1)
    head_grad = ((pull_term - inner_term[:, None] * unit_rows) / row_norm[:, None]).astype(
        jnp.bfloat16
    )
    return (query_loss, head_grad)


def shards(
    mlp_input,
    residual_in,
    gate_weight,
    up_weight,
    down_weight,
    span_index,
    positive_keys,
    request_rows,
    request_counts,
    negative_slots,
):
    dp_count = lax.axis_size("dp")
    fsdp_count = lax.axis_size("fsdp")
    owners = dp_count * fsdp_count
    slot_cap = request_rows.shape[2]
    feature_width = span_index.shape[1]
    whole_input = lax.all_gather(mlp_input, "fsdp", axis=1, tiled=True)
    gate_act = jnp.dot(whole_input, gate_weight, preferred_element_type=jnp.float32)
    up_act = jnp.dot(whole_input, up_weight, preferred_element_type=jnp.float32)
    hidden = (jax.nn.silu(gate_act) * up_act).astype(jnp.bfloat16)
    branch = lax.psum_scatter(
        jnp.dot(hidden, down_weight, preferred_element_type=jnp.float32).astype(jnp.bfloat16),
        "fsdp",
        scatter_dimension=0,
        tiled=True,
    ).astype(jnp.float32)
    top_state = branch + residual_in.astype(jnp.float32)
    row_norm = jnp.sqrt(jnp.sum(top_state * top_state, axis=-1) + eps)
    unit_rows = top_state / row_norm[:, None]
    row_table = request_rows[:, 0, :]
    count_table = request_counts[:, 0]
    picked = jnp.take(span_index, row_table.reshape(-1), axis=0).reshape(
        owners, slot_cap, feature_width
    )
    live_mask = lax.broadcasted_iota(jnp.int32, (owners, slot_cap), 1) < count_table[:, None]
    picked = jnp.where(live_mask[..., None], picked, jnp.zeros_like(picked))
    buffer = lax.all_to_all(picked, ("dp", "fsdp"), split_axis=0, concat_axis=0, tiled=True)
    flat_buffer = buffer.reshape(owners * slot_cap, feature_width)
    fetched = jnp.take(flat_buffer, negative_slots.reshape(-1), axis=0)
    fetched = fetched.reshape(
        negative_slots.shape[0], negative_slots.shape[1], feature_width
    ).astype(jnp.float32)
    key_block = jnp.concatenate([positive_keys.astype(jnp.float32)[:, None, :], fetched], axis=1)
    query_loss, head_grad = contrast(unit_rows, row_norm, key_block)
    gathered_grad = lax.all_gather(head_grad, "fsdp", axis=0, tiled=True)
    hidden_grad = lax.dot_general(
        gathered_grad, down_weight, contract_last, preferred_element_type=jnp.float32
    )
    gate_grad_act = (hidden_grad * up_act * silu_grad(gate_act)).astype(jnp.bfloat16)
    up_grad_act = (hidden_grad * jax.nn.silu(gate_act)).astype(jnp.bfloat16)
    input_term = lax.dot_general(
        gate_grad_act, gate_weight, contract_last, preferred_element_type=jnp.float32
    ) + lax.dot_general(up_grad_act, up_weight, contract_last, preferred_element_type=jnp.float32)
    input_grad = lax.psum_scatter(
        input_term.astype(jnp.bfloat16), "fsdp", scatter_dimension=1, tiled=True
    )
    gate_term = lax.dot_general(
        whole_input, gate_grad_act, contract_first, preferred_element_type=jnp.float32
    )
    up_term = lax.dot_general(
        whole_input, up_grad_act, contract_first, preferred_element_type=jnp.float32
    )
    down_term = lax.dot_general(
        hidden, gathered_grad, contract_first, preferred_element_type=jnp.float32
    )
    gate_sum, up_sum = (
        lax.psum_scatter(
            gate_term.astype(jnp.bfloat16), "dp", scatter_dimension=0, tiled=True
        ).astype(jnp.float32),
        lax.psum_scatter(
            up_term.astype(jnp.bfloat16), "dp", scatter_dimension=0, tiled=True
        ).astype(jnp.float32),
    )
    down_sum = lax.psum_scatter(
        down_term.astype(jnp.bfloat16), "dp", scatter_dimension=1, tiled=True
    )
    gate_grad = gate_sum.astype(jnp.bfloat16)
    up_grad = up_sum.astype(jnp.bfloat16)
    return (query_loss, input_grad, gate_grad, up_grad, down_sum)


def solution(mesh):
    return jax.shard_map(
        shards,
        mesh=mesh,
        in_specs=(
            P("dp", "fsdp"),
            P(("dp", "fsdp"), None),
            P(None, "fsdp"),
            P(None, "fsdp"),
            P("fsdp", None),
            P(("dp", "fsdp"), None),
            P(("dp", "fsdp"), None),
            P(None, ("dp", "fsdp"), None),
            P(None, ("dp", "fsdp")),
            P(("dp", "fsdp"), None),
        ),
        out_specs=(
            P(("dp", "fsdp")),
            P("dp", "fsdp"),
            P("dp", "fsdp"),
            P("dp", "fsdp"),
            P("fsdp", "dp"),
        ),
        check_vma=False,
    )
```

profile of v0, /device:TPU:0, one launch (start us, length us, event | category | flops | bytes accessed | tf_op | source)
XLA Modules:
  0.0 812.0 jit_solution(11343145795055637390)
XLA Ops:
  10.0 17.8 %gather_fusion = bf16[1024,4096]{1,0:T(8,128)(2,1)} fusion(bf16[512,4096]{1,0:T(8,128)(2,1)} %param.15, s32[1024]{0:T(1024)S(1)} %broadcast_clamp_fusion), kind=kCustom, calls=%fused_computation | custom fusion | bytes 16781312 | tf_op jit(solution)/shard_map/jit(_take)/gather | solution.py:69
  27.8 7.4 select_select_fusion
  35.2 7.4 all-to-all-start
  42.7 191.5 %all_gather.6 = bf16[64,4096]{1,0:T(8,128)(2,1)S(1)} all-gather(bf16[64,512]{1,0:T(8,128)(2,1)S(1)} %copy-done.3), channel_id=1, replica_groups=mesh['dp'=4,'fsdp'=8] {'fsdp'}, dimensions={1}, use_global_device_ids=true | all-gather | bytes 589824 | tf_op jit(solution)/shard_map/all_gather | solution.py:54
  234.2 7.9 fusion.19
  242.2 8.0 multiply_convert_fusion.2
  250.2 3.5 convolution_convert_fusion.3
  254.2 31.1 %reduce-scatter.6.cloned.1.call-done = bf16[8,4096]{1,0:T(8,128)(2,1)} async-done(((bf16[64,4096]{1,0:T(8,128)(2,1)}), bf16[8,4096]{1,0:T(8,128)(2,1)}) %reduce-scatter.6.cloned.1.call-update) | async-done | bytes 65552 | tf_op jit(solution)/shard_map/reduce_scatter | solution.py:58
  287.3 13.0 %gather_fusion.1 = bf16[512,4096]{1,0:T(8,128)(2,1)} fusion(bf16[1024,4096]{1,0:T(8,128)(2,1)} %bitcast.6, s32[1024]{0:T(1024)S(1)} %pad_clamp_fusion), kind=kCustom, calls=%fused_computation.1 | custom fusion | bytes 8390656 | tf_op jit(solution)/shard_map/jit(_take)/gather | solution.py:76
  305.2 8.5 %fusion.4 = f32[8,1,65]{2,1,0:T(1,128)S(1)} fusion(f32[8,65]{1,0:T(8,128)S(1)} %add_sqrt_fusion, bf16[8,64,4096]{2,1,0:T(8,128)(2,1)S(1)} %broadcast_select_fusion, bf16[8,1,4096]{2,1,0:T(2,128)(2,1)S(1)} %copy.15, f32[8,4096,1]{1,0,2:T(8,128)S(1)} %fusion.15), kind=kOutput, calls=%fused_computation.12 | convolution fusion | flops 36208640 | bytes 4395072 | tf_op jit(solution)/shard_map/qd,qnd->qn/dot_general | solution.py:19
  314.0 7.8 fusion.3
  321.9 15.0 %all_gather.7 = bf16[64,4096]{1,0:T(8,128)(2,1)S(1)} all-gather(bf16[8,4096]{1,0:T(8,128)(2,1)S(1)} %fusion.11), channel_id=1, replica_groups=mesh['dp'=4,'fsdp'=8] {'fsdp'}, dimensions={0}, use_global_device_ids=true | all-gather | bytes 589824 | tf_op jit(solution)/shard_map/all_gather | solution.py:82
  336.9 9.8 %multiply_convert_fusion = (bf16[64,1792]{1,0:T(8,128)(2,1)S(1)}, bf16[64,1792]{1,0:T(8,128)(2,1)S(1)}) fusion(f32[64,1792]{1,0:T(8,128)S(1)} %fusion.19, f32[64,1792]{1,0:T(8,128)S(1)} %get-tuple-element.16, bf16[64,4096]{1,0:T(8,128)(2,1)S(1)} %all_gather.7, bf16[1792,4096]{1,0:T(8,128)(2,1)} %param.14), kind=kOutput, calls=%fused_computation.20 | convolution fusion | flops 941015040 | bytes 16580608 | tf_op jit(solution)/shard_map/dot_general | solution.py:83
  346.7 7.2 fusion.1
  354.0 8.0 fusion
  362.3 9.7 %fusion.20 = f32[64,4096]{1,0:T(8,128)S(1)} fusion(bf16[64,1792]{1,0:T(8,128)(2,1)S(1)} %get-tuple-element.11, bf16[4096,1792]{1,0:T(8,128)(2,1)} %param.12), kind=kOutput, calls=%fused_computation.56 | convolution fusion | flops 939524096 | bytes 15958016 | tf_op jit(solution)/shard_map/dot_general | solution.py:88
  372.0 10.9 %fusion.7 = bf16[64,4096]{1,0:T(8,128)(2,1)} fusion(f32[64,4096]{1,0:T(8,128)S(1)} %fusion.20, bf16[64,1792]{1,0:T(8,128)(2,1)S(1)} %get-tuple-element.10, bf16[4096,1792]{1,0:T(8,128)(2,1)} %param.13), kind=kOutput, calls=%fused_computation.17 | convolution fusion | flops 940048384 | bytes 16482304 | tf_op jit(solution)/shard_map/dot_general | solution.py:90
  383.0 7.4 convolution_convert_fusion
  390.9 99.4 %reduce-scatter.12.cloned.1.call-done = bf16[1024,1792]{0,1:T(8,128)(2,1)} async-done(((bf16[4096,1792]{0,1:T(8,128)(2,1)}), bf16[1024,1792]{0,1:T(8,128)(2,1)}) %reduce-scatter.12.cloned.1.call-update) | async-done | bytes 3670032 | tf_op jit(solution)/shard_map/reduce_scatter | solution.py:107
  490.3 5.9 copy.17
  496.2 135.4 %reduce-scatter.10.cloned.1.call-done = bf16[1024,1792]{0,1:T(8,128)(2,1)} async-done(((bf16[4096,1792]{0,1:T(8,128)(2,1)}), bf16[1024,1792]{0,1:T(8,128)(2,1)}) %reduce-scatter.10.cloned.1.call-update) | async-done | bytes 3670032 | tf_op jit(solution)/shard_map/reduce_scatter | solution.py:104
  631.6 5.9 copy.16
  637.5 27.8 %reduce-scatter.8.cloned.1.call-done = bf16[64,512]{1,0:T(8,128)(2,1)} async-done(((bf16[64,4096]{1,0:T(8,128)(2,1)}), bf16[64,512]{1,0:T(8,128)(2,1)}) %reduce-scatter.8.cloned.1.call-update) | async-done | bytes 65552 | tf_op jit(solution)/shard_map/reduce_scatter | solution.py:91
  665.3 139.7 %reduce-scatter.14.cloned.1.call-done = bf16[1792,1024]{1,0:T(8,128)(2,1)} async-done(((bf16[1792,4096]{1,0:T(8,128)(2,1)}), bf16[1792,1024]{1,0:T(8,128)(2,1)}) %reduce-scatter.14.cloned.1.call-update) | async-done | bytes 3670032 | tf_op jit(solution)/shard_map/reduce_scatter | solution.py:111
  (56 shorter events, 11.5 us)
Async XLA Ops:
  35.2 7.5 copy-start.3
  35.2 252.0 %all-to-all-start = ((bf16[32,32,4096]{2,1,0:T(8,128)(2,1)}), bf16[32,32,4096]{2,1,0:T(8,128)(2,1)}, u32[]{:S(2)}, u32[]{:S(2)}) async-start(bf16[32,32,4096]{2,1,0:T(8,128)(2,1)} %select_select_fusion), calls=%async_computation.1 | async-start | bytes 16777216 | tf_op jit(solution)/shard_map/all_to_all | solution.py:74
  42.7 242.7 %reduce-scatter.6.cloned.1.call-start = ((), (), s32[]{:S(2)}) async-start(), calls=%async_computation.6 | async-start | bytes 589824 | tf_op jit(solution)/shard_map/reduce_scatter | solution.py:58
  234.2 16.0 %slice-start = ((s8[14680064]{0:T(1024)(128)(4,1)}), s8[4194304]{0:T(1024)(128)(4,1)S(1)}, s32[]{:S(2)}) async-start(s8[14680064]{0:T(1024)(128)(4,1)} %bitcast.55), calls=%async_computation.11 | async-start | bytes 8388608
  234.2 16.0 %slice-start.1 = ((s8[14680064]{0:T(1024)(128)(4,1)}), s8[4194304]{0:T(1024)(128)(4,1)S(1)}, s32[]{:S(2)}) async-start(s8[14680064]{0:T(1024)(128)(4,1)} %bitcast.55), calls=%async_computation.12 | async-start | bytes 8388608
  234.2 16.0 %slice-start.2 = ((s8[14680064]{0:T(1024)(128)(4,1)}), s8[4194304]{0:T(1024)(128)(4,1)S(1)}, s32[]{:S(2)}) async-start(s8[14680064]{0:T(1024)(128)(4,1)} %bitcast.55), calls=%async_computation.13 | async-start | bytes 8388608
  242.1 8.0 slice-start.3
  250.2 3.8 copy-start.5
  250.2 3.9 copy-start.4
  250.2 35.1 %copy-start.1 = (bf16[8,4096]{1,0:T(8,128)(2,1)S(1)}, bf16[8,4096]{1,0:T(8,128)(2,1)}, u32[]{:S(2)}) copy-start(bf16[8,4096]{1,0:T(8,128)(2,1)} %param.11) | copy-start | bytes 196612
  253.8 236.5 %reduce-scatter.12.cloned.1.call-start = ((), (), s32[]{:S(2)}) async-start(), calls=%async_computation.9 | async-start | bytes 18350080 | tf_op jit(solution)/shard_map/reduce_scatter | solution.py:107
  303.0 2.2 copy-start
  314.0 7.8 copy-start.2
  353.9 277.7 %reduce-scatter.10.cloned.1.call-start = ((), (), s32[]{:S(2)}) async-start(), calls=%async_computation.8 | async-start | bytes 18350080 | tf_op jit(solution)/shard_map/reduce_scatter | solution.py:104
  362.0 303.3 %reduce-scatter.8.cloned.1.call-start = ((), (), s32[]{:S(2)}) async-start(), calls=%async_computation.7 | async-start | bytes 589824 | tf_op jit(solution)/shard_map/reduce_scatter | solution.py:91
  382.9 422.1 %reduce-scatter.14.cloned.1.call-start = ((), (), s32[]{:S(2)}) async-start(), calls=%async_computation.10 | async-start | bytes 18350080 | tf_op jit(solution)/shard_map/reduce_scatter | solution.py:111
Sparse Core Ops, SparseCore 0:
  253.9 31.4 reduce-scatter.5
  354.1 136.1 reduce-scatter.11
  493.7 137.8 reduce-scatter.9
  634.4 30.8 reduce-scatter.7
  668.8 136.1 reduce-scatter.13
where the time goes:
time: 820 us; the launch traced here: 812 us
  waiting for transfers between devices  434 us (53%)
  blocking collectives  206 us (25%)
  matrix products  88.7 us (11%)
  local copies, waits for them, and re-layouts  43.7 us (5%)
  other arithmetic  17.2 us (2%)
  between operations  14.4 us (2%)
    all_gather x1, blocking collectives, shards(): whole_input = lax.all_gather(mlp_input, 'fsdp', axis=1, tiled=True)  191 us
    reduce_scatter x1, waiting for transfers between devices, shards(): lax.psum_scatter(down_term.astype(jnp.bfloat16), 'dp', scatter_dimension=...  140 us
    reduce_scatter x1, waiting for transfers between devices, shards(): lax.psum_scatter(gate_term.astype(jnp.bfloat16), 'dp', scatter_dimension=...  135 us
    reduce_scatter x1, waiting for transfers between devices, shards(): lax.psum_scatter(up_term.astype(jnp.bfloat16), 'dp', scatter_dimension=0,...  99.4 us
    reduce_scatter x1, waiting for transfers between devices, shards(): lax.psum_scatter(jnp.dot(hidden, down_weight, preferred_element_type=jnp....  31.1 us
    reduce_scatter x1, waiting for transfers between devices, shards(): lax.psum_scatter(input_term.astype(jnp.bfloat16), 'fsdp', scatter_dimensi...  27.8 us
    gather x1, local copies, waits for them, and re-layouts, shards(): jnp.take(span_index, row_table.reshape(-1), axis=0)  17.8 us
  transfers between devices with their start and end apart: 6, of which 5 were waited for; matrix products, arithmetic and copies ran while one was open for 9% of the time, Pallas kernels for 0%

commit v1 on v0

v1 whole, which is shorter than its diff:
```python
import jax
import jax.numpy as jnp
from jax import lax
from jax.sharding import PartitionSpec as P

inverse_temp = 50.0
eps = 1e-06
contract_first = (((0,), (0,)), ((), ()))
contract_last = (((1,), (1,)), ((), ()))
every = ("dp", "fsdp")


def silu_grad(gate_act):
    sigmoid_gate = jax.nn.sigmoid(gate_act)
    return sigmoid_gate * (1.0 + gate_act * (1.0 - sigmoid_gate))


def dot32(left, right, dims=(((1,), (0,)), ((), ()))):
    return lax.dot_general(left, right, dims, preferred_element_type=jnp.float32)


def norm_of(rows):
    return jnp.sqrt(jnp.sum(rows * rows, axis=-1) + eps)


def sum_to_owner(partial, axis, parts):
    pieces = lax.all_to_all(partial, axis, split_axis=0, concat_axis=0, tiled=True)
    pieces = pieces.reshape(parts, partial.shape[0] // parts, partial.shape[1])
    return jnp.sum(pieces.astype(jnp.float32), axis=0)


def use_counts(all_slots, row_table, count_table, me, shard_rows):
    owners, slot_cap = row_table.shape
    queries = all_slots.shape[0]
    slot = lax.broadcasted_iota(jnp.int32, (1, 1, slot_cap), 2) + me * slot_cap
    asked = jnp.sum((all_slots[:, :, None] == slot).astype(jnp.float32), axis=1)
    asked = asked.reshape(owners, queries // owners, slot_cap)
    live = lax.broadcasted_iota(jnp.int32, (owners, 1, slot_cap), 2) < count_table[:, None, None]
    used = jnp.where(live, asked, 0.0)
    dead = jnp.sum(asked - used, axis=-1).reshape(queries)
    row = lax.broadcasted_iota(jnp.int32, (1, 1, shard_rows), 2)
    picks = (row_table[:, :, None] == row).astype(jnp.bfloat16)
    counts = lax.dot_general(
        used.astype(jnp.bfloat16),
        picks,
        (((2,), (1,)), ((0,), (0,))),
        preferred_element_type=jnp.float32,
    )
    return counts.reshape(queries, shard_rows), dead


def shards(
    mlp_input,
    residual_in,
    gate_weight,
    up_weight,
    down_weight,
    span_index,
    positive_keys,
    request_rows,
    request_counts,
    negative_slots,
):
    dp_count = lax.axis_size("dp")
    fsdp_count = lax.axis_size("fsdp")
    owners = dp_count * fsdp_count
    me = lax.axis_index(every)
    width = span_index.shape[1]

    whole_input = lax.all_gather(mlp_input, "fsdp", axis=1, tiled=True)
    gate_act = dot32(whole_input, gate_weight)
    up_act = dot32(whole_input, up_weight)
    hidden = (jax.nn.silu(gate_act) * up_act).astype(jnp.bfloat16)
    branch = sum_to_owner(dot32(hidden, down_weight).astype(jnp.bfloat16), "fsdp", fsdp_count)
    top_state = branch + residual_in.astype(jnp.float32)
    row_norm = norm_of(top_state)
    unit_rows = top_state / row_norm[:, None]

    all_slots = lax.all_gather(negative_slots, every, axis=0, tiled=True)
    counts, dead = use_counts(
        all_slots, request_rows[:, 0, :], request_counts[:, 0], me, span_index.shape[0]
    )
    span_values = span_index.astype(jnp.float32)
    span_norm = norm_of(span_values)
    all_states = lax.all_gather(top_state.astype(jnp.bfloat16), "fsdp", axis=0, tiled=True)
    all_states = lax.all_gather(all_states, "dp", axis=0, tiled=True)
    state_norm = norm_of(all_states.astype(jnp.float32))
    raw_scores = dot32(all_states, span_index, contract_last)
    scores = inverse_temp * raw_scores / state_norm[:, None] / span_norm[None, :]
    weights = counts * jnp.exp(scores)
    shard_total = jnp.sum(weights, axis=-1) + dead
    shard_pull = dot32((weights / span_norm[None, :]).astype(jnp.bfloat16), span_index)

    total_high = shard_total.astype(jnp.bfloat16)
    total_low = (shard_total - total_high.astype(jnp.float32)).astype(jnp.bfloat16)
    column = lax.broadcasted_iota(jnp.int32, (shard_total.shape[0], 128), 1)
    totals = jnp.where(column == 0, total_high[:, None], jnp.where(column == 1, total_low[:, None], 0))
    sums = sum_to_owner(
        jnp.concatenate([shard_pull.astype(jnp.bfloat16), totals.astype(jnp.bfloat16)], axis=1),
        every,
        owners,
    )
    negative_total = sums[:, width] + sums[:, width + 1]
    positive_rows = positive_keys.astype(jnp.float32)
    positive_unit = positive_rows / norm_of(positive_rows)[:, None]
    positive_score = inverse_temp * jnp.sum(unit_rows * positive_unit, axis=-1)
    exp_total = jnp.exp(positive_score) + negative_total
    query_loss = jnp.log(exp_total) - positive_score
    pull = (sums[:, :width] - negative_total[:, None] * positive_unit) / exp_total[:, None]
    inner = jnp.sum(pull * unit_rows, axis=-1)
    head_grad = (
        inverse_temp * (pull - inner[:, None] * unit_rows) / row_norm[:, None]
    ).astype(jnp.bfloat16)

    gathered_grad = lax.all_gather(head_grad, "fsdp", axis=0, tiled=True)
    hidden_grad = dot32(gathered_grad, down_weight, contract_last)
    gate_grad_act = (hidden_grad * up_act * silu_grad(gate_act)).astype(jnp.bfloat16)
    up_grad_act = (hidden_grad * jax.nn.silu(gate_act)).astype(jnp.bfloat16)
    input_term = dot32(gate_grad_act, gate_weight, contract_last) + dot32(
        up_grad_act, up_weight, contract_last
    )
    input_grad = lax.psum_scatter(
        input_term.astype(jnp.bfloat16), "fsdp", scatter_dimension=1, tiled=True
    )

    def columns_of_all(rows):
        return lax.all_to_all(rows, "dp", split_axis=1, concat_axis=0, tiled=True)

    def rows_of_all(rows):
        return lax.all_gather(rows, "dp", axis=0, tiled=True)

    input_columns = columns_of_all(whole_input)
    grad_columns = columns_of_all(gathered_grad)
    down_grad = dot32(rows_of_all(hidden), grad_columns, contract_first).astype(jnp.bfloat16)
    gate_grad = dot32(input_columns, rows_of_all(gate_grad_act), contract_first).astype(jnp.bfloat16)
    up_grad = dot32(input_columns, rows_of_all(up_grad_act), contract_first).astype(jnp.bfloat16)
    return (query_loss, input_grad, gate_grad, up_grad, down_grad)


def solution(mesh):
    return jax.shard_map(
        shards,
        mesh=mesh,
        in_specs=(
            P("dp", "fsdp"),
            P(("dp", "fsdp"), None),
            P(None, "fsdp"),
            P(None, "fsdp"),
            P("fsdp", None),
            P(("dp", "fsdp"), None),
            P(("dp", "fsdp"), None),
            P(None, ("dp", "fsdp"), None),
            P(None, ("dp", "fsdp")),
            P(("dp", "fsdp"), None),
        ),
        out_specs=(
            P(("dp", "fsdp")),
            P("dp", "fsdp"),
            P("dp", "fsdp"),
            P("dp", "fsdp"),
            P("fsdp", "dp"),
        ),
        check_vma=False,
    )
```

time: 820 us -> 297 us (0.36)
  waiting for transfers between devices: 434 us -> 37.7 us
  blocking collectives: 206 us -> 144 us
  matrix products: 88.7 us -> 60 us
  local copies, waits for them, and re-layouts: 43.7 us -> 16.6 us
    reduce_scatter x4 -> x0, waiting for transfers between devices: 406 us -> none  [the longest x1 140 us: shards(): lax.psum_scatter(down_term.astype(jnp.bfloat16), 'dp', scatter_dimension=...]
    all_gather x1, blocking collectives: 191 us -> 16.8 us  [shards(): whole_input = lax.all_gather(mlp_input, 'fsdp', axis=1, tiled=True)]
    all_gather x0 -> x5, blocking collectives: none -> 112 us  [the longest x3 55.2 us: rows_of_all(): return lax.all_gather(rows, 'dp', axis=0, tiled=True)]
    all_to_all x1 -> x4, waiting for transfers between devices: 0.01 us -> 37.6 us  [the longest x2 37.6 us: sum_to_owner(): lax.all_to_all(partial, axis, split_axis=0, concat_axis=0, tiled=True)]
    gather x2 -> x0, local copies, waits for them, and re-layouts: 30.9 us -> none  [the longest x1 17.8 us: shards(): jnp.take(span_index, row_table.reshape(-1), axis=0)]
    dot_general x11 -> x12, matrix products: 88.7 us -> 60 us  [the longest x11 59.4 us: dot32(): lax.dot_general(left, right, dims, preferred_element_type=jnp.float32)]
    reduce_scatter x1, waiting for transfers between devices: 27.8 us -> 0.01 us  [shards(): lax.psum_scatter(input_term.astype(jnp.bfloat16), 'fsdp', scatter_dimensi...]
    select_n x4 -> x1, other arithmetic: 10 us -> 0.13 us  [shards(): jnp.where(column == 0, total_high[:, None], jnp.where(column == 1, total_...]
  transfers between devices with their start and end apart: 6 -> 6, of which waited for: 5 -> 2; matrix products, arithmetic and copies ran while one was open for 9% -> 20% of each run, Pallas kernels for 0% -> 0%
where the time goes in v1:
time: 297 us; the launch traced here: 296 us
  blocking collectives  144 us (48%)
  matrix products  60 us (20%)
  waiting for transfers between devices  37.7 us (13%)
  local copies, waits for them, and re-layouts  16.6 us (6%)
  starting transfers between devices  14.4 us (5%)
  between operations  14.3 us (5%)
  other arithmetic  9.31 us (3%)
    dot_general x11, matrix products, dot32(): lax.dot_general(left, right, dims, preferred_element_type=jnp.float32)  59.4 us
    all_gather x3, blocking collectives, rows_of_all(): return lax.all_gather(rows, 'dp', axis=0, tiled=True)  55.2 us
    all_gather x1, blocking collectives, shards(): all_slots = lax.all_gather(negative_slots, every, axis=0, tiled=True)  40.7 us
    all_to_all x2, waiting for transfers between devices, sum_to_owner(): lax.all_to_all(partial, axis, split_axis=0, concat_axis=0, tiled=True)  37.6 us
    all_gather x1, blocking collectives, shards(): whole_input = lax.all_gather(mlp_input, 'fsdp', axis=1, tiled=True)  16.8 us
    all_gather x1, blocking collectives, shards(): lax.all_gather(top_state.astype(jnp.bfloat16), 'fsdp', axis=0, tiled=True)  15.7 us
    all_gather x1, blocking collectives, shards(): gathered_grad = lax.all_gather(head_grad, 'fsdp', axis=0, tiled=True)  15.2 us
    unnamed x28, local copies, waits for them, and re-layouts  14.6 us
  transfers between devices with their start and end apart: 6, of which 2 were waited for; matrix products, arithmetic and copies ran while one was open for 20% of the time, Pallas kernels for 0%

profile of v1, /device:TPU:0, one launch (start us, length us, event | category | flops | bytes accessed | tf_op | source)
XLA Modules:
  0.0 295.9 jit_solution(5243264349445211836)
XLA Ops:
  7.2 16.8 %all_gather.24 = bf16[64,4096]{1,0:T(8,128)(2,1)S(1)} all-gather(bf16[64,512]{1,0:T(8,128)(2,1)} %param.10), channel_id=1, replica_groups=mesh['dp'=4,'fsdp'=8] {'fsdp'}, dimensions={1}, use_global_device_ids=true | all-gather | bytes 589824 | tf_op jit(solution)/shard_map/all_gather | solution.py:70
  24.0 7.9 %fusion.22 = f32[64,1792]{1,0:T(8,128)S(1)} fusion(bf16[64,4096]{1,0:T(8,128)(2,1)S(1)} %all_gather.24, bf16[4096,1792]{1,0:T(8,128)(2,1)} %param.12), kind=kOutput, calls=%fused_computation.68 | convolution fusion | flops 939524096 | bytes 15663104 | tf_op jit(solution)/shard_map/dot_general | solution.py:19
  33.3 3.5 %multiply_convert_fusion.2 = (bf16[64,1792]{1,0:T(8,128)(2,1)S(1)}, f32[64,1792]{1,0:T(8,128)}) fusion(f32[64,1792]{1,0:T(8,128)S(1)} %fusion.22, bf16[64,4096]{1,0:T(8,128)(2,1)S(1)} %all_gather.24, bf16[4096,1792]{1,0:T(8,128)(2,1)S(1)} %copy-done), kind=kOutput, calls=%fused_computation.29 | convolution fusion | flops 940212224 | bytes 16351232 | tf_op jit(solution)/shard_map/dot_general | solution.py:19
  38.0 3.5 %fusion.1 = bf16[8,8,4096]{2,1,0:T(8,128)(2,1)} fusion(bf16[64,1792]{1,0:T(8,128)(2,1)S(1)} %get-tuple-element.55, bf16[1792,4096]{1,0:T(8,128)(2,1)S(1)} %bitcast.58), kind=kOutput, calls=%fused_computation.5 | convolution fusion | flops 939786240 | bytes 15433728 | tf_op jit(solution)/shard_map/dot_general | solution.py:19
  41.5 4.6 %all-to-all-start = ((bf16[8,8,4096]{2,1,0:T(8,128)(2,1)}), bf16[8,8,4096]{2,1,0:T(8,128)(2,1)S(1)}, u32[]{:S(2)}, u32[]{:S(2)}) async-start(bf16[8,8,4096]{2,1,0:T(8,128)(2,1)} %fusion.1), calls=%async_computation | async-start | bytes 1048576 | tf_op jit(solution)/shard_map/all_to_all | solution.py:27
  46.4 15.1 %all-to-all-done = bf16[8,8,4096]{2,1,0:T(8,128)(2,1)S(1)} async-done(((bf16[8,8,4096]{2,1,0:T(8,128)(2,1)}), bf16[8,8,4096]{2,1,0:T(8,128)(2,1)S(1)}, u32[]{:S(2)}, u32[]{:S(2)}) %all-to-all-start) | async-done | bytes 524320 | tf_op jit(solution)/shard_map/all_to_all | solution.py:27
  62.0 15.7 %all_gather.26 = bf16[64,4096]{1,0:T(8,128)(2,1)} all-gather(bf16[8,4096]{1,0:T(8,128)(2,1)S(1)} %get-tuple-element.51), channel_id=1, replica_groups=mesh['dp'=4,'fsdp'=8] {'fsdp'}, dimensions={0}, use_global_device_ids=true | all-gather | bytes 589824 | tf_op jit(solution)/shard_map/all_gather | solution.py:85
  77.8 40.7 %all_gather.25 = s32[256,64]{1,0:T(8,128)S(1)} all-gather(s32[8,64]{1,0:T(8,128)S(1)} %copy-done.7), channel_id=1, replica_groups=mesh['dp'=4,'fsdp'=8] {'dp','fsdp'}, dimensions={0}, use_global_device_ids=true | all-gather | bytes 67584 | tf_op jit(solution)/shard_map/all_gather | solution.py:79
  119.3 3.1 %multiply_reduce_fusion = f32[512]{0:T(512)S(1)} fusion(bf16[512,4096]{1,0:T(8,128)(2,1)} %param.15), kind=kLoop, calls=%fused_computation | loop fusion | flops 6290944 | bytes 4196352 | tf_op jit(solution)/shard_map/reduce_sum | solution.py:23
  124.5 4.3 %fusion.8 = f32[256,512]{1,0:T(8,128)S(1)} fusion(bf16[256,4096]{1,0:T(8,128)(2,1)} %all-gather.2.cloned.1.call-done, bf16[512,4096]{1,0:T(8,128)(2,1)} %param.15, f32[512]{0:T(512)S(1)} %add_sqrt_fusion, f32[256]{0:T(256)S(1)} %add_sqrt_fusion.1), kind=kOutput, calls=%fused_computation.21 | convolution fusion | flops 1074135040 | bytes 6818816 | tf_op jit(solution)/shard_map/dot_general | solution.py:19
  136.0 28.1 %all_gather.31 = bf16[256,1792]{1,0:T(8,128)(2,1)} all-gather(bf16[64,1792]{1,0:T(8,128)(2,1)S(1)} %get-tuple-element.55), channel_id=1, replica_groups=mesh['dp'=4,'fsdp'=8] {'dp'}, dimensions={0}, use_global_device_ids=true | all-gather | bytes 1146880 | tf_op jit(solution)/shard_map/all_gather | solution.py:130
  164.1 22.5 %all-to-all-done.1 = bf16[32,8,4224]{2,1,0:T(8,128)(2,1)S(1)} async-done(((bf16[32,8,4224]{2,1,0:T(8,128)(2,1)}), bf16[32,8,4224]{2,1,0:T(8,128)(2,1)S(1)}, u32[]{:S(2)}, u32[]{:S(2)}) %all-to-all-start.1) | async-done | bytes 2162720 | tf_op jit(solution)/shard_map/all_to_all | solution.py:27
  186.6 3.5 %all-to-all-start.2 = ((bf16[64,4,1024]{2,0,1:T(8,128)(2,1)}), bf16[64,4,1024]{2,0,1:T(8,128)(2,1)S(1)}, u32[]{:S(2)}, u32[]{:S(2)}) async-start(bf16[64,4,1024]{2,0,1:T(8,128)(2,1)} %bitcast.64), calls=%async_computation.3 | async-start | bytes 1048576 | tf_op jit(solution)/shard_map/all_to_all | solution.py:127
  191.0 15.2 %all_gather.28 = bf16[64,4096]{1,0:T(8,128)(2,1)S(1)} all-gather(bf16[8,4096]{1,0:T(8,128)(2,1)S(1)} %divide_convert_fusion.2), channel_id=1, replica_groups=mesh['dp'=4,'fsdp'=8] {'fsdp'}, dimensions={0}, use_global_device_ids=true | all-gather | bytes 589824 | tf_op jit(solution)/shard_map/all_gather | solution.py:115
  206.2 9.9 %multiply_convert_fusion = (bf16[64,1792]{1,0:T(8,128)(2,1)S(1)}, bf16[64,1792]{1,0:T(8,128)(2,1)S(1)}) fusion(f32[64,1792]{1,0:T(8,128)} %copy-done.3, f32[64,1792]{1,0:T(8,128)} %get-tuple-element.56, bf16[64,4096]{1,0:T(8,128)(2,1)S(1)} %all_gather.28, bf16[1792,4096]{1,0:T(8,128)(2,1)} %param.14), kind=kOutput, calls=%fused_computation.27 | convolution fusion | flops 941015040 | bytes 16580608 | tf_op jit(solution)/shard_map/dot_general | solution.py:19
  216.2 9.7 %fusion.23 = f32[64,4096]{1,0:T(8,128)S(1)} fusion(bf16[64,1792]{1,0:T(8,128)(2,1)S(1)} %get-tuple-element.50, bf16[4096,1792]{1,0:T(8,128)(2,1)} %param.12), kind=kOutput, calls=%fused_computation.69 | convolution fusion | flops 939524096 | bytes 15958016 | tf_op jit(solution)/shard_map/dot_general | solution.py:19
  225.8 10.5 %fusion = bf16[64,4096]{1,0:T(8,128)(2,1)} fusion(f32[64,4096]{1,0:T(8,128)S(1)} %fusion.23, bf16[64,1792]{1,0:T(8,128)(2,1)S(1)} %get-tuple-element.49, bf16[4096,1792]{1,0:T(8,128)(2,1)} %param.13), kind=kOutput, calls=%fused_computation.3 | convolution fusion | flops 940048384 | bytes 16482304 | tf_op jit(solution)/shard_map/dot_general | solution.py:19
  237.2 13.8 %all_gather.29 = bf16[256,1792]{1,0:T(8,128)(2,1)S(1)} all-gather(bf16[64,1792]{1,0:T(8,128)(2,1)S(1)} %get-tuple-element.50), channel_id=1, replica_groups=mesh['dp'=4,'fsdp'=8] {'dp'}, dimensions={0}, use_global_device_ids=true | all-gather | bytes 1146880 | tf_op jit(solution)/shard_map/all_gather | solution.py:130
  251.0 3.5 %all-to-all-start.3 = ((bf16[64,4,1024]{2,0,1:T(8,128)(2,1)}), bf16[64,4,1024]{2,0,1:T(8,128)(2,1)S(1)}, u32[]{:S(2)}, u32[]{:S(2)}) async-start(bf16[64,4,1024]{2,0,1:T(8,128)(2,1)} %bitcast.55), calls=%async_computation.4 | async-start | bytes 1048576 | tf_op jit(solution)/shard_map/all_to_all | solution.py:127
  254.5 3.0 %fusion.2 = bf16[1024,1792]{0,1:T(8,128)(2,1)} fusion(bf16[256,1792]{1,0:T(8,128)(2,1)S(1)} %all_gather.29, bf16[256,1024]{1,0:T(8,128)(2,1)S(1)} %bitcast.60), kind=kOutput, calls=%fused_computation.11 | convolution fusion | flops 941359104 | bytes 5111808 | tf_op jit(solution)/shard_map/dot_general | solution.py:19
  257.5 13.2 %all_gather.30 = bf16[256,1792]{1,0:T(8,128)(2,1)S(1)} all-gather(bf16[64,1792]{1,0:T(8,128)(2,1)S(1)} %get-tuple-element.49), channel_id=1, replica_groups=mesh['dp'=4,'fsdp'=8] {'dp'}, dimensions={0}, use_global_device_ids=true | all-gather | bytes 1146880 | tf_op jit(solution)/shard_map/all_gather | solution.py:130
  273.7 5.9 %copy.90 = bf16[1024,1792]{1,0:T(8,128)(2,1)} copy(bf16[1024,1792]{0,1:T(8,128)(2,1)} %fusion.2) | data formatting | bytes 7340032
  279.6 6.0 %copy.91 = bf16[1024,1792]{1,0:T(8,128)(2,1)} copy(bf16[1024,1792]{0,1:T(8,128)(2,1)} %fusion.3) | data formatting | bytes 7340032
  286.1 3.0 %convolution_convert_fusion.2 = bf16[1792,1024]{1,0:T(8,128)(2,1)} fusion(bf16[256,1792]{1,0:T(8,128)(2,1)S(1)} %copy-done.1, bf16[256,1024]{1,0:T(8,128)(2,1)S(1)} %bitcast.63), kind=kOutput, calls=%fused_computation.8 | convolution fusion | flops 941359104 | bytes 5111808 | tf_op jit(solution)/shard_map/dot_general | solution.py:19
  (68 shorter events, 18.6 us)
Async XLA Ops:
  24.0 9.3 %copy-start = (bf16[4096,1792]{1,0:T(8,128)(2,1)S(1)}, bf16[4096,1792]{1,0:T(8,128)(2,1)}, u32[]{:S(2)}) copy-start(bf16[4096,1792]{1,0:T(8,128)(2,1)} %param.13) | copy-start | bytes 44040196
  24.0 12.8 %slice-start = ((s8[14680064]{0:T(1024)(128)(4,1)}), s8[4194304]{0:T(1024)(128)(4,1)S(1)}, s32[]{:S(2)}) async-start(s8[14680064]{0:T(1024)(128)(4,1)} %bitcast.57), calls=%async_computation.7 | async-start | bytes 8388608
  24.0 12.8 %slice-start.1 = ((s8[14680064]{0:T(1024)(128)(4,1)}), s8[4194304]{0:T(1024)(128)(4,1)S(1)}, s32[]{:S(2)}) async-start(s8[14680064]{0:T(1024)(128)(4,1)} %bitcast.57), calls=%async_computation.8 | async-start | bytes 8388608
  24.0 13.2 %slice-start.2 = ((s8[14680064]{0:T(1024)(128)(4,1)}), s8[4194304]{0:T(1024)(128)(4,1)S(1)}, s32[]{:S(2)}) async-start(s8[14680064]{0:T(1024)(128)(4,1)} %bitcast.57), calls=%async_computation.9 | async-start | bytes 8388608
  33.3 3.5 %copy-start.3 = (f32[64,1792]{1,0:T(8,128)}, f32[64,1792]{1,0:T(8,128)S(1)}, u32[]{:S(2)}) copy-start(f32[64,1792]{1,0:T(8,128)S(1)} %fusion.22) | copy-start | bytes 1376260
  33.3 4.7 %slice-start.3 = ((s8[14680064]{0:T(1024)(128)(4,1)}), s8[2097152]{0:T(1024)(128)(4,1)S(1)}, s32[]{:S(2)}) async-start(s8[14680064]{0:T(1024)(128)(4,1)} %bitcast.57), calls=%async_computation.10 | async-start | bytes 4194304
  38.0 8.2 %copy-start.5 = (bf16[8,4096]{1,0:T(8,128)(2,1)S(1)}, bf16[8,4096]{1,0:T(8,128)(2,1)}, u32[]{:S(2)}) copy-start(bf16[8,4096]{1,0:T(8,128)(2,1)} %param.16) | copy-start | bytes 196612
  38.0 23.6 %copy-start.4 = (bf16[8,4096]{1,0:T(8,128)(2,1)S(1)}, bf16[8,4096]{1,0:T(8,128)(2,1)}, u32[]{:S(2)}) copy-start(bf16[8,4096]{1,0:T(8,128)(2,1)} %param.11) | copy-start | bytes 196612
  38.0 39.7 %copy-start.7 = (s32[8,64]{1,0:T(8,128)S(1)}, s32[8,64]{1,0:T(8,128)}, u32[]{:S(2)}) copy-start(s32[8,64]{1,0:T(8,128)} %param.19) | copy-start | bytes 6148
  38.0 81.0 %copy-start.8 = (s32[32,1]{0,1:T(1,128)S(1)}, s32[32,1]{0,1:T(1,128)}, u32[]{:S(2)}) copy-start(s32[32,1]{0,1:T(1,128)} %param.18) | copy-start | bytes 388
  41.5 20.0 %all-to-all-start = ((bf16[8,8,4096]{2,1,0:T(8,128)(2,1)}), bf16[8,8,4096]{2,1,0:T(8,128)(2,1)S(1)}, u32[]{:S(2)}, u32[]{:S(2)}) async-start(bf16[8,8,4096]{2,1,0:T(8,128)(2,1)} %fusion.1), calls=%async_computation | async-start | bytes 1048576 | tf_op jit(solution)/shard_map/all_to_all | solution.py:27
  46.2 76.2 %all-gather.2.cloned.1.call-start = ((), (), s32[]{:S(2)}) async-start(), calls=%async_computation.5 | async-start | bytes 2621440 | tf_op jit(solution)/shard_map/all_gather | solution.py:86
  124.5 4.3 %copy-start.6 = (s32[32,1,32]{2,1,0:T(1,128)S(1)}, s32[32,1,32]{2,1,0:T(1,128)}, u32[]{:S(2)}) copy-start(s32[32,1,32]{2,1,0:T(1,128)} %param.17) | copy-start | bytes 12292
  124.5 4.9 %copy-start.2 = (bf16[512,4096]{1,0:T(8,128)(2,1)S(1)}, bf16[512,4096]{1,0:T(8,128)(2,1)}, u32[]{:S(2)}) copy-start(bf16[512,4096]{1,0:T(8,128)(2,1)} %param.15) | copy-start | bytes 12582916
  132.3 54.3 %all-to-all-start.1 = ((bf16[32,8,4224]{2,1,0:T(8,128)(2,1)}), bf16[32,8,4224]{2,1,0:T(8,128)(2,1)S(1)}, u32[]{:S(2)}, u32[]{:S(2)}) async-start(bf16[32,8,4224]{2,1,0:T(8,128)(2,1)} %maximum_bitcast_fusion), calls=%async_computation.1 | async-start | bytes 4325376 | tf_op jit(solution)/shard_map/all_to_all | solution.py:27
  186.6 64.4 %all-to-all-start.2 = ((bf16[64,4,1024]{2,0,1:T(8,128)(2,1)}), bf16[64,4,1024]{2,0,1:T(8,128)(2,1)S(1)}, u32[]{:S(2)}, u32[]{:S(2)}) async-start(bf16[64,4,1024]{2,0,1:T(8,128)(2,1)} %bitcast.64), calls=%async_computation.3 | async-start | bytes 1048576 | tf_op jit(solution)/shard_map/all_to_all | solution.py:127
  190.1 99.0 %reduce-scatter.2.cloned.1.call-start = ((), (), s32[]{:S(2)}) async-start(), calls=%async_computation.6 | async-start | bytes 589824 | tf_op jit(solution)/shard_map/reduce_scatter | solution.py:122
  251.0 35.1 %all-to-all-start.3 = ((bf16[64,4,1024]{2,0,1:T(8,128)(2,1)}), bf16[64,4,1024]{2,0,1:T(8,128)(2,1)S(1)}, u32[]{:S(2)}, u32[]{:S(2)}) async-start(bf16[64,4,1024]{2,0,1:T(8,128)(2,1)} %bitcast.55), calls=%async_computation.4 | async-start | bytes 1048576 | tf_op jit(solution)/shard_map/all_to_all | solution.py:127
  279.6 6.5 %copy-start.1 = (bf16[256,1792]{1,0:T(8,128)(2,1)S(1)}, bf16[256,1792]{1,0:T(8,128)(2,1)}, u32[]{:S(2)}) copy-start(bf16[256,1792]{1,0:T(8,128)(2,1)} %all_gather.31) | copy-start | bytes 2752516
Sparse Core Ops, SparseCore 0:
  77.9 34.7 all-gather.1
  236.5 29.6 reduce-scatter.1

commit v2 on v1

v2 whole, which is shorter than its diff:
```python
import jax
import jax.numpy as jnp
from jax import lax
from jax.sharding import PartitionSpec as P

inverse_temp = 50.0
eps = 1e-06
contract_first = (((0,), (0,)), ((), ()))
contract_last = (((1,), (1,)), ((), ()))
every = ("dp", "fsdp")


def silu_grad(gate_act):
    sigmoid_gate = jax.nn.sigmoid(gate_act)
    return sigmoid_gate * (1.0 + gate_act * (1.0 - sigmoid_gate))


def dot32(left, right, dims=(((1,), (0,)), ((), ()))):
    return lax.dot_general(left, right, dims, preferred_element_type=jnp.float32)


def norm_of(rows):
    return jnp.sqrt(jnp.sum(rows * rows, axis=-1) + eps)


def swap(x, axis, difference):
    pairs = [(i, i ^ difference) for i in range(lax.axis_size(axis))]
    return lax.ppermute(x, axis, pairs)


def swap_core(x):
    return swap(x, "fsdp", 1)


def gather_chips(x):
    chips = lax.axis_size("fsdp") // 2
    return jnp.concatenate([x] + [swap(x, "fsdp", 2 * j) for j in range(1, chips)], axis=0)


def gather_dp(x):
    return jnp.concatenate([x] + [swap(x, "dp", j) for j in range(1, lax.axis_size("dp"))], axis=0)


def gather_core(x):
    return jnp.concatenate([x, swap_core(x)], axis=0)


def add_up(pieces):
    total = pieces[0].astype(jnp.float32)
    for piece in pieces[1:]:
        total = total + piece.astype(jnp.float32)
    return total


def sum_core(x):
    rows = x.shape[0] // 2
    return add_up([x[:rows], swap_core(x[rows:])])


def sum_over(x, axis, parts, unit):
    rows = x.shape[0] // parts
    return add_up(
        [x[:rows]]
        + [swap(x[j * rows : (j + 1) * rows], axis, j * unit) for j in range(1, parts)]
    )


def sum_chips(x):
    return sum_over(x, "fsdp", lax.axis_size("fsdp") // 2, 2)


def sum_dp(x):
    return sum_over(x, "dp", lax.axis_size("dp"), 1)


def relative_order(blocks, block_rows):
    mine = lax.axis_index("fsdp")
    rows = blocks * block_rows
    place = lax.broadcasted_iota(jnp.int32, (rows, rows), 0)
    block, row = place // block_rows, place % block_rows
    core, chip = block // (blocks // 2), block % (blocks // 2)
    source = jnp.bitwise_xor(mine, 2 * chip + core) * block_rows + row
    return (source == lax.broadcasted_iota(jnp.int32, (rows, rows), 1)).astype(jnp.bfloat16)


def in_fsdp_order(pieces):
    mine = lax.axis_index("fsdp")
    blocks = pieces.shape[0]
    pieces = pieces.reshape((2, blocks // 2) + pieces.shape[1:])
    pieces = jnp.where(mine % 2 == 1, pieces[::-1], pieces)
    bit = 1
    while bit < blocks // 2:
        split = pieces.reshape((2, blocks // 4 // bit, 2, bit) + pieces.shape[2:])
        split = jnp.where((mine // (2 * bit)) % 2 == 1, split[:, :, ::-1], split)
        pieces = split.reshape(pieces.shape)
        bit *= 2
    return jnp.swapaxes(pieces, 0, 1).reshape((blocks,) + pieces.shape[2:])


def use_counts(slots, row_table, count_table, shard, shard_rows):
    devices, queries, negatives = slots.shape
    slot_cap = row_table.shape[1]
    slot = lax.broadcasted_iota(jnp.int32, (1, 1, 1, slot_cap), 3) + shard * slot_cap
    asked = jnp.sum((slots[..., None] == slot).astype(jnp.float32), axis=2)
    live = lax.broadcasted_iota(jnp.int32, (devices, 1, slot_cap), 2) < count_table[:, None, None]
    used = jnp.where(live, asked, 0.0)
    dead = jnp.sum(asked - used, axis=-1).reshape(devices * queries)
    row = lax.broadcasted_iota(jnp.int32, (1, 1, shard_rows), 2)
    picks = (row_table[:, :, None] == row).astype(jnp.bfloat16)
    counts = lax.dot_general(
        used.astype(jnp.bfloat16),
        picks,
        (((2,), (1,)), ((0,), (0,))),
        preferred_element_type=jnp.float32,
    )
    return counts.reshape(devices * queries, shard_rows), dead


def shards(
    mlp_input,
    residual_in,
    gate_weight,
    up_weight,
    down_weight,
    span_index,
    positive_keys,
    request_rows,
    request_counts,
    negative_slots,
):
    dp_count = lax.axis_size("dp")
    fsdp_count = lax.axis_size("fsdp")
    chips = fsdp_count // 2
    my_dp, my_fsdp = lax.axis_index("dp"), lax.axis_index("fsdp")
    me = my_dp * fsdp_count + my_fsdp
    width = span_index.shape[1]
    own_queries = negative_slots.shape[0]
    group_rows = mlp_input.shape[0]

    pieces = gather_core(gather_chips(mlp_input[None]))
    whole_input = jnp.swapaxes(in_fsdp_order(pieces), 0, 1).reshape(group_rows, width)
    to_relative = relative_order(fsdp_count, own_queries)
    whole_input = dot32(to_relative, whole_input).astype(jnp.bfloat16)

    chip_index = gather_core(span_index[None])
    tables = gather_core(jnp.concatenate([request_rows[:, 0, :], request_counts], axis=1)[None])
    slots = gather_dp(gather_chips(negative_slots[None]))
    j = jnp.arange(dp_count * chips, dtype=jnp.int32)
    asker = jnp.bitwise_xor(my_dp, j // chips) * fsdp_count + jnp.bitwise_xor(
        my_fsdp, 2 * (j % chips)
    )
    tables = jnp.take(tables, asker, axis=1)
    counts, dead = [], 0.0
    for k in range(2):
        shard_counts, shard_dead = use_counts(
            slots,
            tables[k, :, :-1],
            tables[k, :, -1],
            jnp.bitwise_xor(me, k),
            span_index.shape[0],
        )
        counts.append(shard_counts)
        dead = dead + shard_dead
    counts = jnp.concatenate(counts, axis=1)
    chip_index = chip_index.reshape(-1, width)
    index_norm = norm_of(chip_index.astype(jnp.float32))

    gate_act = dot32(whole_input, gate_weight)
    up_act = dot32(whole_input, up_weight)
    hidden = (jax.nn.silu(gate_act) * up_act).astype(jnp.bfloat16)
    branch = sum_core(dot32(hidden, down_weight).astype(jnp.bfloat16))
    branch = sum_chips(branch.astype(jnp.bfloat16))
    top_state = branch + residual_in.astype(jnp.float32)
    row_norm = norm_of(top_state)
    unit_rows = top_state / row_norm[:, None]

    states = gather_dp(gather_chips(top_state.astype(jnp.bfloat16)))
    state_norm = norm_of(states.astype(jnp.float32))
    raw_scores = dot32(states, chip_index, contract_last)
    scores = inverse_temp * raw_scores / state_norm[:, None] / index_norm[None, :]
    weights = counts * jnp.exp(scores)
    chip_total = jnp.sum(weights, axis=-1) + dead
    chip_pull = dot32((weights / index_norm[None, :]).astype(jnp.bfloat16), chip_index)

    column = lax.broadcasted_iota(jnp.int32, (chip_total.shape[0], 128), 1)
    totals = jnp.where(column == 0, chip_total[:, None], 0.0).astype(jnp.bfloat16)
    sums = sum_dp(jnp.concatenate([chip_pull.astype(jnp.bfloat16), totals], axis=1))
    sums = sum_chips(sums.astype(jnp.bfloat16))
    negative_total = sums[:, width]
    positive_rows = positive_keys.astype(jnp.float32)
    positive_unit = positive_rows / norm_of(positive_rows)[:, None]
    positive_score = inverse_temp * jnp.sum(unit_rows * positive_unit, axis=-1)
    exp_total = jnp.exp(positive_score) + negative_total
    query_loss = jnp.log(exp_total) - positive_score
    pull = (sums[:, :width] - negative_total[:, None] * positive_unit) / exp_total[:, None]
    inner = jnp.sum(pull * unit_rows, axis=-1)
    head_grad = (
        inverse_temp * (pull - inner[:, None] * unit_rows) / row_norm[:, None]
    ).astype(jnp.bfloat16)

    def columns_of_all(rows):
        part = rows.shape[1] // dp_count
        return jnp.concatenate(
            [
                swap(
                    lax.dynamic_slice_in_dim(rows, jnp.bitwise_xor(my_dp, k) * part, part, axis=1),
                    "dp",
                    k,
                )
                if k
                else lax.dynamic_slice_in_dim(rows, my_dp * part, part, axis=1)
                for k in range(dp_count)
            ],
            axis=0,
        )

    input_columns = columns_of_all(whole_input)
    gate_all = gather_dp(gate_act.astype(jnp.bfloat16)).astype(jnp.float32)
    up_all = gather_dp(up_act.astype(jnp.bfloat16)).astype(jnp.float32)

    gathered_grad = gather_core(gather_chips(head_grad))
    hidden_grad = dot32(gathered_grad, down_weight, contract_last)
    own_gate_grad = (hidden_grad * up_act * silu_grad(gate_act)).astype(jnp.bfloat16)
    own_up_grad = (hidden_grad * jax.nn.silu(gate_act)).astype(jnp.bfloat16)
    own_gate_grad = dot32(to_relative, own_gate_grad, contract_first).astype(jnp.bfloat16)
    own_up_grad = dot32(to_relative, own_up_grad, contract_first).astype(jnp.bfloat16)
    input_term = dot32(own_gate_grad, gate_weight, contract_last) + dot32(
        own_up_grad, up_weight, contract_last
    )
    input_blocks = input_term.astype(jnp.bfloat16).reshape(group_rows, fsdp_count, -1)
    source = jnp.arange(fsdp_count, dtype=jnp.int32)
    source = jnp.bitwise_xor(my_fsdp, 2 * (source % chips) + source // chips)
    input_blocks = jnp.take(jnp.swapaxes(input_blocks, 0, 1), source, axis=0)
    input_grad = sum_chips(sum_core(input_blocks).astype(jnp.bfloat16))[0].astype(jnp.bfloat16)

    grad_columns = columns_of_all(gathered_grad)
    hidden_all = (jax.nn.silu(gate_all) * up_all).astype(jnp.bfloat16)
    down_grad = dot32(hidden_all, grad_columns, contract_first).astype(jnp.bfloat16)
    grad_all = gather_dp(hidden_grad.astype(jnp.bfloat16)).astype(jnp.float32)
    gate_grad_all = (grad_all * up_all * silu_grad(gate_all)).astype(jnp.bfloat16)
    up_grad_all = (grad_all * jax.nn.silu(gate_all)).astype(jnp.bfloat16)
    gate_grad = dot32(input_columns.T, gate_grad_all).astype(jnp.bfloat16)
    up_grad = dot32(input_columns.T, up_grad_all).astype(jnp.bfloat16)
    return (query_loss, input_grad, gate_grad, up_grad, down_grad)


def solution(mesh):
    return jax.shard_map(
        shards,
        mesh=mesh,
        in_specs=(
            P("dp", "fsdp"),
            P(("dp", "fsdp"), None),
            P(None, "fsdp"),
            P(None, "fsdp"),
            P("fsdp", None),
            P(("dp", "fsdp"), None),
            P(("dp", "fsdp"), None),
            P(None, ("dp", "fsdp"), None),
            P(None, ("dp", "fsdp")),
            P(("dp", "fsdp"), None),
        ),
        out_specs=(
            P(("dp", "fsdp")),
            P("dp", "fsdp"),
            P("dp", "fsdp"),
            P("dp", "fsdp"),
            P("fsdp", "dp"),
        ),
        check_vma=False,
    )
```

time: 297 us -> 213 us (0.72)
  blocking collectives: 144 us -> 0 us
  starting transfers between devices: 14.4 us -> 60.7 us
  waiting for transfers between devices: 37.7 us -> 58 us
  between operations: 14.3 us -> 1.33 us
  local copies, waits for them, and re-layouts: 16.6 us -> 6.87 us
  other arithmetic: 9.31 us -> 18.8 us
  matrix products: 60 us -> 66.7 us
    all_gather x7 -> x0, blocking collectives: 144 us -> none  [the longest x3 55.2 us: rows_of_all(): return lax.all_gather(rows, 'dp', axis=0, tiled=True)]
    ppermute x0 -> x51, starting transfers between devices: none -> 60.7 us  [swap(): return lax.ppermute(x, axis, pairs)]
    ppermute x0 -> x51, waiting for transfers between devices: none -> 58 us  [swap(): return lax.ppermute(x, axis, pairs)]
    all_to_all x4 -> x0, waiting for transfers between devices: 37.6 us -> none  [the longest x2 37.6 us: sum_to_owner(): lax.all_to_all(partial, axis, split_axis=0, concat_axis=0, tiled=True)]
    all_to_all x4 -> x0, starting transfers between devices: 14.4 us -> none  [the longest x2 7.41 us: sum_to_owner(): lax.all_to_all(partial, axis, split_axis=0, concat_axis=0, tiled=True)]
    unnamed x28 -> x52, local copies, waits for them, and re-layouts: 14.6 us -> 3.69 us
    concatenate x0 -> x8, other arithmetic: none -> 8.75 us  [the longest x2 6.29 us: gather_core(): return jnp.concatenate([x, swap_core(x)], axis=0)]
    dot_general x11 -> x12, matrix products: 59.4 us -> 65.3 us  [dot32(): lax.dot_general(left, right, dims, preferred_element_type=jnp.float32)]
  transfers between devices with their start and end apart: 6 -> 51, of which waited for: 2 -> 26; matrix products, arithmetic and copies ran while one was open for 20% -> 43% of each run, Pallas kernels for 0% -> 0%
where the time goes in v2:
time: 213 us; the launch traced here: 212 us
  matrix products  66.7 us (31%)
  starting transfers between devices  60.7 us (28%)
  waiting for transfers between devices  58 us (27%)
  other arithmetic  18.8 us (9%)
  local copies, waits for them, and re-layouts  6.87 us (3%)
    dot_general x12, matrix products, dot32(): lax.dot_general(left, right, dims, preferred_element_type=jnp.float32)  65.3 us
    ppermute x51, starting transfers between devices, swap(): return lax.ppermute(x, axis, pairs)  60.7 us
    ppermute x51, waiting for transfers between devices, swap(): return lax.ppermute(x, axis, pairs)  58 us
    concatenate x2, other arithmetic, gather_core(): return jnp.concatenate([x, swap_core(x)], axis=0)  6.29 us
    reduce_sum x4, other arithmetic, norm_of(): return jnp.sqrt(jnp.sum(rows * rows, axis=-1) + eps)  5.64 us
  transfers between devices with their start and end apart: 51, of which 26 were waited for; matrix products, arithmetic and copies ran while one was open for 43% of the time, Pallas kernels for 0%

profile of v2, /device:TPU:0, one launch (start us, length us, event | category | flops | bytes accessed | tf_op | source)
XLA Modules:
  0.0 212.5 jit_solution(661310956967444575)
XLA Ops:
  0.6 3.1 %collective-permute-start = (bf16[1,64,512]{2,1,0:T(8,128)(2,1)}, bf16[1,64,512]{2,1,0:T(8,128)(2,1)S(1)}, u32[]{:S(2)}, u32[]{:S(2)}) collective-permute-start(bf16[1,64,512]{2,1,0:T(8,128)(2,1)} %bitcast.75), channel_id=1, source_target_pairs={{0,2},{1,3},{2,0},{3,1},{4,6},{5,7},{6,4},{7,5},{8,10},{9,11},{10,... | collective-permute-start | bytes 196616 | tf_op jit(solution)/shard_map/ppermute | solution.py:28
  7.2 3.5 %collective-permute-start.10 = (s32[1,8,64]{2,1,0:T(8,128)}, s32[1,8,64]{2,1,0:T(8,128)S(1)}, u32[]{:S(2)}, u32[]{:S(2)}) collective-permute-start(s32[1,8,64]{2,1,0:T(8,128)} %bitcast.85), channel_id=1, source_target_pairs={{0,4},{1,5},{2,6},{3,7},{4,0},{5,1},{6,2},{7,3},{8,12},{9,13},{10,... | collective-permute-start | bytes 6152 | tf_op jit(solution)/shard_map/ppermute | solution.py:28
  15.1 5.5 %collective-permute-done.11 = s32[1,8,64]{2,1,0:T(8,128)S(1)} collective-permute-done((s32[1,8,64]{2,1,0:T(8,128)}, s32[1,8,64]{2,1,0:T(8,128)S(1)}, u32[]{:S(2)}, u32[]{:S(2)}) %collective-permute-start.11) | collective-permute-done | bytes 2080 | tf_op jit(solution)/shard_map/ppermute | solution.py:28
  38.9 8.8 %fusion.99 = (bf16[64,1792]{1,0:T(8,128)(2,1)}, f32[64,1792]{1,0:T(8,128)S(1)}) fusion(bf16[64,4096]{1,0:T(8,128)(2,1)S(1)} %convolution_convert_fusion.1, bf16[4096,1792]{1,0:T(8,128)(2,1)} %param.13), kind=kOutput, calls=%fused_computation.248 | convolution fusion | flops 939638784 | bytes 15892480 | tf_op jit(solution)/shard_map/dot_general | solution.py:19
  47.9 3.4 %fusion.101 = (bf16[64,1792]{1,0:T(8,128)(2,1)}, f32[64,1792]{1,0:T(8,128)S(1)}) fusion(bf16[64,4096]{1,0:T(8,128)(2,1)S(1)} %convolution_convert_fusion.1, bf16[4096,1792]{1,0:T(8,128)(2,1)S(1)} %bitcast.61), kind=kOutput, calls=%fused_computation.250 | convolution fusion | flops 939638784 | bytes 15892480 | tf_op jit(solution)/shard_map/dot_general | solution.py:19
  52.3 2.7 %convolution_convert_fusion.2 = bf16[64,4096]{1,0:T(8,128)(2,1)S(1)} fusion(bf16[1792,4096]{1,0:T(8,128)(2,1)S(1)} %bitcast.63, f32[64,1792]{1,0:T(8,128)S(1)} %get-tuple-element.43, f32[64,1792]{1,0:T(8,128)S(1)} %get-tuple-element.47), kind=kOutput, calls=%fused_computation.8 | convolution fusion | flops 940474368 | bytes 16121856 | tf_op jit(solution)/shard_map/dot_general | solution.py:19
  56.9 2.6 %collective-permute-start.44 = (bf16[64,1792]{1,0:T(8,128)(2,1)}, bf16[64,1792]{1,0:T(8,128)(2,1)}, u32[]{:S(2)}, u32[]{:S(2)}) collective-permute-start(bf16[64,1792]{1,0:T(8,128)(2,1)} %get-tuple-element.42), channel_id=1, source_target_pairs={{0,24},{8,16},{16,8},{24,0},{1,25},{9,17},{17,9},{25,1},{2,26},{10... | collective-permute-start | bytes 688136 | tf_op jit(solution)/shard_map/ppermute | solution.py:28
  59.6 3.7 %collective-permute-start.7 = (bf16[8,4096]{1,0:T(8,128)(2,1)S(1)}, bf16[8,4096]{1,0:T(8,128)(2,1)S(1)}, u32[]{:S(2)}, u32[]{:S(2)}) collective-permute-start(bf16[8,4096]{1,0:T(8,128)(2,1)S(1)} %get-tuple-element.36), channel_id=1, source_target_pairs={{0,6},{1,7},{2,4},{3,5},{4,2},{5,3},{6,0},{7,1},{8,14},{9,15},{10,... | collective-permute-start | bytes 196616 | tf_op jit(solution)/shard_map/ppermute | solution.py:28
  74.1 2.7 %collective-permute-done.16 = bf16[8,4096]{1,0:T(8,128)(2,1)S(1)} collective-permute-done((bf16[8,4096]{1,0:T(8,128)(2,1)S(1)}, bf16[8,4096]{1,0:T(8,128)(2,1)S(1)}, u32[]{:S(2)}, u32[]{:S(2)}) %collective-permute-start.16) | collective-permute-done | bytes 65568 | tf_op jit(solution)/shard_map/ppermute | solution.py:28
  79.2 5.7 %collective-permute-done.18 = bf16[32,4096]{1,0:T(8,128)(2,1)S(1)} collective-permute-done((bf16[32,4096]{1,0:T(8,128)(2,1)S(1)}, bf16[32,4096]{1,0:T(8,128)(2,1)S(1)}, u32[]{:S(2)}, u32[]{:S(2)}) %collective-permute-start.18) | collective-permute-done | bytes 262176 | tf_op jit(solution)/shard_map/ppermute | solution.py:28
  85.1 3.6 %collective-permute-done.19 = bf16[32,4096]{1,0:T(8,128)(2,1)S(1)} collective-permute-done((bf16[32,4096]{1,0:T(8,128)(2,1)S(1)}, bf16[32,4096]{1,0:T(8,128)(2,1)S(1)}, u32[]{:S(2)}, u32[]{:S(2)}) %collective-permute-start.19) | collective-permute-done | bytes 262176 | tf_op jit(solution)/shard_map/ppermute | solution.py:28
  88.7 3.6 %collective-permute-done.20 = bf16[32,4096]{1,0:T(8,128)(2,1)S(1)} collective-permute-done((bf16[32,4096]{1,0:T(8,128)(2,1)S(1)}, bf16[32,4096]{1,0:T(8,128)(2,1)S(1)}, u32[]{:S(2)}, u32[]{:S(2)}) %collective-permute-start.20) | collective-permute-done | bytes 262176 | tf_op jit(solution)/shard_map/ppermute | solution.py:28
  92.6 4.2 %multiply_reduce_fusion = f32[2,512]{1,0:T(2,128)S(1)} fusion(bf16[1,512,4096]{2,1,0:T(8,128)(2,1)} %collective-permute-done.21, bf16[1,512,4096]{2,1,0:T(8,128)(2,1)S(1)} %bitcast.65), kind=kLoop, calls=%fused_computation.2 | loop fusion | flops 16776192 | bytes 8392704 | tf_op jit(solution)/shard_map/reduce_sum | solution.py:23
  96.8 6.3 %pad_maximum_fusion = bf16[2,512,4096]{2,1,0:T(8,128)(2,1)} fusion(bf16[1,512,4096]{2,1,0:T(8,128)(2,1)} %collective-permute-done.21, bf16[1,512,4096]{2,1,0:T(8,128)(2,1)S(1)} %bitcast.66), kind=kLoop, calls=%fused_computation.3 | loop fusion | flops 4194304 | bytes 16777216 | tf_op jit(solution)/shard_map/concatenate | solution.py:45
  103.1 6.6 %fusion.98 = (f32[128]{0:T(128)S(1)}, f32[128,1024]{1,0:T(8,128)S(1)}) fusion(f32[1024]{0:T(1024)S(1)} %bitcast.88, f32[128]{0:T(128)S(1)} %add_sqrt_fusion, bf16[128,4096]{1,0:T(8,128)(2,1)S(1)} %constant_dynamic-update-slice_fusion.12, bf16[1024,4096]{1,0:T(8,128)(2,1)} %bitcast.67, f32[128,512]{1,0:T(8,128)S(1)} %convolution_bitcast_fusion, ...), kind=kOutput, calls=%fused_computation.247 | convolution fusion | flops 1074528128 | bytes 10490880 | tf_op jit(solution)/shard_map/dot_general | solution.py:19
  114.9 4.2 %collective-permute-done.24 = bf16[32,4224]{1,0:T(8,128)(2,1)S(1)} collective-permute-done((bf16[32,4224]{1,0:T(8,128)(2,1)S(1)}, bf16[32,4224]{1,0:T(8,128)(2,1)S(1)}, u32[]{:S(2)}, u32[]{:S(2)}) %collective-permute-start.24) | collective-permute-done | bytes 270368 | tf_op jit(solution)/shard_map/ppermute | solution.py:28
  142.7 10.4 %fusion.100 = (bf16[64,1792]{1,0:T(8,128)(2,1)}, f32[64,1792]{1,0:T(8,128)S(1)}) fusion(bf16[64,4096]{1,0:T(8,128)(2,1)S(1)} %constant_dynamic-update-slice_fusion.19, bf16[1792,4096]{1,0:T(8,128)(2,1)} %param.14), kind=kOutput, calls=%fused_computation.249 | convolution fusion | flops 939638784 | bytes 15892480 | tf_op jit(solution)/shard_map/dot_general | solution.py:19
  153.1 8.2 %fusion.13 = f32[64,4096]{1,0:T(8,128)S(1)} fusion(bf16[4096,1792]{1,0:T(8,128)(2,1)} %param.12, f32[64,1792]{1,0:T(8,128)S(1)} %get-tuple-element.47, f32[64,1792]{1,0:T(8,128)S(1)} %get-tuple-element.45, f32[64,1792]{1,0:T(8,128)S(1)} %get-tuple-element.43, s32[64]{0:T(128)S(1)} %get-tuple-element.51, s32[64]{0:T(128)S(1)} %get-tuple-element.52, ...), kind=kOutput, calls=%fused_computation.41 | convolution fusion | flops 955576320 | bytes 17106052 | tf_op jit(solution)/shard_map/dot_general | solution.py:19
  161.4 9.9 %fusion = bf16[64,4096]{1,0:T(8,128)(2,1)S(1)} fusion(f32[64,4096]{1,0:T(8,128)S(1)} %fusion.13, bf16[4096,1792]{1,0:T(8,128)(2,1)} %param.13, f32[64,1792]{1,0:T(8,128)S(1)} %get-tuple-element.45, f32[64,1792]{1,0:T(8,128)S(1)} %get-tuple-element.47, s32[64]{0:T(128)S(1)} %get-tuple-element.51, s32[64]{0:T(128)S(1)} %get-tuple-element.52, ...), kind=kOutput, calls=%fused_computation.7 | convolution fusion | flops 955641856 | bytes 17171588 | tf_op jit(solution)/shard_map/dot_general | solution.py:19
  176.9 5.3 %collective-permute-done.46 = bf16[64,1792]{1,0:T(8,128)(2,1)S(1)} collective-permute-done((bf16[64,1792]{1,0:T(8,128)(2,1)}, bf16[64,1792]{1,0:T(8,128)(2,1)S(1)}, u32[]{:S(2)}, u32[]{:S(2)}) %collective-permute-start.46) | collective-permute-done | bytes 229408 | tf_op jit(solution)/shard_map/ppermute | solution.py:28
  188.6 4.7 %convolution_convert_fusion.3 = bf16[1792,1024]{1,0:T(8,128)(2,1)} fusion(bf16[64,1024]{1,0:T(8,128)(2,1)S(1)} %collective-permute-done.50, bf16[64,1024]{1,0:T(8,128)(2,1)S(1)} %collective-permute-done.49, bf16[64,1024]{1,0:T(8,128)(2,1)S(1)} %collective-permute-done.48, bf16[64,1024]{1,0:T(8,128)(2,1)S(1)} %get-tuple-element.21, ...), kind=kOutput, calls=%fused_computation.9 | convolution fusion | flops 953548800 | bytes 6029312 | tf_op jit(solution)/shard_map/dot_general | solution.py:19
  198.3 4.7 %convolution_convert_fusion.5 = bf16[1024,1792]{1,0:T(8,128)(2,1)} fusion(bf16[64,1792]{1,0:T(8,128)(2,1)} %collective-permute-done.44, bf16[64,1792]{1,0:T(8,128)(2,1)} %collective-permute-done.43, bf16[64,1792]{1,0:T(8,128)(2,1)} %collective-permute-done.42, bf16[64,1792]{1,0:T(8,128)(2,1)} %get-tuple-element.42, ...), kind=kOutput, calls=%fused_computation.11 | convolution fusion | flops 959053824 | bytes 6946816 | tf_op jit(solution)/shard_map/dot_general | solution.py:19
  203.1 2.9 %collective-permute-start.35 = (bf16[1,64,512]{2,1,0:T(8,128)(2,1)S(1)}, bf16[1,64,512]{2,1,0:T(8,128)(2,1)S(1)}, u32[]{:S(2)}, u32[]{:S(2)}) collective-permute-start(bf16[1,64,512]{2,1,0:T(8,128)(2,1)S(1)} %get-tuple-element.33), channel_id=1, source_target_pairs={{0,6},{1,7},{2,4},{3,5},{4,2},{5,3},{6,0},{7,1},{8,14},{9,15},{10,... | collective-permute-start | bytes 196616 | tf_op jit(solution)/shard_map/ppermute | solution.py:28
  207.6 4.2 %convolution_convert_fusion.4 = bf16[1024,1792]{1,0:T(8,128)(2,1)} fusion(bf16[64,1792]{1,0:T(8,128)(2,1)S(1)} %collective-permute-done.41, bf16[64,1792]{1,0:T(8,128)(2,1)S(1)} %collective-permute-done.40, bf16[64,1792]{1,0:T(8,128)(2,1)S(1)} %collective-permute-done.39, bf16[64,1792]{1,0:T(8,128)(2,1)S(1)} %copy-done.3, ...), kind=kOutput, calls=%fused_computation.10 | convolution fusion | flops 953548800 | bytes 6029312 | tf_op jit(solution)/shard_map/dot_general | solution.py:19
  (218 shorter events, 90.7 us)
Async XLA Ops:
  0.6 34.9 %collective-permute-start = (bf16[1,64,512]{2,1,0:T(8,128)(2,1)}, bf16[1,64,512]{2,1,0:T(8,128)(2,1)S(1)}, u32[]{:S(2)}, u32[]{:S(2)}) collective-permute-start(bf16[1,64,512]{2,1,0:T(8,128)(2,1)} %bitcast.75), channel_id=1, source_target_pairs={{0,2},{1,3},{2,0},{3,1},{4,6},{5,7},{6,4},{7,5},{8,10},{9,11},{10,... | collective-permute-start | bytes 196616 | tf_op jit(solution)/shard_map/ppermute | solution.py:28
  3.7 31.9 %collective-permute-start.1 = (bf16[1,64,512]{2,1,0:T(8,128)(2,1)}, bf16[1,64,512]{2,1,0:T(8,128)(2,1)S(1)}, u32[]{:S(2)}, u32[]{:S(2)}) collective-permute-start(bf16[1,64,512]{2,1,0:T(8,128)(2,1)} %bitcast.76), channel_id=1, source_target_pairs={{0,4},{1,5},{2,6},{3,7},{4,0},{5,1},{6,2},{7,3},{8,12},{9,13},{10,... | collective-permute-start | bytes 196616 | tf_op jit(solution)/shard_map/ppermute | solution.py:28
  6.3 29.3 %collective-permute-start.2 = (bf16[1,64,512]{2,1,0:T(8,128)(2,1)}, bf16[1,64,512]{2,1,0:T(8,128)(2,1)S(1)}, u32[]{:S(2)}, u32[]{:S(2)}) collective-permute-start(bf16[1,64,512]{2,1,0:T(8,128)(2,1)} %bitcast.77), channel_id=1, source_target_pairs={{0,6},{1,7},{2,4},{3,5},{4,2},{5,3},{6,0},{7,1},{8,14},{9,15},{10,... | collective-permute-start | bytes 196616 | tf_op jit(solution)/shard_map/ppermute | solution.py:28
  6.3 8.6 %collective-permute-start.9 = (s32[1,8,64]{2,1,0:T(8,128)}, s32[1,8,64]{2,1,0:T(8,128)S(1)}, u32[]{:S(2)}, u32[]{:S(2)}) collective-permute-start(s32[1,8,64]{2,1,0:T(8,128)} %bitcast.84), channel_id=1, source_target_pairs={{0,2},{1,3},{2,0},{3,1},{4,6},{5,7},{6,4},{7,5},{8,10},{9,11},{10,... | collective-permute-start | bytes 6152 | tf_op jit(solution)/shard_map/ppermute | solution.py:28
  15.0 77.6 %collective-permute-start.21 = (bf16[1,512,4096]{2,1,0:T(8,128)(2,1)}, bf16[1,512,4096]{2,1,0:T(8,128)(2,1)}, u32[]{:S(2)}, u32[]{:S(2)}) collective-permute-start(bf16[1,512,4096]{2,1,0:T(8,128)(2,1)} %bitcast.64), channel_id=1, source_target_pairs={{0,1},{1,0},{2,3},{3,2},{4,5},{5,4},{6,7},{7,6},{8,9},{9,8},{10,11... | collective-permute-start | bytes 12582920 | tf_op jit(solution)/shard_map/ppermute | solution.py:28
  56.9 115.8 %collective-permute-start.44 = (bf16[64,1792]{1,0:T(8,128)(2,1)}, bf16[64,1792]{1,0:T(8,128)(2,1)}, u32[]{:S(2)}, u32[]{:S(2)}) collective-permute-start(bf16[64,1792]{1,0:T(8,128)(2,1)} %get-tuple-element.42), channel_id=1, source_target_pairs={{0,24},{8,16},{16,8},{24,0},{1,25},{9,17},{17,9},{25,1},{2,26},{10... | collective-permute-start | bytes 688136 | tf_op jit(solution)/shard_map/ppermute | solution.py:28
  74.0 99.3 %collective-permute-start.43 = (bf16[64,1792]{1,0:T(8,128)(2,1)}, bf16[64,1792]{1,0:T(8,128)(2,1)}, u32[]{:S(2)}, u32[]{:S(2)}) collective-permute-start(bf16[64,1792]{1,0:T(8,128)(2,1)} %get-tuple-element.42), channel_id=1, source_target_pairs={{0,16},{8,24},{16,0},{24,8},{1,17},{9,25},{17,1},{25,9},{2,18},{10... | collective-permute-start | bytes 688136 | tf_op jit(solution)/shard_map/ppermute | solution.py:28
  78.7 9.9 %collective-permute-start.19 = (bf16[32,4096]{1,0:T(8,128)(2,1)S(1)}, bf16[32,4096]{1,0:T(8,128)(2,1)S(1)}, u32[]{:S(2)}, u32[]{:S(2)}) collective-permute-start(bf16[32,4096]{1,0:T(8,128)(2,1)S(1)} %pad_maximum_fusion.7), channel_id=1, source_target_pairs={{0,16},{8,24},{16,0},{24,8},{1,17},{9,25},{17,1},{25,9},{2,18},{10... | collective-permute-start | bytes 786440 | tf_op jit(solution)/shard_map/ppermute | solution.py:28
  111.3 10.3 %collective-permute-start.23 = (bf16[32,4224]{1,0:T(8,128)(2,1)S(1)}, bf16[32,4224]{1,0:T(8,128)(2,1)S(1)}, u32[]{:S(2)}, u32[]{:S(2)}) collective-permute-start(bf16[32,4224]{1,0:T(8,128)(2,1)S(1)} %get-tuple-element.20), channel_id=1, source_target_pairs={{0,16},{8,24},{16,0},{24,8},{1,17},{9,25},{17,1},{25,9},{2,18},{10... | collective-permute-start | bytes 811016 | tf_op jit(solution)/shard_map/ppermute | solution.py:28
  135.0 40.6 %collective-permute-start.42 = (bf16[64,1792]{1,0:T(8,128)(2,1)}, bf16[64,1792]{1,0:T(8,128)(2,1)}, u32[]{:S(2)}, u32[]{:S(2)}) collective-permute-start(bf16[64,1792]{1,0:T(8,128)(2,1)} %get-tuple-element.42), channel_id=1, source_target_pairs={{0,8},{8,0},{16,24},{24,16},{1,9},{9,1},{17,25},{25,17},{2,10},{10... | collective-permute-start | bytes 688136 | tf_op jit(solution)/shard_map/ppermute | solution.py:28
  137.5 34.6 %collective-permute-start.38 = (bf16[64,1024]{1,0:T(8,128)(2,1)}, bf16[64,1024]{1,0:T(8,128)(2,1)}, u32[]{:S(2)}, u32[]{:S(2)}) collective-permute-start(bf16[64,1024]{1,0:T(8,128)(2,1)} %get-tuple-element.26), channel_id=1, source_target_pairs={{0,24},{8,16},{16,8},{24,0},{1,25},{9,17},{17,9},{25,1},{2,26},{10... | collective-permute-start | bytes 393224 | tf_op jit(solution)/shard_map/ppermute | solution.py:28
  140.3 35.9 %collective-permute-start.47 = (bf16[64,1792]{1,0:T(8,128)(2,1)}, bf16[64,1792]{1,0:T(8,128)(2,1)}, u32[]{:S(2)}, u32[]{:S(2)}) collective-permute-start(bf16[64,1792]{1,0:T(8,128)(2,1)} %get-tuple-element.46), channel_id=1, source_target_pairs={{0,24},{8,16},{16,8},{24,0},{1,25},{9,17},{17,9},{25,1},{2,26},{10... | collective-permute-start | bytes 688136 | tf_op jit(solution)/shard_map/ppermute | solution.py:28
  172.0 10.1 %collective-permute-start.46 = (bf16[64,1792]{1,0:T(8,128)(2,1)}, bf16[64,1792]{1,0:T(8,128)(2,1)S(1)}, u32[]{:S(2)}, u32[]{:S(2)}) collective-permute-start(bf16[64,1792]{1,0:T(8,128)(2,1)} %get-tuple-element.46), channel_id=1, source_target_pairs={{0,16},{8,24},{16,0},{24,8},{1,17},{9,25},{17,1},{25,9},{2,18},{10... | collective-permute-start | bytes 688136 | tf_op jit(solution)/shard_map/ppermute | solution.py:28
  172.7 10.1 %collective-permute-start.45 = (bf16[64,1792]{1,0:T(8,128)(2,1)}, bf16[64,1792]{1,0:T(8,128)(2,1)S(1)}, u32[]{:S(2)}, u32[]{:S(2)}) collective-permute-start(bf16[64,1792]{1,0:T(8,128)(2,1)} %get-tuple-element.46), channel_id=1, source_target_pairs={{0,8},{8,0},{16,24},{24,16},{1,9},{9,1},{17,25},{25,17},{2,10},{10... | collective-permute-start | bytes 688136 | tf_op jit(solution)/shard_map/ppermute | solution.py:28
  173.2 11.9 %collective-permute-start.50 = (bf16[64,1024]{1,0:T(8,128)(2,1)S(1)}, bf16[64,1024]{1,0:T(8,128)(2,1)S(1)}, u32[]{:S(2)}, u32[]{:S(2)}) collective-permute-start(bf16[64,1024]{1,0:T(8,128)(2,1)S(1)} %get-tuple-element.22), channel_id=1, source_target_pairs={{0,24},{8,16},{16,8},{24,0},{1,25},{9,17},{17,9},{25,1},{2,26},{10... | collective-permute-start | bytes 393224 | tf_op jit(solution)/shard_map/ppermute | solution.py:28
  175.6 10.8 %collective-permute-start.49 = (bf16[64,1024]{1,0:T(8,128)(2,1)S(1)}, bf16[64,1024]{1,0:T(8,128)(2,1)S(1)}, u32[]{:S(2)}, u32[]{:S(2)}) collective-permute-start(bf16[64,1024]{1,0:T(8,128)(2,1)S(1)} %get-tuple-element.23), channel_id=1, source_target_pairs={{0,16},{8,24},{16,0},{24,8},{1,17},{9,25},{17,1},{25,9},{2,18},{10... | collective-permute-start | bytes 393224 | tf_op jit(solution)/shard_map/ppermute | solution.py:28
  176.2 10.9 %collective-permute-start.48 = (bf16[64,1024]{1,0:T(8,128)(2,1)S(1)}, bf16[64,1024]{1,0:T(8,128)(2,1)S(1)}, u32[]{:S(2)}, u32[]{:S(2)}) collective-permute-start(bf16[64,1024]{1,0:T(8,128)(2,1)S(1)} %get-tuple-element.24), channel_id=1, source_target_pairs={{0,8},{8,0},{16,24},{24,16},{1,9},{9,1},{17,25},{25,17},{2,10},{10... | collective-permute-start | bytes 393224 | tf_op jit(solution)/shard_map/ppermute | solution.py:28
  182.2 11.1 %collective-permute-start.37 = (bf16[64,1024]{1,0:T(8,128)(2,1)S(1)}, bf16[64,1024]{1,0:T(8,128)(2,1)S(1)}, u32[]{:S(2)}, u32[]{:S(2)}) collective-permute-start(bf16[64,1024]{1,0:T(8,128)(2,1)S(1)} %copy-done.6), channel_id=1, source_target_pairs={{0,16},{8,24},{16,0},{24,8},{1,17},{9,25},{17,1},{25,9},{2,18},{10... | collective-permute-start | bytes 393224 | tf_op jit(solution)/shard_map/ppermute | solution.py:28
  182.8 10.6 %collective-permute-start.36 = (bf16[64,1024]{1,0:T(8,128)(2,1)S(1)}, bf16[64,1024]{1,0:T(8,128)(2,1)S(1)}, u32[]{:S(2)}, u32[]{:S(2)}) collective-permute-start(bf16[64,1024]{1,0:T(8,128)(2,1)S(1)} %copy-done.5), channel_id=1, source_target_pairs={{0,8},{8,0},{16,24},{24,16},{1,9},{9,1},{17,25},{25,17},{2,10},{10... | collective-permute-start | bytes 393224 | tf_op jit(solution)/shard_map/ppermute | solution.py:28
  185.1 10.6 %collective-permute-start.41 = (bf16[64,1792]{1,0:T(8,128)(2,1)S(1)}, bf16[64,1792]{1,0:T(8,128)(2,1)S(1)}, u32[]{:S(2)}, u32[]{:S(2)}) collective-permute-start(bf16[64,1792]{1,0:T(8,128)(2,1)S(1)} %copy-done.3), channel_id=1, source_target_pairs={{0,24},{8,16},{16,8},{24,0},{1,25},{9,17},{17,9},{25,1},{2,26},{10... | collective-permute-start | bytes 688136 | tf_op jit(solution)/shard_map/ppermute | solution.py:28
  186.4 11.5 %collective-permute-start.40 = (bf16[64,1792]{1,0:T(8,128)(2,1)S(1)}, bf16[64,1792]{1,0:T(8,128)(2,1)S(1)}, u32[]{:S(2)}, u32[]{:S(2)}) collective-permute-start(bf16[64,1792]{1,0:T(8,128)(2,1)S(1)} %copy-done.3), channel_id=1, source_target_pairs={{0,16},{8,24},{16,0},{24,8},{1,17},{9,25},{17,1},{25,9},{2,18},{10... | collective-permute-start | bytes 688136 | tf_op jit(solution)/shard_map/ppermute | solution.py:28
  187.1 11.2 %collective-permute-start.39 = (bf16[64,1792]{1,0:T(8,128)(2,1)S(1)}, bf16[64,1792]{1,0:T(8,128)(2,1)S(1)}, u32[]{:S(2)}, u32[]{:S(2)}) collective-permute-start(bf16[64,1792]{1,0:T(8,128)(2,1)S(1)} %copy-done.3), channel_id=1, source_target_pairs={{0,8},{8,0},{16,24},{24,16},{1,9},{9,1},{17,25},{25,17},{2,10},{10... | collective-permute-start | bytes 688136 | tf_op jit(solution)/shard_map/ppermute | solution.py:28
  193.3 9.7 %collective-permute-start.32 = (bf16[4,64,512]{2,1,0:T(8,128)(2,1)S(1)}, bf16[4,64,512]{2,1,0:T(8,128)(2,1)S(1)}, u32[]{:S(2)}, u32[]{:S(2)}) collective-permute-start(bf16[4,64,512]{2,1,0:T(8,128)(2,1)S(1)} %slice.131), channel_id=1, source_target_pairs={{0,1},{1,0},{2,3},{3,2},{4,5},{5,4},{6,7},{7,6},{8,9},{9,8},{10,11... | collective-permute-start | bytes 786440 | tf_op jit(solution)/shard_map/ppermute | solution.py:28
  203.1 8.7 %collective-permute-start.35 = (bf16[1,64,512]{2,1,0:T(8,128)(2,1)S(1)}, bf16[1,64,512]{2,1,0:T(8,128)(2,1)S(1)}, u32[]{:S(2)}, u32[]{:S(2)}) collective-permute-start(bf16[1,64,512]{2,1,0:T(8,128)(2,1)S(1)} %get-tuple-element.33), channel_id=1, source_target_pairs={{0,6},{1,7},{2,4},{3,5},{4,2},{5,3},{6,0},{7,1},{8,14},{9,15},{10,... | collective-permute-start | bytes 196616 | tf_op jit(solution)/shard_map/ppermute | solution.py:28
  (43 other events, 309.6 us)

commit v3 on v2

v3 whole, which is shorter than its diff:
```python
import jax
import jax.numpy as jnp
from jax import lax
from jax.experimental import pallas as pl
from jax.experimental.pallas import tpu as pltpu
from jax.sharding import PartitionSpec as P

inverse_temp = 50.0
eps = 1e-06
contract_first = (((0,), (0,)), ((), ()))
contract_last = (((1,), (1,)), ((), ()))
every = ("dp", "fsdp")


def sigmoid(v):
    return 1.0 / (1.0 + jnp.exp(-v))


def activation_grads(hidden_grad, gate_act, up_act):
    gate = sigmoid(gate_act)
    gate_grad = hidden_grad * up_act * gate * (1.0 + gate_act * (1.0 - gate))
    return gate_grad.astype(jnp.bfloat16), (hidden_grad * gate_act * gate).astype(jnp.bfloat16)


def dot32(left, right, dims=(((1,), (0,)), ((), ()))):
    return lax.dot_general(left, right, dims, preferred_element_type=jnp.float32)


def norm_of(rows):
    return jnp.sqrt(jnp.sum(rows * rows, axis=-1) + eps)


def swap(x, axis, difference):
    pairs = [(i, i ^ difference) for i in range(lax.axis_size(axis))]
    return lax.ppermute(x, axis, pairs)


def swap_core(x):
    return swap(x, "fsdp", 1)


def gather_chips(x):
    chips = lax.axis_size("fsdp") // 2
    return jnp.concatenate([x] + [swap(x, "fsdp", 2 * j) for j in range(1, chips)], axis=0)


def gather_dp(x):
    return jnp.concatenate([x] + [swap(x, "dp", j) for j in range(1, lax.axis_size("dp"))], axis=0)


def gather_core(x):
    return jnp.concatenate([x, swap_core(x)], axis=0)


def add_up(pieces):
    total = pieces[0].astype(jnp.float32)
    for piece in pieces[1:]:
        total = total + piece.astype(jnp.float32)
    return total


def sum_core(x):
    rows = x.shape[0] // 2
    return add_up([x[:rows], swap_core(x[rows:])])


def sum_over(x, axis, parts, unit):
    rows = x.shape[0] // parts
    return add_up(
        [x[:rows]]
        + [swap(x[j * rows : (j + 1) * rows], axis, j * unit) for j in range(1, parts)]
    )


def sum_chips(x):
    return sum_over(x, "fsdp", lax.axis_size("fsdp") // 2, 2)


def sum_dp(x):
    return sum_over(x, "dp", lax.axis_size("dp"), 1)


def relative_order(mine, blocks, block_rows):
    rows = blocks * block_rows
    place = lax.broadcasted_iota(jnp.int32, (rows, rows), 0)
    block, row = place // block_rows, place % block_rows
    core, chip = block // (blocks // 2), block % (blocks // 2)
    source = jnp.bitwise_xor(mine[:, None], 2 * chip + core) * block_rows + row
    return (source == lax.broadcasted_iota(jnp.int32, (rows, rows), 1)).astype(jnp.bfloat16)


def use_counts(slots, row_table, count_table, shard, shard_rows):
    devices, queries, negatives = slots.shape
    slot_cap = row_table.shape[1]
    slot = lax.broadcasted_iota(jnp.int32, (1, 1, 1, slot_cap), 3) + shard[:, None, None, None] * slot_cap
    asked = jnp.sum((slots[..., None] == slot).astype(jnp.float32), axis=2)
    live = lax.broadcasted_iota(jnp.int32, (devices, 1, slot_cap), 2) < count_table[:, None, None]
    used = jnp.where(live, asked, 0.0)
    dead = jnp.sum(asked - used, axis=-1).reshape(devices * queries)
    row = lax.broadcasted_iota(jnp.int32, (1, 1, shard_rows), 2)
    picks = (row_table[:, :, None] == row).astype(jnp.bfloat16)
    counts = lax.dot_general(
        used.astype(jnp.bfloat16),
        picks,
        (((2,), (1,)), ((0,), (0,))),
        preferred_element_type=jnp.float32,
    )
    return counts.reshape(devices * queries, shard_rows), dead


in_vmem = pl.BlockSpec(memory_space=pltpu.VMEM)
in_smem = pl.BlockSpec(memory_space=pltpu.SMEM)
in_hbm = pl.BlockSpec(memory_space=pltpu.HBM)
mib = 2**20


def held(x):
    return pltpu.with_memory_space_constraint(x, pltpu.VMEM)


def in_place(x):
    return pltpu.with_memory_space_constraint(x, pltpu.HBM)


def shape_of(shape, dtype=jnp.bfloat16):
    return jax.ShapeDtypeStruct(shape, dtype)


def kernel_call(body, in_specs, out_shape, limit, scratch=()):
    outs = out_shape if isinstance(out_shape, (list, tuple)) else [out_shape]
    specs = [in_vmem] * len(outs)
    return pl.pallas_call(
        body,
        in_specs=in_specs,
        out_specs=specs if isinstance(out_shape, (list, tuple)) else specs[0],
        out_shape=out_shape,
        scratch_shapes=list(scratch),
        compiler_params=pltpu.CompilerParams(vmem_limit_bytes=limit * mib),
    )


def together(*arrays):
    return lax.optimization_barrier(arrays)


def load(place, *arrays):
    count = len(arrays)

    def body(place_ref, *refs):
        token, sems = refs[-2:]
        copies = [
            pltpu.make_async_copy(refs[i], refs[count + i], sems.at[i]) for i in range(count)
        ]
        for copy in copies:
            copy.start()
        token[...] = jnp.zeros_like(token)
        for copy in copies:
            copy.wait()

    outs = kernel_call(
        body,
        [in_smem] + [in_hbm] * count,
        [pltpu.VMEM(a.shape, a.dtype) for a in arrays] + [shape_of((8, 128), jnp.float32)],
        2,
        [pltpu.SemaphoreType.DMA((count,))],
    )(place, *[in_place(x) for x in arrays])
    return [held(x) for x in outs[:count]] + [outs[count]]


def forward_first(order, pieces, rows, gate_weight, up_weight):
    parts, _, depth = pieces.shape
    units = gate_weight.shape[1]

    def body(order_ref, x_ref, gate_ref, up_ref, gate_out, up_out):
        for out, weight in ((gate_out, gate_ref), (up_out, up_ref)):
            total = jnp.zeros((rows, units), jnp.float32)
            for i in range(parts):
                at = pl.ds(pl.multiple_of(order_ref[i] * depth, depth), depth)
                total = total + dot32(x_ref[i, :rows], weight[at, :])
            out[...] = total

    return kernel_call(
        body,
        [in_smem, in_vmem, in_vmem, in_vmem],
        [shape_of((rows, units), jnp.float32)] * 2,
        6,
    )(order, pieces, gate_weight, up_weight)


def forward_rest(
    order, pieces, gate_part, up_part, gate_weight, up_weight, down_weight, to_relative, extra
):
    parts, _, depth = pieces.shape
    rows, units = gate_part.shape
    width = down_weight.shape[1]
    chunk = units // 4
    slots = 2

    def body(
        order_ref, x_ref, gate_in, up_in, gate_ref, up_ref, down_ref, one_hot, extra_ref,
        gate_out, up_out, own_out, other_out, held_ref, total_ref, sems,
    ):
        copies = [
            pltpu.make_async_copy(
                down_ref.at[pl.ds(i * chunk, chunk)], held_ref.at[i % slots], sems.at[i % slots]
            )
            for i in range(4)
        ]
        copies[0].start()
        copies[1].start()
        values = []
        for start, weight in ((gate_in, gate_ref), (up_in, up_ref)):
            total = start[...]
            for i in range(parts):
                at = pl.ds(pl.multiple_of(order_ref[parts + i] * depth, depth), depth)
                total = total + dot32(x_ref[i, :rows], weight[at, :])
            values.append(total)
        gate, up = values
        gate_out[:rows] = gate.astype(jnp.bfloat16)
        gate_out[rows:] = extra_ref[...]
        up_out[:rows] = up.astype(jnp.bfloat16)
        up_out[rows:] = extra_ref[...]
        hidden = (gate * sigmoid(gate) * up).astype(jnp.bfloat16)
        hidden = dot32(one_hot[...], hidden).astype(jnp.bfloat16)
        for i, copy in enumerate(copies):
            copy.wait()
            term = dot32(hidden[:, i * chunk : (i + 1) * chunk], held_ref[i % slots])
            total_ref[...] = term if i == 0 else total_ref[...] + term
            if i + slots < 4:
                copies[i + slots].start()
        own_out[...] = total_ref[: rows // 2].astype(jnp.bfloat16)
        other_out[...] = total_ref[rows // 2 :].astype(jnp.bfloat16)

    return kernel_call(
        body,
        [in_smem] + [in_vmem] * 5 + [in_hbm, in_vmem, in_vmem],
        [
            shape_of((rows + extra.shape[0], units)),
            shape_of((rows + extra.shape[0], units)),
            shape_of((rows // 2, width)),
            shape_of((rows // 2, width)),
        ],
        13,
        [
            pltpu.VMEM((slots, chunk, width), down_weight.dtype),
            pltpu.VMEM((rows, width), jnp.float32),
            pltpu.SemaphoreType.DMA((slots,)),
        ],
    )(
        order,
        pieces,
        gate_part,
        up_part,
        gate_weight,
        up_weight,
        in_place(down_weight),
        to_relative,
        extra,
    )


def input_blocks(place, order, first, second, rows, parts):
    half, _, depth = first.shape
    share = 2 * half // parts

    def body(place_ref, order_ref, first_ref, second_ref, *refs):
        outs, whole = refs[:parts], refs[parts]
        for j in range(2 * half):
            at = order_ref[j]
            to = pl.ds(pl.multiple_of((at % share) * depth, depth), depth)
            piece = first_ref[j, :rows] if j < half else second_ref[j - half, :rows]
            whole[at // share ^ place_ref[0], :, to] = piece
        for k, out in enumerate(outs):
            out[...] = whole[k]

    return kernel_call(
        body,
        [in_smem, in_smem, in_vmem, in_vmem],
        [shape_of((rows, share * depth))] * parts,
        4,
        [pltpu.VMEM((parts, rows, share * depth), first.dtype)],
    )(place, order, first, second)


def score_kernel(states, index_parts, inverse_norm, counts, dead, pad):
    pieces = len(states)
    rows, width = states[0].shape
    shard = index_parts[0].shape[0]
    chunk = width // 8

    def body(*refs):
        state_refs, refs = refs[:pieces], refs[pieces:]
        first, second, inverse_ref, counts_ref, dead_ref = refs[:5]
        outs = refs[5:]
        block = jnp.concatenate([r[...] for r in state_refs], axis=0)
        values = block.astype(jnp.float32)
        state_scale = inverse_temp / jnp.sqrt(jnp.sum(values * values, axis=1, keepdims=True) + eps)
        total = dead_ref[...]
        coeffs = []
        for k, index_ref in enumerate((first, second)):
            inverse = inverse_ref[:, k * shard : (k + 1) * shard]
            raw = dot32(block, index_ref[...], contract_last)
            weights = counts_ref[:, k * shard : (k + 1) * shard] * jnp.exp(raw * state_scale * inverse)
            total = total + jnp.sum(weights, axis=1, keepdims=True)
            coeffs.append((weights * inverse).astype(jnp.bfloat16))
        column = lax.broadcasted_iota(jnp.int32, (pieces * rows, pad), 1)
        last = jnp.where(column == 0, total, 0.0).astype(jnp.bfloat16)
        for p in range(pieces):
            outs[p][:, width:] = last[p * rows : (p + 1) * rows]
        for i in range(width // chunk):
            at = pl.ds(i * chunk, chunk)
            pull = dot32(coeffs[0], first[:, at]) + dot32(coeffs[1], second[:, at])
            for p in range(pieces):
                outs[p][:, at] = pull[p * rows : (p + 1) * rows].astype(jnp.bfloat16)

    return kernel_call(
        body,
        [in_vmem] * (pieces + 5),
        [shape_of((rows, width + pad))] * pieces,
        13,
    )(*states, *index_parts, inverse_norm, counts, dead)


def backward_hidden(order, own_rows, other_rows, down_weight, gate_act, up_act, to_relative, parts):
    half, width = own_rows.shape
    rows, units = 2 * half, down_weight.shape[0]
    part = width // parts
    chunk = 256 if units % 256 == 0 else units
    chunks = units // chunk
    slots = min(chunks, 3)

    def body(order_ref, own_ref, other_ref, down_ref, gate_ref, up_ref, one_hot, *refs):
        gate_out, up_out = refs[:2]
        outs, (grad_ref, held_ref, sems) = refs[2:-3], refs[-3:]
        spans = [pl.ds(i * chunk, chunk) for i in range(chunks)]
        copies = [
            pltpu.make_async_copy(down_ref.at[at], held_ref.at[i % slots], sems.at[i % slots])
            for i, at in enumerate(spans)
        ]
        for copy in copies[: max(slots - 1, 1)]:
            copy.start()
        grad = jnp.concatenate([own_ref[...], other_ref[...]], axis=0)
        grad_ref[...] = dot32(one_hot[...], grad, contract_first).astype(jnp.bfloat16)
        for k, out in enumerate(outs):
            out[:, units:] = grad_ref[:, pl.ds(pl.multiple_of(order_ref[k] * part, part), part)]
        for i, at in enumerate(spans):
            copies[i].wait()
            if i + slots - 1 < chunks and slots > 1:
                copies[i + slots - 1].start()
            hidden_grad = dot32(grad_ref[...], held_ref[i % slots], contract_last)
            for out in outs:
                out[:, at] = hidden_grad.astype(jnp.bfloat16)
            gate_out[:, at], up_out[:, at] = activation_grads(
                hidden_grad,
                gate_ref[:rows, at].astype(jnp.float32),
                up_ref[:rows, at].astype(jnp.float32),
            )

    outs = kernel_call(
        body,
        [in_smem, in_vmem, in_vmem, in_hbm, in_vmem, in_vmem, in_vmem],
        [shape_of((rows, units))] * 2 + [shape_of((rows, units + part))] * parts,
        13,
        [
            pltpu.VMEM((rows, width), jnp.bfloat16),
            pltpu.VMEM((slots, chunk, width), down_weight.dtype),
            pltpu.SemaphoreType.DMA((slots,)),
        ],
    )(order, own_rows, other_rows, in_place(down_weight), gate_act, up_act, to_relative)
    return outs[0], outs[1], outs[2:]


def backward_input(order, gate_grad, up_grad, gate_weight, up_weight):
    rows, units = gate_grad.shape
    width = gate_weight.shape[0]
    blocks = order.shape[0]
    depth = width // (2 * blocks)
    slots = 3

    def body(order_ref, gate_grad_ref, up_grad_ref, gate_ref, up_ref, out, held_ref, sems):
        def copies_of(n):
            at = pl.ds(pl.multiple_of(order_ref[n] * depth, depth), depth)
            return [
                pltpu.make_async_copy(source.at[at], held_ref.at[k, n % slots], sems.at[k, n % slots])
                for k, source in enumerate((gate_ref, up_ref))
            ]

        for n in range(slots - 1):
            for copy in copies_of(n):
                copy.start()
        for n in range(blocks):
            for copy in copies_of(n):
                copy.wait()
            if n + slots - 1 < blocks:
                for copy in copies_of(n + slots - 1):
                    copy.start()
            block = dot32(gate_grad_ref[...], held_ref[0, n % slots], contract_last) + dot32(
                up_grad_ref[...], held_ref[1, n % slots], contract_last
            )
            out[n] = block.astype(jnp.bfloat16)

    return kernel_call(
        body,
        [in_smem, in_vmem, in_vmem, in_hbm, in_hbm],
        shape_of((blocks, rows, depth)),
        14,
        [
            pltpu.VMEM((2, slots, depth, units), gate_weight.dtype),
            pltpu.SemaphoreType.DMA((2, slots)),
        ],
    )(order, gate_grad, up_grad, in_place(gate_weight), in_place(up_weight))


def weight_grads(input_columns, grads, gate_acts, up_acts):
    groups = len(grads)
    rows, units = grads[0].shape[0], gate_acts[0].shape[1]
    width = input_columns.shape[0]
    chunk = 256 if units % 256 == 0 else units

    def body(x_ref, *refs):
        at = pl.ds(0, units)
        if chunk < units:
            at = pl.ds(pl.multiple_of(pl.program_id(0) * chunk, chunk), chunk)
        hidden_grad, gate, up = (
            jnp.concatenate([r[:rows, at] for r in refs[k * groups : (k + 1) * groups]], axis=0)
            for k in range(3)
        )
        gate_out, up_out = refs[3 * groups :]
        gate_grad, up_grad = activation_grads(
            hidden_grad.astype(jnp.float32), gate.astype(jnp.float32), up.astype(jnp.float32)
        )
        gate_out[...] = dot32(x_ref[...], gate_grad).astype(jnp.bfloat16)
        up_out[...] = dot32(x_ref[...], up_grad).astype(jnp.bfloat16)

    return pl.pallas_call(
        body,
        grid=(units // chunk,),
        in_specs=[in_vmem] * (1 + 3 * groups),
        out_specs=[pl.BlockSpec((width, chunk), lambda i: (0, i))] * 2,
        out_shape=[shape_of((width, units))] * 2,
        compiler_params=pltpu.CompilerParams(vmem_limit_bytes=12 * mib),
    )(input_columns, *grads, *gate_acts, *up_acts)


def shards(
    mlp_input,
    residual_in,
    gate_weight,
    up_weight,
    down_weight,
    span_index,
    positive_keys,
    request_rows,
    request_counts,
    negative_slots,
):
    dp_count = lax.axis_size("dp")
    fsdp_count = lax.axis_size("fsdp")
    chips = fsdp_count // 2
    place = jnp.stack([lax.axis_index("dp"), lax.axis_index("fsdp")])
    my_dp, my_fsdp = place[:1], place[1:]
    me = my_dp * fsdp_count + my_fsdp
    width = span_index.shape[1]
    own_queries = negative_slots.shape[0]
    group_rows = mlp_input.shape[0]
    j = jnp.arange(fsdp_count, dtype=jnp.int32)
    fsdp_order = jnp.bitwise_xor(my_fsdp, 2 * (j % chips) + j // chips).astype(jnp.int32)
    dp_order = jnp.bitwise_xor(my_dp, jnp.arange(dp_count, dtype=jnp.int32)).astype(jnp.int32)
    to_relative = relative_order(my_fsdp, fsdp_count, own_queries)
    j = jnp.arange(dp_count * chips, dtype=jnp.int32)
    asker = jnp.bitwise_xor(my_dp, j // chips) * fsdp_count + jnp.bitwise_xor(
        my_fsdp, 2 * (j % chips)
    )
    both = jnp.concatenate([me, jnp.bitwise_xor(me, 1)])
    place, fsdp_order, dp_order, to_relative, asker, both = together(
        place, fsdp_order, dp_order, to_relative, asker, both
    )

    slot_cap, negatives = request_rows.shape[2], negative_slots.shape[1]
    slots = jnp.concatenate([negative_slots // slot_cap, negative_slots % slot_cap], axis=1)
    slots = jnp.pad(slots, ((0, 0), (0, mlp_input.shape[1] - 2 * negatives)))
    message = jnp.concatenate([mlp_input, slots.astype(jnp.bfloat16)], axis=0)
    gate_held, up_held, loaded = load(place, gate_weight, up_weight)
    first = gather_chips(message[None]) + loaded[0, 0].astype(jnp.bfloat16)
    second = swap_core(first)
    gate_part, up_part = forward_first(fsdp_order, first, group_rows, gate_held, up_held)
    gate_part, up_part, second, span_later = together(gate_part, up_part, second, span_index)
    units = up_weight.shape[1]
    bands = units // (2 * negatives)
    extra = [first[c, group_rows:, : 2 * negatives] for c in range(chips)]
    extra = [jnp.concatenate(extra[i : i + bands], axis=1) for i in range(0, chips, bands)]
    extra = [jnp.pad(x, ((0, 0), (0, units - x.shape[1]))) for x in extra]
    extra = jnp.concatenate(extra, axis=0)
    other_index = swap_core(span_later)
    gate_act, up_act, own_part, other_part = forward_rest(
        fsdp_order,
        second,
        gate_part,
        up_part,
        gate_held,
        up_held,
        down_weight,
        to_relative,
        extra,
    )

    near, far = 1, dp_count // 2
    own_part, other_part, other_index = together(own_part, other_part, other_index)
    own_part, received, request_rows, request_counts, span_later = together(
        own_part, swap_core(other_part), request_rows, request_counts, span_later
    )
    branch = add_up([own_part, received]).astype(jnp.bfloat16)

    tables = jnp.concatenate([request_rows[:, 0, :], request_counts], axis=1)[None]
    tables = gather_core(tables)
    top_state, gate_near, up_far, own_norm, other_index, tables = together(
        sum_chips(branch) + residual_in.astype(jnp.float32),
        swap(gate_act, "dp", near),
        swap(up_act, "dp", far),
        norm_of(span_later.astype(jnp.float32)),
        other_index,
        tables,
    )
    row_norm = norm_of(top_state)
    unit_rows = top_state / row_norm[:, None]

    states, gate_far, up_near, other_norm, span_later, tables, positive_keys = together(
        gather_chips(top_state.astype(jnp.bfloat16)),
        swap(
            jnp.concatenate([gate_act[:group_rows], gate_near[group_rows:]], axis=0), "dp", far
        ),
        swap(up_act, "dp", near),
        norm_of(other_index.astype(jnp.float32)),
        span_later,
        tables,
        positive_keys,
    )
    index_norm = jnp.concatenate([own_norm, other_norm], axis=0)
    slots = [x[group_rows:] for x in (gate_act, gate_near, up_far, gate_far)]
    slots = jnp.stack(slots).astype(jnp.int32)
    slots = [
        slots[
            :,
            c // bands * own_queries : (c // bands + 1) * own_queries,
            c % bands * 2 * negatives : (c % bands + 1) * 2 * negatives,
        ]
        for c in range(chips)
    ]
    slots = jnp.stack(slots, axis=1).reshape(dp_count * chips, own_queries, 2 * negatives)
    slots = slots[..., :negatives] * slot_cap + slots[..., negatives:]
    tables = jnp.take(tables, asker, axis=1)
    counts, dead = [], 0.0
    for k in range(2):
        shard_counts, shard_dead = use_counts(
            slots,
            tables[k, :, :-1],
            tables[k, :, -1],
            both[k : k + 1],
            span_index.shape[0],
        )
        counts.append(shard_counts)
        dead = dead + shard_dead
    counts = jnp.concatenate(counts, axis=1)
    states = [states] + [swap(states, "dp", k) for k in range(1, dp_count)]
    own_held, loaded = load(place, span_later)
    counts, dead, loaded, *states = together(counts, dead, loaded, *states)
    counts = counts + loaded[0, 0]
    index_parts = [own_held, held(other_index)]
    pulls = score_kernel(
        states, index_parts, (1.0 / index_norm)[None, :], counts, dead[:, None], 128
    )

    sums = add_up([pulls[0]] + [swap(pulls[k], "dp", k) for k in range(1, dp_count)])
    sums, gate_near, up_far = together(sums.astype(jnp.bfloat16), gate_near, up_far)
    sums, gate_last, up_last, first, second = together(
        sum_chips(sums), swap(gate_near, "dp", far), swap(up_far, "dp", near), first, second
    )
    negative_total = sums[:, width]
    positive_rows = positive_keys.astype(jnp.float32)
    positive_unit = positive_rows / norm_of(positive_rows)[:, None]
    positive_score = inverse_temp * jnp.sum(unit_rows * positive_unit, axis=-1)
    exp_total = jnp.exp(positive_score) + negative_total
    query_loss = jnp.log(exp_total) - positive_score
    pull = (sums[:, :width] - negative_total[:, None] * positive_unit) / exp_total[:, None]
    inner = jnp.sum(pull * unit_rows, axis=-1)
    head_grad = (
        inverse_temp * (pull - inner[:, None] * unit_rows) / row_norm[:, None]
    ).astype(jnp.bfloat16)

    blocks = input_blocks(place, fsdp_order, first, second, group_rows, dp_count)
    own_rows, *blocks = together(
        gather_chips(head_grad),
        blocks[0],
        swap(blocks[1], "dp", 1),
        swap(blocks[2], "dp", 2),
        blocks[3],
    )
    own_rows, other_rows = together(own_rows, swap_core(own_rows))
    gates = [gate_act, gate_near, gate_far, gate_last]
    ups = [up_act, up_near, up_far, up_last]
    hidden_all = jnp.concatenate(
        [
            (g * sigmoid(g) * u).astype(jnp.bfloat16).T
            for g, u in (
                (g[:group_rows].astype(jnp.float32), u[:group_rows].astype(jnp.float32))
                for g, u in zip(gates, ups)
            )
        ],
        axis=1,
    )

    own_gate_grad, own_up_grad, grads = backward_hidden(
        dp_order, own_rows, other_rows, down_weight, gate_act, up_act, to_relative, dp_count
    )
    own_gate_grad, own_up_grad, last_block = together(
        own_gate_grad, own_up_grad, swap(blocks[3], "dp", 3)
    )
    grads = [grads[0]] + [swap(grads[k], "dp", k) for k in range(1, dp_count)]
    other_blocks = backward_input(
        fsdp_order[chips:], own_gate_grad, own_up_grad, gate_weight, up_weight
    )
    other_blocks, own_gate_grad, own_up_grad = together(other_blocks, own_gate_grad, own_up_grad)
    own_blocks = backward_input(
        fsdp_order[:chips], own_gate_grad, own_up_grad, gate_weight, up_weight
    )
    own_blocks, received, *grads = together(own_blocks, swap_core(other_blocks), *grads)
    blocks_sum = add_up([own_blocks, received]).astype(jnp.bfloat16)
    input_grad = sum_chips(blocks_sum)[0].astype(jnp.bfloat16)

    grad_columns = jnp.concatenate([g[:, units:] for g in grads], axis=0)
    down_grad = dot32(hidden_all, grad_columns).astype(jnp.bfloat16)
    input_columns = jnp.concatenate(blocks[:3] + [last_block], axis=0).T
    gate_grad, up_grad = weight_grads(input_columns, grads, gates, ups)
    return (query_loss, input_grad, gate_grad, up_grad, down_grad)


def solution(mesh):
    return jax.shard_map(
        shards,
        mesh=mesh,
        in_specs=(
            P("dp", "fsdp"),
            P(("dp", "fsdp"), None),
            P(None, "fsdp"),
            P(None, "fsdp"),
            P("fsdp", None),
            P(("dp", "fsdp"), None),
            P(("dp", "fsdp"), None),
            P(None, ("dp", "fsdp"), None),
            P(None, ("dp", "fsdp")),
            P(("dp", "fsdp"), None),
        ),
        out_specs=(
            P(("dp", "fsdp")),
            P("dp", "fsdp"),
            P("dp", "fsdp"),
            P("dp", "fsdp"),
            P("fsdp", "dp"),
        ),
        check_vma=False,
    )
```

time: 213 us -> 191 us (0.90)
  Pallas kernels: 0 us -> 67.6 us
  matrix products: 66.7 us -> 4.38 us
  waiting for transfers between devices: 58 us -> 25.6 us
  starting transfers between devices: 60.7 us -> 49.3 us
  local copies, waits for them, and re-layouts: 6.87 us -> 16.5 us
  other arithmetic: 18.8 us -> 24 us
    pallas_call x0 -> x10, Pallas kernels: none -> 67.6 us  [the longest x2 15.3 us: backward_input(): kernel_call(body, [in_smem, in_vmem, in_vmem, in_hbm, in_hbm], shape_of((...]
    dot_general x12 -> x1, matrix products: 65.3 us -> 2.99 us  [dot32(): lax.dot_general(left, right, dims, preferred_element_type=jnp.float32)]
    ppermute x51 -> x42, waiting for transfers between devices: 58 us -> 25.6 us  [swap(): return lax.ppermute(x, axis, pairs)]
    ppermute x51 -> x42, starting transfers between devices: 60.7 us -> 49.3 us  [swap(): return lax.ppermute(x, axis, pairs)]
    concatenate x2 -> x1, other arithmetic: 6.29 us -> 0.04 us  [gather_core(): return jnp.concatenate([x, swap_core(x)], axis=0)]
    slice x2 -> x9, local copies, waits for them, and re-layouts: 0.04 us -> 4.45 us  [the longest x4 2.75 us: shards(): grad_columns = jnp.concatenate([g[:, units:] for g in grads], axis=0)]
    transpose x0 -> x5, other arithmetic: none -> 3.72 us  [the longest x4 3.37 us: shards(): (g * sigmoid(g) * u).astype(jnp.bfloat16)]
    add x3 -> x7, other arithmetic: 0.01 us -> 3.58 us  [the longest x1 1.73 us: shards(): counts = counts + loaded[0, 0]]
  transfers between devices with their start and end apart: 51 -> 42, of which waited for: 26 -> 13; matrix products, arithmetic and copies ran while one was open for 43% -> 15% of each run, Pallas kernels for 0% -> 32%
where the time goes in v3:
time: 191 us; the launch traced here: 190 us
  Pallas kernels  67.6 us (35%)
  starting transfers between devices  49.3 us (26%)
  waiting for transfers between devices  25.6 us (13%)
  other arithmetic  24 us (13%)
  local copies, waits for them, and re-layouts  16.5 us (9%)
  matrix products  4.38 us (2%)
  between operations  2.66 us (1%)
    ppermute x42, starting transfers between devices, swap(): return lax.ppermute(x, axis, pairs)  49.3 us
    ppermute x42, waiting for transfers between devices, swap(): return lax.ppermute(x, axis, pairs)  25.6 us
    pallas_call x2, Pallas kernels, backward_input(): kernel_call(body, [in_smem, in_vmem, in_vmem, in_hbm, in_hbm], shape_of((...  15.3 us
    pallas_call x2, Pallas kernels, load(): kernel_call(body, [in_smem] + [in_hbm] * count, [pltpu.VMEM(a.shape, a.dt...  12.7 us
    pallas_call x1, Pallas kernels, backward_hidden(): kernel_call(body, [in_smem, in_vmem, in_vmem, in_hbm, in_vmem, in_vmem, i...  11.4 us
    pallas_call x1, Pallas kernels, forward_rest(): kernel_call(body, [in_smem] + [in_vmem] * 5 + [in_hbm, in_vmem, in_vmem],...  10.8 us
    pallas_call x1, Pallas kernels, weight_grads(): pl.pallas_call(body, grid=(units // chunk,), in_specs=[in_vmem] * (1 + 3...  7.26 us
    unnamed x50, local copies, waits for them, and re-layouts  6.34 us
  transfers between devices with their start and end apart: 42, of which 13 were waited for; matrix products, arithmetic and copies ran while one was open for 15% of the time, Pallas kernels for 32%

profile of v3, /device:TPU:0, one launch (start us, length us, event | category | flops | bytes accessed | tf_op | source)
XLA Modules:
  0.0 190.0 jit_solution(15504377189630236787)
XLA Ops:
  2.3 5.0 %collective-permute-start.2 = (bf16[1,72,512]{2,1,0:T(8,128)(2,1)S(1)}, bf16[1,72,512]{2,1,0:T(8,128)(2,1)S(1)}, u32[]{:S(2)}, u32[]{:S(2)}) collective-permute-start(bf16[1,72,512]{2,1,0:T(8,128)(2,1)S(1)} %maximum_bitcast_fusion.1), channel_id=1, source_target_pairs={{0,6},{1,7},{2,4},{3,5},{4,2},{5,3},{6,0},{7,1},{8,14},{9,15},{10,... | collective-permute-start | bytes 221192 | tf_op jit(solution)/shard_map/ppermute | solution.py:35
  8.2 10.0 %shard_map.137 = (bf16[4096,1792]{1,0:T(8,128)(2,1)S(1)}, bf16[4096,1792]{1,0:T(8,128)(2,1)S(1)}, f32[8,128]{1,0:T(8,128)S(1)}) custom-call(s32[2]{0:T(128)S(1)} %get-tuple-element.98.place_ref, bf16[4096,1792]{1,0:T(8,128)(2,1)} %gate_ref.3, bf16[4096,1792]{1,0:T(8,128)(2,1)} %up_ref.3), custom_call_target="tpu_custom_call" | custom-call | tf_op jit(solution)/shard_map/pallas_call | solution.py:160
  19.5 3.2 %shard_map.138 = (f32[64,1792]{1,0:T(8,128)S(1)}, f32[64,1792]{1,0:T(8,128)S(1)}) custom-call(s32[8]{0:T(128)S(1)} %fusion.78.order_ref, bf16[4,72,512]{2,1,0:T(8,128)(2,1)S(1)} %maximum_add_fusion.x_ref.first_ref, bf16[4096,1792]{1,0:T(8,128)(2,1)S(1)} %get-tuple-element.100.gate_ref, bf16[4096,1792]{1,0:T(8,128)(2,1)S(1)} %get-tuple-element.101.up_ref), custom_call_target="tpu_custom_call" | custom-call | tf_op jit(solution)/shard_map/pallas_call | solution.py:182
  26.3 10.8 %shard_map.139 = (bf16[72,1792]{1,0:T(8,128)(2,1)S(1)}, bf16[72,1792]{1,0:T(8,128)(2,1)S(1)}, bf16[32,4096]{1,0:T(8,128)(2,1)S(1)}, bf16[32,4096]{1,0:T(8,128)(2,1)S(1)}) custom-call(s32[8]{0:T(128)S(1)} %fusion.78.order_ref, bf16[4,72,512]{2,1,0:T(8,128)(2,1)S(1)} %collective-permute-done.3.x_ref.second_ref, f32[64,1792]{1,0:T(8,128)S(1)} %get-tuple-element.105.gate_in, ...), custom_call_target="tpu_custom_call" | custom-call | tf_op jit(solution)/shard_map/pallas_call | solution.py:234
  42.9 3.7 %collective-permute-start.8 = (bf16[8,4096]{1,0:T(8,128)(2,1)S(1)}, bf16[8,4096]{1,0:T(8,128)(2,1)S(1)}, u32[]{:S(2)}, u32[]{:S(2)}) collective-permute-start(bf16[8,4096]{1,0:T(8,128)(2,1)S(1)} %get-tuple-element.208), channel_id=1, source_target_pairs={{0,6},{1,7},{2,4},{3,5},{4,2},{5,3},{6,0},{7,1},{8,14},{9,15},{10,... | collective-permute-start | bytes 196616 | tf_op jit(solution)/shard_map/ppermute | solution.py:35
  53.8 2.5 %collective-permute-start.14 = (bf16[8,4096]{1,0:T(8,128)(2,1)S(1)}, bf16[8,4096]{1,0:T(8,128)(2,1)S(1)}, u32[]{:S(2)}, u32[]{:S(2)}) collective-permute-start(bf16[8,4096]{1,0:T(8,128)(2,1)S(1)} %get-tuple-element.213), channel_id=1, source_target_pairs={{0,6},{1,7},{2,4},{3,5},{4,2},{5,3},{6,0},{7,1},{8,14},{9,15},{10,... | collective-permute-start | bytes 196616 | tf_op jit(solution)/shard_map/ppermute | solution.py:35
  59.4 3.1 %multiply_reduce_fusion = f32[512]{0:T(512)S(1)} fusion(bf16[512,4096]{1,0:T(8,128)(2,1)} %collective-permute-done.4.refs_5_), kind=kLoop, calls=%fused_computation.1 | loop fusion | flops 6290944 | bytes 4196352 | tf_op jit(solution)/shard_map/reduce_sum | solution.py:30
  63.2 2.8 %collective-permute-done.15.refs_6_ = bf16[72,1792]{1,0:T(8,128)(2,1)S(1)} collective-permute-done((bf16[72,1792]{1,0:T(8,128)(2,1)S(1)}, bf16[72,1792]{1,0:T(8,128)(2,1)S(1)}, u32[]{:S(2)}, u32[]{:S(2)}) %collective-permute-start.15) | collective-permute-done | bytes 258080 | tf_op jit(solution)/shard_map/ppermute | solution.py:35
  68.6 2.4 %collective-permute-start.19 = (bf16[32,4096]{1,0:T(8,128)(2,1)S(1)}, bf16[32,4096]{1,0:T(8,128)(2,1)S(1)}, u32[]{:S(2)}, u32[]{:S(2)}) collective-permute-start(bf16[32,4096]{1,0:T(8,128)(2,1)S(1)} %pad_maximum_fusion.1.refs_0_), channel_id=1, source_target_pairs={{0,24},{8,16},{16,8},{24,0},{1,25},{9,17},{17,9},{25,1},{2,26},{10... | collective-permute-start | bytes 786440 | tf_op jit(solution)/shard_map/ppermute | solution.py:35
  72.7 2.1 %convert_reduce_fusion.1 = (f32[16,8,32]{2,1,0:T(8,128)S(1)}, f32[16,8,32]{2,1,0:T(8,128)S(1)}) fusion(s32[16,8,64]{2,1,0:T(8,128)S(1)} %slice_add_fusion, s32[32]{0:T(128)} %iota_add_fusion.1, s32[32]{0:T(128)} %iota_add_fusion), kind=kLoop, calls=%fused_computation.5 | loop fusion | flops 1564672 | bytes 65792 | tf_op jit(solution)/shard_map/reduce_sum | solution.py:96
  76.3 2.7 %shard_map.140 = (bf16[512,4096]{1,0:T(8,128)(2,1)S(1)}, f32[8,128]{1,0:T(8,128)S(1)}) custom-call(s32[2]{0:T(128)S(1)} %get-tuple-element.98.place_ref, bf16[512,4096]{1,0:T(8,128)(2,1)} %refs_0_.2), custom_call_target="tpu_custom_call" | custom-call | tf_op jit(solution)/shard_map/pallas_call | solution.py:160
  84.6 2.2 %copy-done.1 = bf16[512,4096]{1,0:T(8,128)(2,1)S(1)} copy-done((bf16[512,4096]{1,0:T(8,128)(2,1)S(1)}, bf16[512,4096]{1,0:T(8,128)(2,1)}, u32[]{:S(2)}) %copy-start.1) | copy-done | bytes 4194328
  86.8 6.3 %shard_map.141 = (bf16[32,4224]{1,0:T(8,128)(2,1)S(1)}, bf16[32,4224]{1,0:T(8,128)(2,1)S(1)}, bf16[32,4224]{1,0:T(8,128)(2,1)S(1)}, bf16[32,4224]{1,0:T(8,128)(2,1)S(1)}) custom-call(bf16[32,4096]{1,0:T(8,128)(2,1)S(1)} %pad_maximum_fusion.1.refs_0_, bf16[32,4096]{1,0:T(8,128)(2,1)S(1)} %collective-permute-done.17.refs_1_, ...), custom_call_target="tpu_custom_call" | custom-call | tf_op jit(solution)/shard_map/pallas_call | solution.py:316
  96.9 5.8 %collective-permute-done.22 = bf16[32,4224]{1,0:T(8,128)(2,1)S(1)} collective-permute-done((bf16[32,4224]{1,0:T(8,128)(2,1)S(1)}, bf16[32,4224]{1,0:T(8,128)(2,1)S(1)}, u32[]{:S(2)}, u32[]{:S(2)}) %collective-permute-start.22) | collective-permute-done | bytes 270368 | tf_op jit(solution)/shard_map/ppermute | solution.py:35
  105.6 2.7 %collective-permute-start.25 = (bf16[8,4224]{1,0:T(8,128)(2,1)}, bf16[8,4224]{1,0:T(8,128)(2,1)S(1)}, u32[]{:S(2)}, u32[]{:S(2)}) collective-permute-start(bf16[8,4224]{1,0:T(8,128)(2,1)} %get-tuple-element.202), channel_id=1, source_target_pairs={{0,6},{1,7},{2,4},{3,5},{4,2},{5,3},{6,0},{7,1},{8,14},{9,15},{10,... | collective-permute-start | bytes 202760 | tf_op jit(solution)/shard_map/ppermute | solution.py:35
  112.1 2.2 %collective-permute-done.24 = bf16[8,4224]{1,0:T(8,128)(2,1)} collective-permute-done((bf16[8,4224]{1,0:T(8,128)(2,1)S(1)}, bf16[8,4224]{1,0:T(8,128)(2,1)}, u32[]{:S(2)}, u32[]{:S(2)}) %collective-permute-start.24) | collective-permute-done | bytes 67616 | tf_op jit(solution)/shard_map/ppermute | solution.py:35
  118.9 2.8 %collective-permute-start.30 = (bf16[8,4096]{1,0:T(8,128)(2,1)S(1)}, bf16[8,4096]{1,0:T(8,128)(2,1)}, u32[]{:S(2)}, u32[]{:S(2)}) collective-permute-start(bf16[8,4096]{1,0:T(8,128)(2,1)S(1)} %divide_convert_fusion), channel_id=1, source_target_pairs={{0,6},{1,7},{2,4},{3,5},{4,2},{5,3},{6,0},{7,1},{8,14},{9,15},{10,... | collective-permute-start | bytes 196616 | tf_op jit(solution)/shard_map/ppermute | solution.py:35
  128.9 3.2 %collective-permute-done.31 = bf16[64,1024]{0,1:T(8,128)(2,1)S(1)} collective-permute-done((bf16[64,1024]{0,1:T(8,128)(2,1)S(1)}, bf16[64,1024]{0,1:T(8,128)(2,1)S(1)}, u32[]{:S(2)}, u32[]{:S(2)}) %collective-permute-start.31) | collective-permute-done | bytes 131104 | tf_op jit(solution)/shard_map/ppermute | solution.py:35
  137.0 11.4 %shard_map.143 = (bf16[64,1792]{1,0:T(8,128)(2,1)S(1)}, bf16[64,1792]{1,0:T(8,128)(2,1)S(1)}, bf16[64,2816]{1,0:T(8,128)(2,1)S(1)}, bf16[64,2816]{1,0:T(8,128)(2...) custom-call(s32[4]{0:T(128)S(1)} %iota_xor_fusion.order_ref, bf16[32,4096]{1,0:T(8,128)(2,1)S(1)} %pad_maximum_fusion.2.own_ref, ...), custom_call_target="tpu_custom_call" | custom-call | tf_op jit(solution)/shard_map/pallas_call | solution.py:359
  153.4 7.8 %shard_map.144 = bf16[4,64,512]{2,1,0:T(8,128)(2,1)S(1)} custom-call(s32[4]{0:T(128)S(1)} %get-tuple-element.222.order_ref, bf16[64,1792]{1,0:T(8,128)(2,1)S(1)} %get-tuple-element.167.gate_grad_ref, bf16[64,1792]{1,0:T(8,128)(2,1)S(1)} %get-tuple-element.168.up_grad_ref, bf16[4096,1792]{1,0:T(8,128)(2,1)} %gate_ref.3, bf16[4096,1792]{1,0:T(8,128)(2,1)} %up_ref.3), custom_call_target="tpu_custom_call" | custom-call | tf_op jit(solution)/shard_map/pallas_call | solution.py:402
  162.7 7.5 %shard_map.145 = bf16[4,64,512]{2,1,0:T(8,128)(2,1)S(1)} custom-call(s32[4]{0:T(128)S(1)} %get-tuple-element.223.order_ref, bf16[64,1792]{1,0:T(8,128)(2,1)S(1)} %get-tuple-element.167.gate_grad_ref, bf16[64,1792]{1,0:T(8,128)(2,1)S(1)} %get-tuple-element.168.up_grad_ref, bf16[4096,1792]{1,0:T(8,128)(2,1)} %gate_ref.3, bf16[4096,1792]{1,0:T(8,128)(2,1)} %up_ref.3), custom_call_target="tpu_custom_call" | custom-call | tf_op jit(solution)/shard_map/pallas_call | solution.py:402
  171.8 2.8 %collective-permute-start.41 = (bf16[1,64,512]{2,1,0:T(8,128)(2,1)S(1)}, bf16[1,64,512]{2,1,0:T(8,128)(2,1)S(1)}, u32[]{:S(2)}, u32[]{:S(2)}) collective-permute-start(bf16[1,64,512]{2,1,0:T(8,128)(2,1)S(1)} %get-tuple-element.205), channel_id=1, source_target_pairs={{0,6},{1,7},{2,4},{3,5},{4,2},{5,3},{6,0},{7,1},{8,14},{9,15},{10,... | collective-permute-start | bytes 196616 | tf_op jit(solution)/shard_map/ppermute | solution.py:35
  179.0 3.0 %convolution_convert_fusion = bf16[1792,1024]{1,0:T(8,128)(2,1)} fusion(bf16[1792,64]{0,1:T(8,128)(2,1)S(1)} %copy-done.19, bf16[1792,64]{0,1:T(8,128)(2,1)S(1)} %copy-done.17, bf16[1792,64]{0,1:T(8,128)(2,1)S(1)} %copy-done.18, bf16[1792,64]{0,1:T(8,128)(2,1)S(1)} %copy-done.16, bf16[64,1024]{1,0:T(8,128)(2,1)S(1)} %slice.202, ...), kind=kOutput, calls=%fused_computation.3 | convolution fusion | flops 947126272 | bytes 5111808 | tf_op jit(solution)/shard_map/dot_general | solution.py:26
  182.0 7.3 %shard_map.146 = (bf16[1024,1792]{1,0:T(8,128)(2,1)}, bf16[1024,1792]{1,0:T(8,128)(2,1)}) custom-call(bf16[1024,256]{1,0:T(8,128)(2,1)S(1)} %maximum_bitcast_fusion.x_ref, bf16[64,2816]{1,0:T(8,128)(2,1)S(1)} %get-tuple-element.180.refs_0_, bf16[64,2816]{1,0:T(8,128)(2,1)} %collective-permute-done.36.refs_1_, ...), custom_call_target="tpu_custom_call" | custom-call | tf_op jit(solution)/shard_map/pallas_call | solution.py:435
  (214 shorter events, 73.9 us)
Async XLA Ops:
  2.3 16.5 %collective-permute-start.2 = (bf16[1,72,512]{2,1,0:T(8,128)(2,1)S(1)}, bf16[1,72,512]{2,1,0:T(8,128)(2,1)S(1)}, u32[]{:S(2)}, u32[]{:S(2)}) collective-permute-start(bf16[1,72,512]{2,1,0:T(8,128)(2,1)S(1)} %maximum_bitcast_fusion.1), channel_id=1, source_target_pairs={{0,6},{1,7},{2,4},{3,5},{4,2},{5,3},{6,0},{7,1},{8,14},{9,15},{10,... | collective-permute-start | bytes 221192 | tf_op jit(solution)/shard_map/ppermute | solution.py:35
  7.3 11.4 %collective-permute-start.1 = (bf16[1,72,512]{2,1,0:T(8,128)(2,1)S(1)}, bf16[1,72,512]{2,1,0:T(8,128)(2,1)S(1)}, u32[]{:S(2)}, u32[]{:S(2)}) collective-permute-start(bf16[1,72,512]{2,1,0:T(8,128)(2,1)S(1)} %maximum_bitcast_fusion.1), channel_id=1, source_target_pairs={{0,4},{1,5},{2,6},{3,7},{4,0},{5,1},{6,2},{7,3},{8,12},{9,13},{10,... | collective-permute-start | bytes 221192 | tf_op jit(solution)/shard_map/ppermute | solution.py:35
  7.3 11.4 %collective-permute-start = (bf16[1,72,512]{2,1,0:T(8,128)(2,1)S(1)}, bf16[1,72,512]{2,1,0:T(8,128)(2,1)S(1)}, u32[]{:S(2)}, u32[]{:S(2)}) collective-permute-start(bf16[1,72,512]{2,1,0:T(8,128)(2,1)S(1)} %maximum_bitcast_fusion.1), channel_id=1, source_target_pairs={{0,2},{1,3},{2,0},{3,1},{4,6},{5,7},{6,4},{7,5},{8,10},{9,11},{10,... | collective-permute-start | bytes 221192 | tf_op jit(solution)/shard_map/ppermute | solution.py:35
  22.8 18.6 %collective-permute-start.4 = (bf16[512,4096]{1,0:T(8,128)(2,1)S(1)}, bf16[512,4096]{1,0:T(8,128)(2,1)}, u32[]{:S(2)}, u32[]{:S(2)}) collective-permute-start(bf16[512,4096]{1,0:T(8,128)(2,1)S(1)} %copy-done.4), channel_id=1, source_target_pairs={{0,1},{1,0},{2,3},{3,2},{4,5},{5,4},{6,7},{7,6},{8,9},{9,8},{10,11... | collective-permute-start | bytes 12582920 | tf_op jit(solution)/shard_map/ppermute | solution.py:35
  37.1 16.5 %collective-permute-start.9 = (bf16[72,1792]{1,0:T(8,128)(2,1)S(1)}, bf16[72,1792]{1,0:T(8,128)(2,1)S(1)}, u32[]{:S(2)}, u32[]{:S(2)}) collective-permute-start(bf16[72,1792]{1,0:T(8,128)(2,1)S(1)} %get-tuple-element.115.gate_ref.refs_4_), channel_id=1, source_target_pairs={{0,8},{8,0},{16,24},{24,16},{1,9},{9,1},{17,25},{25,17},{2,10},{10... | collective-permute-start | bytes 774152 | tf_op jit(solution)/shard_map/ppermute | solution.py:35
  38.9 14.8 %collective-permute-start.10 = (bf16[72,1792]{1,0:T(8,128)(2,1)S(1)}, bf16[72,1792]{1,0:T(8,128)(2,1)S(1)}, u32[]{:S(2)}, u32[]{:S(2)}) collective-permute-start(bf16[72,1792]{1,0:T(8,128)(2,1)S(1)} %get-tuple-element.116.up_ref.refs_8_), channel_id=1, source_target_pairs={{0,16},{8,24},{16,0},{24,8},{1,17},{9,25},{17,1},{25,9},{2,18},{10... | collective-permute-start | bytes 774152 | tf_op jit(solution)/shard_map/ppermute | solution.py:35
  49.7 13.5 %collective-permute-start.16 = (bf16[72,1792]{1,0:T(8,128)(2,1)S(1)}, bf16[72,1792]{1,0:T(8,128)(2,1)S(1)}, u32[]{:S(2)}, u32[]{:S(2)}) collective-permute-start(bf16[72,1792]{1,0:T(8,128)(2,1)S(1)} %get-tuple-element.116.up_ref.refs_8_), channel_id=1, source_target_pairs={{0,8},{8,0},{16,24},{24,16},{1,9},{9,1},{17,25},{25,17},{2,10},{10... | collective-permute-start | bytes 774152 | tf_op jit(solution)/shard_map/ppermute | solution.py:35
  53.8 9.4 %collective-permute-start.14 = (bf16[8,4096]{1,0:T(8,128)(2,1)S(1)}, bf16[8,4096]{1,0:T(8,128)(2,1)S(1)}, u32[]{:S(2)}, u32[]{:S(2)}) collective-permute-start(bf16[8,4096]{1,0:T(8,128)(2,1)S(1)} %get-tuple-element.213), channel_id=1, source_target_pairs={{0,6},{1,7},{2,4},{3,5},{4,2},{5,3},{6,0},{7,1},{8,14},{9,15},{10,... | collective-permute-start | bytes 196616 | tf_op jit(solution)/shard_map/ppermute | solution.py:35
  58.9 7.2 %collective-permute-start.15 = (bf16[72,1792]{1,0:T(8,128)(2,1)S(1)}, bf16[72,1792]{1,0:T(8,128)(2,1)S(1)}, u32[]{:S(2)}, u32[]{:S(2)}) collective-permute-start(bf16[72,1792]{1,0:T(8,128)(2,1)S(1)} %pad_maximum_fusion.3), channel_id=1, source_target_pairs={{0,16},{8,24},{16,0},{24,8},{1,17},{9,25},{17,1},{25,9},{2,18},{10... | collective-permute-start | bytes 774152 | tf_op jit(solution)/shard_map/ppermute | solution.py:35
  67.5 14.7 %collective-permute-start.17 = (bf16[32,4096]{1,0:T(8,128)(2,1)S(1)}, bf16[32,4096]{1,0:T(8,128)(2,1)S(1)}, u32[]{:S(2)}, u32[]{:S(2)}) collective-permute-start(bf16[32,4096]{1,0:T(8,128)(2,1)S(1)} %pad_maximum_fusion.1.refs_0_), channel_id=1, source_target_pairs={{0,8},{8,0},{16,24},{24,16},{1,9},{9,1},{17,25},{25,17},{2,10},{10... | collective-permute-start | bytes 786440 | tf_op jit(solution)/shard_map/ppermute | solution.py:35
  68.1 14.1 %collective-permute-start.18 = (bf16[32,4096]{1,0:T(8,128)(2,1)S(1)}, bf16[32,4096]{1,0:T(8,128)(2,1)S(1)}, u32[]{:S(2)}, u32[]{:S(2)}) collective-permute-start(bf16[32,4096]{1,0:T(8,128)(2,1)S(1)} %pad_maximum_fusion.1.refs_0_), channel_id=1, source_target_pairs={{0,16},{8,24},{16,0},{24,8},{1,17},{9,25},{17,1},{25,9},{2,18},{10... | collective-permute-start | bytes 786440 | tf_op jit(solution)/shard_map/ppermute | solution.py:35
  68.6 13.6 %collective-permute-start.19 = (bf16[32,4096]{1,0:T(8,128)(2,1)S(1)}, bf16[32,4096]{1,0:T(8,128)(2,1)S(1)}, u32[]{:S(2)}, u32[]{:S(2)}) collective-permute-start(bf16[32,4096]{1,0:T(8,128)(2,1)S(1)} %pad_maximum_fusion.1.refs_0_), channel_id=1, source_target_pairs={{0,24},{8,16},{16,8},{24,0},{1,25},{9,17},{17,9},{25,1},{2,26},{10... | collective-permute-start | bytes 786440 | tf_op jit(solution)/shard_map/ppermute | solution.py:35
  93.1 9.6 %collective-permute-start.22 = (bf16[32,4224]{1,0:T(8,128)(2,1)S(1)}, bf16[32,4224]{1,0:T(8,128)(2,1)S(1)}, u32[]{:S(2)}, u32[]{:S(2)}) collective-permute-start(bf16[32,4224]{1,0:T(8,128)(2,1)S(1)} %get-tuple-element.147), channel_id=1, source_target_pairs={{0,24},{8,16},{16,8},{24,0},{1,25},{9,17},{17,9},{25,1},{2,26},{10... | collective-permute-start | bytes 811016 | tf_op jit(solution)/shard_map/ppermute | solution.py:35
  93.7 11.1 %collective-permute-start.21 = (bf16[32,4224]{1,0:T(8,128)(2,1)S(1)}, bf16[32,4224]{1,0:T(8,128)(2,1)S(1)}, u32[]{:S(2)}, u32[]{:S(2)}) collective-permute-start(bf16[32,4224]{1,0:T(8,128)(2,1)S(1)} %get-tuple-element.146), channel_id=1, source_target_pairs={{0,16},{8,24},{16,0},{24,8},{1,17},{9,25},{17,1},{25,9},{2,18},{10... | collective-permute-start | bytes 811016 | tf_op jit(solution)/shard_map/ppermute | solution.py:35
  95.2 9.6 %collective-permute-start.20 = (bf16[32,4224]{1,0:T(8,128)(2,1)S(1)}, bf16[32,4224]{1,0:T(8,128)(2,1)S(1)}, u32[]{:S(2)}, u32[]{:S(2)}) collective-permute-start(bf16[32,4224]{1,0:T(8,128)(2,1)S(1)} %get-tuple-element.145), channel_id=1, source_target_pairs={{0,8},{8,0},{16,24},{24,16},{1,9},{9,1},{17,25},{25,17},{2,10},{10... | collective-permute-start | bytes 811016 | tf_op jit(solution)/shard_map/ppermute | solution.py:35
  118.9 9.1 %collective-permute-start.30 = (bf16[8,4096]{1,0:T(8,128)(2,1)S(1)}, bf16[8,4096]{1,0:T(8,128)(2,1)}, u32[]{:S(2)}, u32[]{:S(2)}) collective-permute-start(bf16[8,4096]{1,0:T(8,128)(2,1)S(1)} %divide_convert_fusion), channel_id=1, source_target_pairs={{0,6},{1,7},{2,4},{3,5},{4,2},{5,3},{6,0},{7,1},{8,14},{9,15},{10,... | collective-permute-start | bytes 196616 | tf_op jit(solution)/shard_map/ppermute | solution.py:35
  135.3 17.4 %collective-permute-start.34 = (bf16[64,1024]{0,1:T(8,128)(2,1)}, bf16[64,1024]{0,1:T(8,128)(2,1)S(1)}, u32[]{:S(2)}, u32[]{:S(2)}) collective-permute-start(bf16[64,1024]{0,1:T(8,128)(2,1)} %copy.36), channel_id=1, source_target_pairs={{0,24},{8,16},{16,8},{24,0},{1,25},{9,17},{17,9},{25,1},{2,26},{10... | collective-permute-start | bytes 393224 | tf_op jit(solution)/shard_map/ppermute | solution.py:35
  148.3 22.3 %collective-permute-start.36 = (bf16[64,2816]{1,0:T(8,128)(2,1)}, bf16[64,2816]{1,0:T(8,128)(2,1)}, u32[]{:S(2)}, u32[]{:S(2)}) collective-permute-start(bf16[64,2816]{1,0:T(8,128)(2,1)} %get-tuple-element.171), channel_id=1, source_target_pairs={{0,8},{8,0},{16,24},{24,16},{1,9},{9,1},{17,25},{25,17},{2,10},{10... | collective-permute-start | bytes 1081352 | tf_op jit(solution)/shard_map/ppermute | solution.py:35
  149.7 21.0 %collective-permute-start.37 = (bf16[64,2816]{1,0:T(8,128)(2,1)}, bf16[64,2816]{1,0:T(8,128)(2,1)}, u32[]{:S(2)}, u32[]{:S(2)}) collective-permute-start(bf16[64,2816]{1,0:T(8,128)(2,1)} %get-tuple-element.172), channel_id=1, source_target_pairs={{0,16},{8,24},{16,0},{24,8},{1,17},{9,25},{17,1},{25,9},{2,18},{10... | collective-permute-start | bytes 1081352 | tf_op jit(solution)/shard_map/ppermute | solution.py:35
  150.3 20.4 %collective-permute-start.38 = (bf16[64,2816]{1,0:T(8,128)(2,1)}, bf16[64,2816]{1,0:T(8,128)(2,1)}, u32[]{:S(2)}, u32[]{:S(2)}) collective-permute-start(bf16[64,2816]{1,0:T(8,128)(2,1)} %get-tuple-element.173), channel_id=1, source_target_pairs={{0,24},{8,16},{16,8},{24,0},{1,25},{9,17},{17,9},{25,1},{2,26},{10... | collective-permute-start | bytes 1081352 | tf_op jit(solution)/shard_map/ppermute | solution.py:35
  161.2 9.5 %collective-permute-start.35 = (bf16[4,64,512]{2,1,0:T(8,128)(2,1)S(1)}, bf16[4,64,512]{2,1,0:T(8,128)(2,1)}, u32[]{:S(2)}, u32[]{:S(2)}) collective-permute-start(bf16[4,64,512]{2,1,0:T(8,128)(2,1)S(1)} %shard_map.144), channel_id=1, source_target_pairs={{0,1},{1,0},{2,3},{3,2},{4,5},{5,4},{6,7},{7,6},{8,9},{9,8},{10,11... | collective-permute-start | bytes 786440 | tf_op jit(solution)/shard_map/ppermute | solution.py:35
  171.8 17.5 %collective-permute-start.41 = (bf16[1,64,512]{2,1,0:T(8,128)(2,1)S(1)}, bf16[1,64,512]{2,1,0:T(8,128)(2,1)S(1)}, u32[]{:S(2)}, u32[]{:S(2)}) collective-permute-start(bf16[1,64,512]{2,1,0:T(8,128)(2,1)S(1)} %get-tuple-element.205), channel_id=1, source_target_pairs={{0,6},{1,7},{2,4},{3,5},{4,2},{5,3},{6,0},{7,1},{8,14},{9,15},{10,... | collective-permute-start | bytes 196616 | tf_op jit(solution)/shard_map/ppermute | solution.py:35
  174.5 14.7 %collective-permute-start.40 = (bf16[1,64,512]{2,1,0:T(8,128)(2,1)S(1)}, bf16[1,64,512]{2,1,0:T(8,128)(2,1)S(1)}, u32[]{:S(2)}, u32[]{:S(2)}) collective-permute-start(bf16[1,64,512]{2,1,0:T(8,128)(2,1)S(1)} %get-tuple-element.206), channel_id=1, source_target_pairs={{0,4},{1,5},{2,6},{3,7},{4,0},{5,1},{6,2},{7,3},{8,12},{9,13},{10,... | collective-permute-start | bytes 196616 | tf_op jit(solution)/shard_map/ppermute | solution.py:35
  174.5 14.7 %collective-permute-start.39 = (bf16[1,64,512]{2,1,0:T(8,128)(2,1)S(1)}, bf16[1,64,512]{2,1,0:T(8,128)(2,1)S(1)}, u32[]{:S(2)}, u32[]{:S(2)}) collective-permute-start(bf16[1,64,512]{2,1,0:T(8,128)(2,1)S(1)} %get-tuple-element.204), channel_id=1, source_target_pairs={{0,2},{1,3},{2,0},{3,1},{4,6},{5,7},{6,4},{7,5},{8,10},{9,11},{10,... | collective-permute-start | bytes 196616 | tf_op jit(solution)/shard_map/ppermute | solution.py:35
  (43 other events, 317.2 us)

commit v4 on v3

--- a/solution.py
+++ b/solution.py
@@ -193,21 +193,21 @@
     parts, _, depth = pieces.shape
     rows, units = gate_part.shape
     width = down_weight.shape[1]
-    chunk = units // 4
-    slots = 2
+    chunk = width // 8
+    slots = 4
 
     def body(
         order_ref, x_ref, gate_in, up_in, gate_ref, up_ref, down_ref, one_hot, extra_ref,
-        gate_out, up_out, own_out, other_out, held_ref, total_ref, sems,
+        gate_out, up_out, own_out, other_out, held_ref, sems,
     ):
         copies = [
             pltpu.make_async_copy(
-                down_ref.at[pl.ds(i * chunk, chunk)], held_ref.at[i % slots], sems.at[i % slots]
+                down_ref.at[:, pl.ds(i * chunk, chunk)], held_ref.at[i % slots], sems.at[i % slots]
             )
-            for i in range(4)
+            for i in range(8)
         ]
-        copies[0].start()
-        copies[1].start()
+        for copy in copies[:slots]:
+            copy.start()
         values = []
         for start, weight in ((gate_in, gate_ref), (up_in, up_ref)):
             total = start[...]
@@ -224,12 +224,12 @@
         hidden = dot32(one_hot[...], hidden).astype(jnp.bfloat16)
         for i, copy in enumerate(copies):
             copy.wait()
-            term = dot32(hidden[:, i * chunk : (i + 1) * chunk], held_ref[i % slots])
-            total_ref[...] = term if i == 0 else total_ref[...] + term
-            if i + slots < 4:
+            at = pl.ds(i * chunk, chunk)
+            total = dot32(hidden, held_ref[i % slots])
+            if i + slots < 8:
                 copies[i + slots].start()
-        own_out[...] = total_ref[: rows // 2].astype(jnp.bfloat16)
-        other_out[...] = total_ref[rows // 2 :].astype(jnp.bfloat16)
+            own_out[:, at] = total[: rows // 2].astype(jnp.bfloat16)
+            other_out[:, at] = total[rows // 2 :].astype(jnp.bfloat16)
 
     return kernel_call(
         body,
@@ -242,8 +242,7 @@
         ],
         13,
         [
-            pltpu.VMEM((slots, chunk, width), down_weight.dtype),
-            pltpu.VMEM((rows, width), jnp.float32),
+            pltpu.VMEM((slots, units, chunk), down_weight.dtype),
             pltpu.SemaphoreType.DMA((slots,)),
         ],
     )(
@@ -290,16 +289,23 @@
 
     def body(*refs):
         state_refs, refs = refs[:pieces], refs[pieces:]
-        first, second, inverse_ref, counts_ref, dead_ref = refs[:5]
-        outs = refs[5:]
+        sources, (inverse_ref, counts_ref, dead_ref) = refs[:2], refs[2:5]
+        outs, (index_held, sems) = refs[5:-2], refs[-2:]
+        copies = [
+            pltpu.make_async_copy(source, index_held.at[k], sems.at[k])
+            for k, source in enumerate(sources)
+        ]
+        for copy in copies:
+            copy.start()
         block = jnp.concatenate([r[...] for r in state_refs], axis=0)
         values = block.astype(jnp.float32)
         state_scale = inverse_temp / jnp.sqrt(jnp.sum(values * values, axis=1, keepdims=True) + eps)
         total = dead_ref[...]
         coeffs = []
-        for k, index_ref in enumerate((first, second)):
+        for k, copy in enumerate(copies):
+            copy.wait()
             inverse = inverse_ref[:, k * shard : (k + 1) * shard]
-            raw = dot32(block, index_ref[...], contract_last)
+            raw = dot32(block, index_held[k], contract_last)
             weights = counts_ref[:, k * shard : (k + 1) * shard] * jnp.exp(raw * state_scale * inverse)
             total = total + jnp.sum(weights, axis=1, keepdims=True)
             coeffs.append((weights * inverse).astype(jnp.bfloat16))
@@ -309,16 +315,20 @@
             outs[p][:, width:] = last[p * rows : (p + 1) * rows]
         for i in range(width // chunk):
             at = pl.ds(i * chunk, chunk)
-            pull = dot32(coeffs[0], first[:, at]) + dot32(coeffs[1], second[:, at])
+            pull = dot32(coeffs[0], index_held[0, :, at]) + dot32(coeffs[1], index_held[1, :, at])
             for p in range(pieces):
                 outs[p][:, at] = pull[p * rows : (p + 1) * rows].astype(jnp.bfloat16)
 
     return kernel_call(
         body,
-        [in_vmem] * (pieces + 5),
+        [in_vmem] * pieces + [in_hbm] * 2 + [in_vmem] * 3,
         [shape_of((rows, width + pad))] * pieces,
-        13,
-    )(*states, *index_parts, inverse_norm, counts, dead)
+        20,
+        [
+            pltpu.VMEM((2, shard, width), index_parts[0].dtype),
+            pltpu.SemaphoreType.DMA((2,)),
+        ],
+    )(*states, *[in_place(x) for x in index_parts], inverse_norm, counts, dead)
 
 
 def backward_hidden(order, own_rows, other_rows, down_weight, gate_act, up_act, to_relative, parts):
@@ -327,11 +337,11 @@
     part = width // parts
     chunk = 256 if units % 256 == 0 else units
     chunks = units // chunk
-    slots = min(chunks, 3)
+    slots = min(chunks, 5)
 
     def body(order_ref, own_ref, other_ref, down_ref, gate_ref, up_ref, one_hot, *refs):
         gate_out, up_out = refs[:2]
-        outs, (grad_ref, held_ref, sems) = refs[2:-3], refs[-3:]
+        outs, (grad_ref, turned_ref, held_ref, sems) = refs[2:-4], refs[-4:]
         spans = [pl.ds(i * chunk, chunk) for i in range(chunks)]
         copies = [
             pltpu.make_async_copy(down_ref.at[at], held_ref.at[i % slots], sems.at[i % slots])
@@ -341,13 +351,14 @@
             copy.start()
         grad = jnp.concatenate([own_ref[...], other_ref[...]], axis=0)
         grad_ref[...] = dot32(one_hot[...], grad, contract_first).astype(jnp.bfloat16)
+        turned_ref[...] = grad_ref[...].T
         for k, out in enumerate(outs):
             out[:, units:] = grad_ref[:, pl.ds(pl.multiple_of(order_ref[k] * part, part), part)]
         for i, at in enumerate(spans):
             copies[i].wait()
             if i + slots - 1 < chunks and slots > 1:
                 copies[i + slots - 1].start()
-            hidden_grad = dot32(grad_ref[...], held_ref[i % slots], contract_last)
+            hidden_grad = dot32(held_ref[i % slots], turned_ref[...]).T
             for out in outs:
                 out[:, at] = hidden_grad.astype(jnp.bfloat16)
             gate_out[:, at], up_out[:, at] = activation_grads(
@@ -360,9 +371,10 @@
         body,
         [in_smem, in_vmem, in_vmem, in_hbm, in_vmem, in_vmem, in_vmem],
         [shape_of((rows, units))] * 2 + [shape_of((rows, units + part))] * parts,
-        13,
+        16,
         [
             pltpu.VMEM((rows, width), jnp.bfloat16),
+            pltpu.VMEM((width, rows), jnp.bfloat16),
             pltpu.VMEM((slots, chunk, width), down_weight.dtype),
             pltpu.SemaphoreType.DMA((slots,)),
         ],
@@ -374,10 +386,11 @@
     rows, units = gate_grad.shape
     width = gate_weight.shape[0]
     blocks = order.shape[0]
-    depth = width // (2 * blocks)
-    slots = 3
-
-    def body(order_ref, gate_grad_ref, up_grad_ref, gate_ref, up_ref, out, held_ref, sems):
+    depth = width // blocks
+    half = blocks // 2
+    slots = 4
+
+    def body(order_ref, gate_grad_ref, up_grad_ref, gate_ref, up_ref, own_out, other_out, held_ref, sems):
         def copies_of(n):
             at = pl.ds(pl.multiple_of(order_ref[n] * depth, depth), depth)
             return [
@@ -397,13 +410,14 @@
             block = dot32(gate_grad_ref[...], held_ref[0, n % slots], contract_last) + dot32(
                 up_grad_ref[...], held_ref[1, n % slots], contract_last
             )
-            out[n] = block.astype(jnp.bfloat16)
+            out = own_out if n < half else other_out
+            out[n % half] = block.astype(jnp.bfloat16)
 
     return kernel_call(
         body,
         [in_smem, in_vmem, in_vmem, in_hbm, in_hbm],
-        shape_of((blocks, rows, depth)),
-        14,
+        [shape_of((half, rows, depth))] * 2,
+        18,
         [
             pltpu.VMEM((2, slots, depth, units), gate_weight.dtype),
             pltpu.SemaphoreType.DMA((2, slots)),
@@ -414,10 +428,16 @@
 def weight_grads(input_columns, grads, gate_acts, up_acts):
     groups = len(grads)
     rows, units = grads[0].shape[0], gate_acts[0].shape[1]
-    width = input_columns.shape[0]
+    width = input_columns[0].shape[1]
     chunk = 256 if units % 256 == 0 else units
 
-    def body(x_ref, *refs):
+    def body(*refs):
+        columns, refs, turned = refs[:groups], refs[groups:-1], refs[-1]
+
+        @pl.when(pl.program_id(0) == 0)
+        def _():
+            turned[...] = jnp.concatenate([r[...] for r in columns], axis=0).T
+
         at = pl.ds(0, units)
         if chunk < units:
             at = pl.ds(pl.multiple_of(pl.program_id(0) * chunk, chunk), chunk)
@@ -429,17 +449,47 @@
         gate_grad, up_grad = activation_grads(
             hidden_grad.astype(jnp.float32), gate.astype(jnp.float32), up.astype(jnp.float32)
         )
-        gate_out[...] = dot32(x_ref[...], gate_grad).astype(jnp.bfloat16)
-        up_out[...] = dot32(x_ref[...], up_grad).astype(jnp.bfloat16)
+        gate_out[...] = dot32(turned[...], gate_grad).astype(jnp.bfloat16)
+        up_out[...] = dot32(turned[...], up_grad).astype(jnp.bfloat16)
 
     return pl.pallas_call(
         body,
         grid=(units // chunk,),
-        in_specs=[in_vmem] * (1 + 3 * groups),
+        in_specs=[in_vmem] * (4 * groups),
         out_specs=[pl.BlockSpec((width, chunk), lambda i: (0, i))] * 2,
         out_shape=[shape_of((width, units))] * 2,
-        compiler_params=pltpu.CompilerParams(vmem_limit_bytes=12 * mib),
-    )(input_columns, *grads, *gate_acts, *up_acts)
+        scratch_shapes=[pltpu.VMEM((width, groups * rows), jnp.bfloat16)],
+        compiler_params=pltpu.CompilerParams(vmem_limit_bytes=14 * mib),
+    )(*input_columns, *grads, *gate_acts, *up_acts)
+
+
+def down_grads(grads, gate_acts, up_acts):
+    groups = len(grads)
+    rows, units = grads[0].shape[0], gate_acts[0].shape[1]
+    width = grads[0].shape[1] - units
+    chunk = 256 if units % 256 == 0 else units
+
+    def body(*refs):
+        at = pl.ds(0, units)
+        if chunk < units:
+            at = pl.ds(pl.multiple_of(pl.program_id(0) * chunk, chunk), chunk)
+        gate, up = (
+            jnp.concatenate([r[:rows, at] for r in refs[k * groups : (k + 1) * groups]], axis=0)
+            for k in (1, 2)
+        )
+        gate, up = gate.astype(jnp.float32), up.astype(jnp.float32)
+        hidden = (gate * sigmoid(gate) * up).astype(jnp.bfloat16)
+        head_grad = jnp.concatenate([r[:, units:] for r in refs[:groups]], axis=0)
+        refs[-1][...] = dot32(hidden, head_grad, contract_first).astype(jnp.bfloat16)
+
+    return pl.pallas_call(
+        body,
+        grid=(units // chunk,),
+        in_specs=[in_vmem] * (3 * groups),
+        out_specs=pl.BlockSpec((chunk, width), lambda i: (i, 0)),
+        out_shape=shape_of((units, width)),
+        compiler_params=pltpu.CompilerParams(vmem_limit_bytes=14 * mib),
+    )(*grads, *gate_acts, *up_acts)
 
 
 def shards(
@@ -513,30 +563,31 @@
 
     tables = jnp.concatenate([request_rows[:, 0, :], request_counts], axis=1)[None]
     tables = gather_core(tables)
-    top_state, gate_near, up_far, own_norm, other_index, tables = together(
+    top_state, gate_near, up_far, span_later, other_index, tables = together(
         sum_chips(branch) + residual_in.astype(jnp.float32),
         swap(gate_act, "dp", near),
         swap(up_act, "dp", far),
-        norm_of(span_later.astype(jnp.float32)),
+        span_later,
         other_index,
         tables,
     )
     row_norm = norm_of(top_state)
     unit_rows = top_state / row_norm[:, None]
 
-    states, gate_far, up_near, other_norm, span_later, tables, positive_keys = together(
+    states, last_slots, own_norm, other_norm, span_later, other_index, tables, positive_keys, asker, both = together(
         gather_chips(top_state.astype(jnp.bfloat16)),
-        swap(
-            jnp.concatenate([gate_act[:group_rows], gate_near[group_rows:]], axis=0), "dp", far
-        ),
-        swap(up_act, "dp", near),
+        swap(gate_near[group_rows:], "dp", far),
+        norm_of(span_later.astype(jnp.float32)),
         norm_of(other_index.astype(jnp.float32)),
         span_later,
+        other_index,
         tables,
         positive_keys,
+        asker,
+        both,
     )
     index_norm = jnp.concatenate([own_norm, other_norm], axis=0)
-    slots = [x[group_rows:] for x in (gate_act, gate_near, up_far, gate_far)]
+    slots = [x[group_rows:] for x in (gate_act, gate_near, up_far)] + [last_slots]
     slots = jnp.stack(slots).astype(jnp.int32)
     slots = [
         slots[
@@ -562,18 +613,21 @@
         dead = dead + shard_dead
     counts = jnp.concatenate(counts, axis=1)
     states = [states] + [swap(states, "dp", k) for k in range(1, dp_count)]
-    own_held, loaded = load(place, span_later)
-    counts, dead, loaded, *states = together(counts, dead, loaded, *states)
-    counts = counts + loaded[0, 0]
-    index_parts = [own_held, held(other_index)]
+    counts, dead, *states = together(counts, dead, *states)
+    index_parts = [span_later, other_index]
     pulls = score_kernel(
         states, index_parts, (1.0 / index_norm)[None, :], counts, dead[:, None], 128
     )
 
     sums = add_up([pulls[0]] + [swap(pulls[k], "dp", k) for k in range(1, dp_count)])
-    sums, gate_near, up_far = together(sums.astype(jnp.bfloat16), gate_near, up_far)
-    sums, gate_last, up_last, first, second = together(
-        sum_chips(sums), swap(gate_near, "dp", far), swap(up_far, "dp", near), first, second
+    sums, gate_act, up_act, first, second = together(
+        sums.astype(jnp.bfloat16), gate_act, up_act, first, second
+    )
+    sums, gate_far, up_near, *blocks = together(
+        sum_chips(sums),
+        swap(gate_act, "dp", far),
+        swap(up_act, "dp", near),
+        *input_blocks(place, fsdp_order, first, second, group_rows, dp_count),
     )
     negative_total = sums[:, width]
     positive_rows = positive_keys.astype(jnp.float32)
@@ -587,50 +641,35 @@
         inverse_temp * (pull - inner[:, None] * unit_rows) / row_norm[:, None]
     ).astype(jnp.bfloat16)
 
-    blocks = input_blocks(place, fsdp_order, first, second, group_rows, dp_count)
-    own_rows, *blocks = together(
-        gather_chips(head_grad),
-        blocks[0],
-        swap(blocks[1], "dp", 1),
-        swap(blocks[2], "dp", 2),
-        blocks[3],
-    )
-    own_rows, other_rows = together(own_rows, swap_core(own_rows))
+    head_grad, gate_near, up_far = together(head_grad, gate_near, up_far)
+    own_rows, gate_last, up_last = together(
+        gather_chips(head_grad), swap(gate_near, "dp", far), swap(up_far, "dp", near)
+    )
+    other_rows = swap_core(own_rows)
     gates = [gate_act, gate_near, gate_far, gate_last]
     ups = [up_act, up_near, up_far, up_last]
-    hidden_all = jnp.concatenate(
-        [
-            (g * sigmoid(g) * u).astype(jnp.bfloat16).T
-            for g, u in (
-                (g[:group_rows].astype(jnp.float32), u[:group_rows].astype(jnp.float32))
-                for g, u in zip(gates, ups)
-            )
-        ],
-        axis=1,
-    )
-
     own_gate_grad, own_up_grad, grads = backward_hidden(
         dp_order, own_rows, other_rows, down_weight, gate_act, up_act, to_relative, dp_count
     )
-    own_gate_grad, own_up_grad, last_block = together(
-        own_gate_grad, own_up_grad, swap(blocks[3], "dp", 3)
-    )
+    own_gate_grad, own_up_grad, *rest = together(
+        own_gate_grad,
+        own_up_grad,
+        *grads,
+        blocks[0],
+        *[swap(blocks[k], "dp", k) for k in range(1, dp_count)],
+    )
+    grads, blocks = rest[:dp_count], rest[dp_count:]
     grads = [grads[0]] + [swap(grads[k], "dp", k) for k in range(1, dp_count)]
-    other_blocks = backward_input(
-        fsdp_order[chips:], own_gate_grad, own_up_grad, gate_weight, up_weight
-    )
-    other_blocks, own_gate_grad, own_up_grad = together(other_blocks, own_gate_grad, own_up_grad)
-    own_blocks = backward_input(
-        fsdp_order[:chips], own_gate_grad, own_up_grad, gate_weight, up_weight
-    )
-    own_blocks, received, *grads = together(own_blocks, swap_core(other_blocks), *grads)
+    own_blocks, other_blocks = backward_input(
+        fsdp_order, own_gate_grad, own_up_grad, gate_weight, up_weight
+    )
+    own_blocks, other_blocks, *grads = together(own_blocks, other_blocks, *grads)
+    received = swap_core(other_blocks)
+    down_grad = down_grads(grads, gates, ups)
+    own_blocks, received, down_grad = together(own_blocks, received, down_grad)
     blocks_sum = add_up([own_blocks, received]).astype(jnp.bfloat16)
     input_grad = sum_chips(blocks_sum)[0].astype(jnp.bfloat16)
-
-    grad_columns = jnp.concatenate([g[:, units:] for g in grads], axis=0)
-    down_grad = dot32(hidden_all, grad_columns).astype(jnp.bfloat16)
-    input_columns = jnp.concatenate(blocks[:3] + [last_block], axis=0).T
-    gate_grad, up_grad = weight_grads(input_columns, grads, gates, ups)
+    gate_grad, up_grad = weight_grads(blocks, grads, gates, ups)
     return (query_loss, input_grad, gate_grad, up_grad, down_grad)
 
 

time: 191 us -> 167 us (0.87)
  local copies, waits for them, and re-layouts: 16.5 us -> 4.88 us
  other arithmetic: 24 us -> 14 us
  waiting for transfers between devices: 25.6 us -> 34.6 us
  Pallas kernels: 67.6 us -> 61.1 us
  matrix products: 4.38 us -> 1.39 us
    ppermute x42 -> x43, waiting for transfers between devices: 25.6 us -> 34.6 us  [swap(): return lax.ppermute(x, axis, pairs)]
    unnamed x50 -> x16, local copies, waits for them, and re-layouts: 6.34 us -> 2 us
    pallas_call x1, Pallas kernels: 11.4 us -> 7.46 us  [backward_hidden(): kernel_call(body, [in_smem, in_vmem, in_vmem, in_hbm, in_vmem, in_vmem, i...]
    transpose x5 -> x0, other arithmetic: 3.72 us -> none  [the longest x4 3.37 us: shards(): (g * sigmoid(g) * u).astype(jnp.bfloat16)]
    slice x7 -> x0, local copies, waits for them, and re-layouts: 3.35 us -> none  [the longest x4 2.75 us: shards(): grad_columns = jnp.concatenate([g[:, units:] for g in grads], axis=0)]
    dot_general x1 -> x0, matrix products: 2.99 us -> none  [dot32(): lax.dot_general(left, right, dims, preferred_element_type=jnp.float32)]
    pallas_call x2 -> x1, Pallas kernels: 12.7 us -> 9.98 us  [load(): kernel_call(body, [in_smem] + [in_hbm] * count, [pltpu.VMEM(a.shape, a.dt...]
    ppermute x42 -> x43, starting transfers between devices: 49.3 us -> 48.7 us  [swap(): return lax.ppermute(x, axis, pairs)]
  transfers between devices with their start and end apart: 42 -> 43, of which waited for: 13 -> 15; matrix products, arithmetic and copies ran while one was open for 15% -> 7% of each run, Pallas kernels for 32% -> 33%
where the time goes in v4:
time: 167 us
  Pallas kernels  61.1 us (37%)
  starting transfers between devices  48.7 us (29%)
  waiting for transfers between devices  34.6 us (21%)
  other arithmetic  14 us (8%)
  local copies, waits for them, and re-layouts  4.88 us (3%)
  between operations  2.46 us (1%)
    ppermute x43, starting transfers between devices, swap(): return lax.ppermute(x, axis, pairs)  48.7 us
    ppermute x43, waiting for transfers between devices, swap(): return lax.ppermute(x, axis, pairs)  34.6 us
    pallas_call x1, Pallas kernels, backward_input(): kernel_call(body, [in_smem, in_vmem, in_vmem, in_hbm, in_hbm], [shape_of(...  12.7 us
    pallas_call x1, Pallas kernels, load(): kernel_call(body, [in_smem] + [in_hbm] * count, [pltpu.VMEM(a.shape, a.dt...  9.98 us
    pallas_call x1, Pallas kernels, forward_rest(): kernel_call(body, [in_smem] + [in_vmem] * 5 + [in_hbm, in_vmem, in_vmem],...  9.56 us
    pallas_call x1, Pallas kernels, backward_hidden(): kernel_call(body, [in_smem, in_vmem, in_vmem, in_hbm, in_vmem, in_vmem, i...  7.46 us
    pallas_call x1, Pallas kernels, score_kernel(): kernel_call(body, [in_vmem] * pieces + [in_hbm] * 2 + [in_vmem] * 3, [sha...  6.69 us
    pallas_call x1, Pallas kernels, weight_grads(): pl.pallas_call(body, grid=(units // chunk,), in_specs=[in_vmem] * (4 * gr...  6.25 us
  transfers between devices with their start and end apart: 43, of which 15 were waited for; matrix products, arithmetic and copies ran while one was open for 7% of the time, Pallas kernels for 33%

profile of v4, /device:TPU:0, one launch (start us, length us, event | category | flops | bytes accessed | tf_op | source)
XLA Modules:
  0.0 167.1 jit_solution(11652474529395189684)
XLA Ops:
  2.3 5.0 %collective-permute-start.2 = (bf16[1,72,512]{2,1,0:T(8,128)(2,1)S(1)}, bf16[1,72,512]{2,1,0:T(8,128)(2,1)S(1)}, u32[]{:S(2)}, u32[]{:S(2)}) collective-permute-start(bf16[1,72,512]{2,1,0:T(8,128)(2,1)S(1)} %maximum_bitcast_fusion), channel_id=1, source_target_pairs={{0,6},{1,7},{2,4},{3,5},{4,2},{5,3},{6,0},{7,1},{8,14},{9,15},{10,... | collective-permute-start | bytes 221192 | tf_op jit(solution)/shard_map/ppermute | solution.py:35
  8.2 10.0 %shard_map.137 = (bf16[4096,1792]{1,0:T(8,128)(2,1)S(1)}, bf16[4096,1792]{1,0:T(8,128)(2,1)S(1)}, f32[8,128]{1,0:T(8,128)S(1)}) custom-call(s32[2]{0:T(128)S(1)} %get-tuple-element.110.place_ref, bf16[4096,1792]{1,0:T(8,128)(2,1)} %gate_ref.1, bf16[4096,1792]{1,0:T(8,128)(2,1)} %up_ref.1), custom_call_target="tpu_custom_call" | custom-call | tf_op jit(solution)/shard_map/pallas_call | solution.py:160
  19.5 3.2 %shard_map.138 = (f32[64,1792]{1,0:T(8,128)S(1)}, f32[64,1792]{1,0:T(8,128)S(1)}) custom-call(s32[8]{0:T(128)S(1)} %fusion.40.order_ref, bf16[4,72,512]{2,1,0:T(8,128)(2,1)S(1)} %maximum_add_fusion.x_ref.first_ref, bf16[4096,1792]{1,0:T(8,128)(2,1)S(1)} %get-tuple-element.112.gate_ref, bf16[4096,1792]{1,0:T(8,128)(2,1)S(1)} %get-tuple-element.113.up_ref), custom_call_target="tpu_custom_call" | custom-call | tf_op jit(solution)/shard_map/pallas_call | solution.py:182
  23.3 9.6 %shard_map.139 = (bf16[72,1792]{1,0:T(8,128)(2,1)S(1)}, bf16[72,1792]{1,0:T(8,128)(2,1)S(1)}, bf16[32,4096]{1,0:T(8,128)(2,1)S(1)}, bf16[32,4096]{1,0:T(8,128)(2,1)S(1)}) custom-call(s32[8]{0:T(128)S(1)} %fusion.40.order_ref, bf16[4,72,512]{2,1,0:T(8,128)(2,1)S(1)} %collective-permute-done.3.x_ref.second_ref, f32[64,1792]{1,0:T(8,128)S(1)} %get-tuple-element.117.gate_in, ...), custom_call_target="tpu_custom_call" | custom-call | tf_op jit(solution)/shard_map/pallas_call | solution.py:234
  36.1 2.0 %copy-done.1 = bf16[512,4096]{1,0:T(8,128)(2,1)} copy-done((bf16[512,4096]{1,0:T(8,128)(2,1)}, bf16[512,4096]{1,0:T(8,128)(2,1)S(1)}, u32[]{:S(2)}) %copy-start.1) | copy-done | bytes 4194328
  39.7 2.4 %collective-permute-start.8 = (bf16[8,4096]{1,0:T(8,128)(2,1)S(1)}, bf16[8,4096]{1,0:T(8,128)(2,1)S(1)}, u32[]{:S(2)}, u32[]{:S(2)}) collective-permute-start(bf16[8,4096]{1,0:T(8,128)(2,1)S(1)} %get-tuple-element.232), channel_id=1, source_target_pairs={{0,6},{1,7},{2,4},{3,5},{4,2},{5,3},{6,0},{7,1},{8,14},{9,15},{10,... | collective-permute-start | bytes 196616 | tf_op jit(solution)/shard_map/ppermute | solution.py:35
  42.9 3.6 %collective-permute-done.8 = bf16[8,4096]{1,0:T(8,128)(2,1)S(1)} collective-permute-done((bf16[8,4096]{1,0:T(8,128)(2,1)S(1)}, bf16[8,4096]{1,0:T(8,128)(2,1)S(1)}, u32[]{:S(2)}, u32[]{:S(2)}) %collective-permute-start.8) | collective-permute-done | bytes 65568 | tf_op jit(solution)/shard_map/ppermute | solution.py:35
  46.5 2.8 %collective-permute-done.7 = bf16[8,4096]{1,0:T(8,128)(2,1)S(1)} collective-permute-done((bf16[8,4096]{1,0:T(8,128)(2,1)S(1)}, bf16[8,4096]{1,0:T(8,128)(2,1)S(1)}, u32[]{:S(2)}, u32[]{:S(2)}) %collective-permute-start.7) | collective-permute-done | bytes 65568 | tf_op jit(solution)/shard_map/ppermute | solution.py:35
  49.5 2.7 %collective-permute-start.14 = (bf16[8,4096]{1,0:T(8,128)(2,1)S(1)}, bf16[8,4096]{1,0:T(8,128)(2,1)S(1)}, u32[]{:S(2)}, u32[]{:S(2)}) collective-permute-start(bf16[8,4096]{1,0:T(8,128)(2,1)S(1)} %get-tuple-element.237), channel_id=1, source_target_pairs={{0,6},{1,7},{2,4},{3,5},{4,2},{5,3},{6,0},{7,1},{8,14},{9,15},{10,... | collective-permute-start | bytes 196616 | tf_op jit(solution)/shard_map/ppermute | solution.py:35
  52.2 1.7 %collective-permute-start.12 = (bf16[8,4096]{1,0:T(8,128)(2,1)S(1)}, bf16[8,4096]{1,0:T(8,128)(2,1)S(1)}, u32[]{:S(2)}, u32[]{:S(2)}) collective-permute-start(bf16[8,4096]{1,0:T(8,128)(2,1)S(1)} %get-tuple-element.237), channel_id=1, source_target_pairs={{0,2},{1,3},{2,0},{3,1},{4,6},{5,7},{6,4},{7,5},{8,10},{9,11},{10,... | collective-permute-start | bytes 196616 | tf_op jit(solution)/shard_map/ppermute | solution.py:35
  54.0 3.1 %multiply_reduce_fusion.1 = f32[512]{0:T(512)S(1)} fusion(bf16[512,4096]{1,0:T(8,128)(2,1)} %refs_4_), kind=kLoop, calls=%fused_computation.2 | loop fusion | flops 6290944 | bytes 4196352 | tf_op jit(solution)/shard_map/reduce_sum | solution.py:30
  58.6 3.3 %collective-permute-done.15 = bf16[8,1792]{1,0:T(8,128)(2,1)S(1)} collective-permute-done((bf16[8,1792]{1,0:T(8,128)(2,1)S(1)}, bf16[8,1792]{1,0:T(8,128)(2,1)S(1)}, u32[]{:S(2)}, u32[]{:S(2)}) %collective-permute-start.15) | collective-permute-done | bytes 28704 | tf_op jit(solution)/shard_map/ppermute | solution.py:35
  73.5 2.0 %collective-permute-done.17.refs_2_ = bf16[32,4096]{1,0:T(8,128)(2,1)S(1)} collective-permute-done((bf16[32,4096]{1,0:T(8,128)(2,1)S(1)}, bf16[32,4096]{1,0:T(8,128)(2,1)S(1)}, u32[]{:S(2)}, u32[]{:S(2)}) %collective-permute-start.17) | collective-permute-done | bytes 262176 | tf_op jit(solution)/shard_map/ppermute | solution.py:35
  75.6 6.7 %shard_map.140 = (bf16[32,4224]{1,0:T(8,128)(2,1)S(1)}, bf16[32,4224]{1,0:T(8,128)(2,1)S(1)}, bf16[32,4224]{1,0:T(8,128)(2,1)S(1)}, bf16[32,4224]{1,0:T(8,128)(2,1)S(1)}) custom-call(bf16[32,4096]{1,0:T(8,128)(2,1)S(1)} %pad_maximum_fusion.1.refs_0_, bf16[32,4096]{1,0:T(8,128)(2,1)S(1)} %collective-permute-done.16.refs_1_, ...), custom_call_target="tpu_custom_call" | custom-call | tf_op jit(solution)/shard_map/pallas_call | solution.py:322
  86.1 5.7 %collective-permute-done.19 = bf16[32,4224]{1,0:T(8,128)(2,1)S(1)} collective-permute-done((bf16[32,4224]{1,0:T(8,128)(2,1)S(1)}, bf16[32,4224]{1,0:T(8,128)(2,1)S(1)}, u32[]{:S(2)}, u32[]{:S(2)}) %collective-permute-start.19) | collective-permute-done | bytes 270368 | tf_op jit(solution)/shard_map/ppermute | solution.py:35
  91.8 5.3 %collective-permute-done.20 = bf16[32,4224]{1,0:T(8,128)(2,1)S(1)} collective-permute-done((bf16[32,4224]{1,0:T(8,128)(2,1)S(1)}, bf16[32,4224]{1,0:T(8,128)(2,1)S(1)}, u32[]{:S(2)}, u32[]{:S(2)}) %collective-permute-start.20) | collective-permute-done | bytes 270368 | tf_op jit(solution)/shard_map/ppermute | solution.py:35
  98.8 2.1 %collective-permute-start.23 = (bf16[8,4224]{1,0:T(8,128)(2,1)S(1)}, bf16[8,4224]{1,0:T(8,128)(2,1)S(1)}, u32[]{:S(2)}, u32[]{:S(2)}) collective-permute-start(bf16[8,4224]{1,0:T(8,128)(2,1)S(1)} %get-tuple-element.227), channel_id=1, source_target_pairs={{0,4},{1,5},{2,6},{3,7},{4,0},{5,1},{6,2},{7,3},{8,12},{9,13},{10,... | collective-permute-start | bytes 202760 | tf_op jit(solution)/shard_map/ppermute | solution.py:35
  105.3 2.0 %collective-permute-done.25.refs_6_.refs_10_ = bf16[72,1792]{1,0:T(8,128)(2,1)S(1)} collective-permute-done((bf16[72,1792]{1,0:T(8,128)(2,1)S(1)}, bf16[72,1792]{1,0:T(8,128)(2,1)S(1)}, u32[]{:S(2)}, u32[]{:S(2)}) %collective-permute-start.25) | collective-permute-done | bytes 258080 | tf_op jit(solution)/shard_map/ppermute | solution.py:35
  112.6 1.7 %collective-permute-start.27 = (bf16[8,4096]{1,0:T(8,128)(2,1)S(1)}, bf16[8,4096]{1,0:T(8,128)(2,1)S(1)}, u32[]{:S(2)}, u32[]{:S(2)}) collective-permute-start(bf16[8,4096]{1,0:T(8,128)(2,1)S(1)} %divide_convert_fusion), channel_id=1, source_target_pairs={{0,2},{1,3},{2,0},{3,1},{4,6},{5,7},{6,4},{7,5},{8,10},{9,11},{10,... | collective-permute-start | bytes 196616 | tf_op jit(solution)/shard_map/ppermute | solution.py:35
  117.5 3.1 %collective-permute-done.30.refs_7_.refs_11_ = bf16[72,1792]{1,0:T(8,128)(2,1)S(1)} collective-permute-done((bf16[72,1792]{1,0:T(8,128)(2,1)S(1)}, bf16[72,1792]{1,0:T(8,128)(2,1)S(1)}, u32[]{:S(2)}, u32[]{:S(2)}) %collective-permute-start.30) | collective-permute-done | bytes 258080 | tf_op jit(solution)/shard_map/ppermute | solution.py:35
  125.9 7.5 %shard_map.142 = (bf16[64,1792]{1,0:T(8,128)(2,1)S(1)}, bf16[64,1792]{1,0:T(8,128)(2,1)S(1)}, bf16[64,2816]{1,0:T(8,128)(2,1)S(1)}, bf16[64,2816]{1,0:T(8,128)(2...) custom-call(s32[4]{0:T(128)S(1)} %iota_xor_fusion.order_ref, ...), custom_call_target="tpu_custom_call" | custom-call | tf_op jit(solution)/shard_map/pallas_call | solution.py:370
  136.9 12.7 %shard_map.143 = (bf16[4,64,512]{2,1,0:T(8,128)(2,1)S(1)}, bf16[4,64,512]{2,1,0:T(8,128)(2,1)S(1)}) custom-call(s32[8]{0:T(128)S(1)} %fusion.40.order_ref, bf16[64,1792]{1,0:T(8,128)(2,1)S(1)} %get-tuple-element.186.gate_grad_ref, bf16[64,1792]{1,0:T(8,128)(2,1)S(1)} %get-tuple-element.187.up_grad_ref, bf16[4096,1792]{1,0:T(8,128)(2,1)} %gate_ref.1, ...), custom_call_target="tpu_custom_call" | custom-call | tf_op jit(solution)/shard_map/pallas_call | solution.py:416
  151.3 4.7 %shard_map.144 = bf16[1792,1024]{1,0:T(8,128)(2,1)} custom-call(bf16[64,2816]{1,0:T(8,128)(2,1)S(1)} %get-tuple-element.196.refs_0_.refs_4_, bf16[64,2816]{1,0:T(8,128)(2,1)S(1)} %collective-permute-done.36.refs_1_.refs_5_, bf16[64,2816]{1,0:T(8,128)(2,1)S(1)} %collective-permute-done.37.refs_2_.refs_6_, ...), custom_call_target="tpu_custom_call" | custom-call | tf_op jit(solution)/shard_map/pallas_call | solution.py:485
  160.2 6.2 %shard_map.145 = (bf16[1024,1792]{1,0:T(8,128)(2,1)}, bf16[1024,1792]{1,0:T(8,128)(2,1)}) custom-call(bf16[64,1024]{1,0:T(8,128)(2,1)S(1)} %get-tuple-element.206.refs_0_, bf16[64,1024]{1,0:T(8,128)(2,1)S(1)} %collective-permute-done.33.refs_1_, bf16[64,1024]{1,0:T(8,128)(2,1)S(1)} %collective-permute-done.34.refs_2_, ...), custom_call_target="tpu_custom_call" | custom-call | tf_op jit(solution)/shard_map/pallas_call | solution.py:455
  (161 shorter events, 55.7 us)
Async XLA Ops:
  2.3 16.5 %collective-permute-start.2 = (bf16[1,72,512]{2,1,0:T(8,128)(2,1)S(1)}, bf16[1,72,512]{2,1,0:T(8,128)(2,1)S(1)}, u32[]{:S(2)}, u32[]{:S(2)}) collective-permute-start(bf16[1,72,512]{2,1,0:T(8,128)(2,1)S(1)} %maximum_bitcast_fusion), channel_id=1, source_target_pairs={{0,6},{1,7},{2,4},{3,5},{4,2},{5,3},{6,0},{7,1},{8,14},{9,15},{10,... | collective-permute-start | bytes 221192 | tf_op jit(solution)/shard_map/ppermute | solution.py:35
  7.3 11.4 %collective-permute-start.1 = (bf16[1,72,512]{2,1,0:T(8,128)(2,1)S(1)}, bf16[1,72,512]{2,1,0:T(8,128)(2,1)S(1)}, u32[]{:S(2)}, u32[]{:S(2)}) collective-permute-start(bf16[1,72,512]{2,1,0:T(8,128)(2,1)S(1)} %maximum_bitcast_fusion), channel_id=1, source_target_pairs={{0,4},{1,5},{2,6},{3,7},{4,0},{5,1},{6,2},{7,3},{8,12},{9,13},{10,... | collective-permute-start | bytes 221192 | tf_op jit(solution)/shard_map/ppermute | solution.py:35
  7.3 11.4 %collective-permute-start = (bf16[1,72,512]{2,1,0:T(8,128)(2,1)S(1)}, bf16[1,72,512]{2,1,0:T(8,128)(2,1)S(1)}, u32[]{:S(2)}, u32[]{:S(2)}) collective-permute-start(bf16[1,72,512]{2,1,0:T(8,128)(2,1)S(1)} %maximum_bitcast_fusion), channel_id=1, source_target_pairs={{0,2},{1,3},{2,0},{3,1},{4,6},{5,7},{6,4},{7,5},{8,10},{9,11},{10,... | collective-permute-start | bytes 221192 | tf_op jit(solution)/shard_map/ppermute | solution.py:35
  22.7 13.4 %collective-permute-start.4 = (bf16[512,4096]{1,0:T(8,128)(2,1)S(1)}, bf16[512,4096]{1,0:T(8,128)(2,1)S(1)}, u32[]{:S(2)}, u32[]{:S(2)}) collective-permute-start(bf16[512,4096]{1,0:T(8,128)(2,1)S(1)} %copy-done), channel_id=1, source_target_pairs={{0,1},{1,0},{2,3},{3,2},{4,5},{5,4},{6,7},{7,6},{8,9},{9,8},{10,11... | collective-permute-start | bytes 12582920 | tf_op jit(solution)/shard_map/ppermute | solution.py:35
  32.9 16.5 %collective-permute-start.10 = (bf16[72,1792]{1,0:T(8,128)(2,1)S(1)}, bf16[72,1792]{1,0:T(8,128)(2,1)S(1)}, u32[]{:S(2)}, u32[]{:S(2)}) collective-permute-start(bf16[72,1792]{1,0:T(8,128)(2,1)S(1)} %get-tuple-element.163.up_ref.refs_8_.refs_12_), channel_id=1, source_target_pairs={{0,16},{8,24},{16,0},{24,8},{1,17},{9,25},{17,1},{25,9},{2,18},{10... | collective-permute-start | bytes 774152 | tf_op jit(solution)/shard_map/ppermute | solution.py:35
  34.6 14.7 %collective-permute-start.9 = (bf16[72,1792]{1,0:T(8,128)(2,1)S(1)}, bf16[72,1792]{1,0:T(8,128)(2,1)S(1)}, u32[]{:S(2)}, u32[]{:S(2)}) collective-permute-start(bf16[72,1792]{1,0:T(8,128)(2,1)S(1)} %get-tuple-element.162.gate_ref.refs_4_.refs_8_), channel_id=1, source_target_pairs={{0,8},{8,0},{16,24},{24,16},{1,9},{9,1},{17,25},{25,17},{2,10},{10... | collective-permute-start | bytes 774152 | tf_op jit(solution)/shard_map/ppermute | solution.py:35
  39.7 6.8 %collective-permute-start.8 = (bf16[8,4096]{1,0:T(8,128)(2,1)S(1)}, bf16[8,4096]{1,0:T(8,128)(2,1)S(1)}, u32[]{:S(2)}, u32[]{:S(2)}) collective-permute-start(bf16[8,4096]{1,0:T(8,128)(2,1)S(1)} %get-tuple-element.232), channel_id=1, source_target_pairs={{0,6},{1,7},{2,4},{3,5},{4,2},{5,3},{6,0},{7,1},{8,14},{9,15},{10,... | collective-permute-start | bytes 196616 | tf_op jit(solution)/shard_map/ppermute | solution.py:35
  42.1 7.2 %collective-permute-start.7 = (bf16[8,4096]{1,0:T(8,128)(2,1)S(1)}, bf16[8,4096]{1,0:T(8,128)(2,1)S(1)}, u32[]{:S(2)}, u32[]{:S(2)}) collective-permute-start(bf16[8,4096]{1,0:T(8,128)(2,1)S(1)} %get-tuple-element.233), channel_id=1, source_target_pairs={{0,4},{1,5},{2,6},{3,7},{4,0},{5,1},{6,2},{7,3},{8,12},{9,13},{10,... | collective-permute-start | bytes 196616 | tf_op jit(solution)/shard_map/ppermute | solution.py:35
  49.5 9.1 %collective-permute-start.14 = (bf16[8,4096]{1,0:T(8,128)(2,1)S(1)}, bf16[8,4096]{1,0:T(8,128)(2,1)S(1)}, u32[]{:S(2)}, u32[]{:S(2)}) collective-permute-start(bf16[8,4096]{1,0:T(8,128)(2,1)S(1)} %get-tuple-element.237), channel_id=1, source_target_pairs={{0,6},{1,7},{2,4},{3,5},{4,2},{5,3},{6,0},{7,1},{8,14},{9,15},{10,... | collective-permute-start | bytes 196616 | tf_op jit(solution)/shard_map/ppermute | solution.py:35
  63.4 10.1 %collective-permute-start.18 = (bf16[32,4096]{1,0:T(8,128)(2,1)S(1)}, bf16[32,4096]{1,0:T(8,128)(2,1)S(1)}, u32[]{:S(2)}, u32[]{:S(2)}) collective-permute-start(bf16[32,4096]{1,0:T(8,128)(2,1)S(1)} %pad_maximum_fusion.1.refs_0_), channel_id=1, source_target_pairs={{0,24},{8,16},{16,8},{24,0},{1,25},{9,17},{17,9},{25,1},{2,26},{10... | collective-permute-start | bytes 786440 | tf_op jit(solution)/shard_map/ppermute | solution.py:35
  64.0 11.6 %collective-permute-start.17 = (bf16[32,4096]{1,0:T(8,128)(2,1)S(1)}, bf16[32,4096]{1,0:T(8,128)(2,1)S(1)}, u32[]{:S(2)}, u32[]{:S(2)}) collective-permute-start(bf16[32,4096]{1,0:T(8,128)(2,1)S(1)} %pad_maximum_fusion.1.refs_0_), channel_id=1, source_target_pairs={{0,16},{8,24},{16,0},{24,8},{1,17},{9,25},{17,1},{25,9},{2,18},{10... | collective-permute-start | bytes 786440 | tf_op jit(solution)/shard_map/ppermute | solution.py:35
  65.5 10.0 %collective-permute-start.16 = (bf16[32,4096]{1,0:T(8,128)(2,1)S(1)}, bf16[32,4096]{1,0:T(8,128)(2,1)S(1)}, u32[]{:S(2)}, u32[]{:S(2)}) collective-permute-start(bf16[32,4096]{1,0:T(8,128)(2,1)S(1)} %pad_maximum_fusion.1.refs_0_), channel_id=1, source_target_pairs={{0,8},{8,0},{16,24},{24,16},{1,9},{9,1},{17,25},{25,17},{2,10},{10... | collective-permute-start | bytes 786440 | tf_op jit(solution)/shard_map/ppermute | solution.py:35
  82.3 9.5 %collective-permute-start.19 = (bf16[32,4224]{1,0:T(8,128)(2,1)S(1)}, bf16[32,4224]{1,0:T(8,128)(2,1)S(1)}, u32[]{:S(2)}, u32[]{:S(2)}) collective-permute-start(bf16[32,4224]{1,0:T(8,128)(2,1)S(1)} %get-tuple-element.158), channel_id=1, source_target_pairs={{0,8},{8,0},{16,24},{24,16},{1,9},{9,1},{17,25},{25,17},{2,10},{10... | collective-permute-start | bytes 811016 | tf_op jit(solution)/shard_map/ppermute | solution.py:35
  83.6 13.5 %collective-permute-start.20 = (bf16[32,4224]{1,0:T(8,128)(2,1)S(1)}, bf16[32,4224]{1,0:T(8,128)(2,1)S(1)}, u32[]{:S(2)}, u32[]{:S(2)}) collective-permute-start(bf16[32,4224]{1,0:T(8,128)(2,1)S(1)} %get-tuple-element.159), channel_id=1, source_target_pairs={{0,16},{8,24},{16,0},{24,8},{1,17},{9,25},{17,1},{25,9},{2,18},{10... | collective-permute-start | bytes 811016 | tf_op jit(solution)/shard_map/ppermute | solution.py:35
  84.2 12.9 %collective-permute-start.21 = (bf16[32,4224]{1,0:T(8,128)(2,1)S(1)}, bf16[32,4224]{1,0:T(8,128)(2,1)S(1)}, u32[]{:S(2)}, u32[]{:S(2)}) collective-permute-start(bf16[32,4224]{1,0:T(8,128)(2,1)S(1)} %get-tuple-element.160), channel_id=1, source_target_pairs={{0,24},{8,16},{16,8},{24,0},{1,25},{9,17},{17,9},{25,1},{2,26},{10... | collective-permute-start | bytes 811016 | tf_op jit(solution)/shard_map/ppermute | solution.py:35
  122.4 11.0 %collective-permute-start.33 = (bf16[64,1024]{1,0:T(8,128)(2,1)S(1)}, bf16[64,1024]{1,0:T(8,128)(2,1)S(1)}, u32[]{:S(2)}, u32[]{:S(2)}) collective-permute-start(bf16[64,1024]{1,0:T(8,128)(2,1)S(1)} %get-tuple-element.183), channel_id=1, source_target_pairs={{0,8},{8,0},{16,24},{24,16},{1,9},{9,1},{17,25},{25,17},{2,10},{10... | collective-permute-start | bytes 393224 | tf_op jit(solution)/shard_map/ppermute | solution.py:35
  122.8 10.5 %collective-permute-start.34 = (bf16[64,1024]{1,0:T(8,128)(2,1)S(1)}, bf16[64,1024]{1,0:T(8,128)(2,1)S(1)}, u32[]{:S(2)}, u32[]{:S(2)}) collective-permute-start(bf16[64,1024]{1,0:T(8,128)(2,1)S(1)} %get-tuple-element.184), channel_id=1, source_target_pairs={{0,16},{8,24},{16,0},{24,8},{1,17},{9,25},{17,1},{25,9},{2,18},{10... | collective-permute-start | bytes 393224 | tf_op jit(solution)/shard_map/ppermute | solution.py:35
  124.4 9.0 %collective-permute-start.35 = (bf16[64,1024]{1,0:T(8,128)(2,1)S(1)}, bf16[64,1024]{1,0:T(8,128)(2,1)S(1)}, u32[]{:S(2)}, u32[]{:S(2)}) collective-permute-start(bf16[64,1024]{1,0:T(8,128)(2,1)S(1)} %get-tuple-element.185), channel_id=1, source_target_pairs={{0,24},{8,16},{16,8},{24,0},{1,25},{9,17},{17,9},{25,1},{2,26},{10... | collective-permute-start | bytes 393224 | tf_op jit(solution)/shard_map/ppermute | solution.py:35
  133.4 16.2 %collective-permute-start.36 = (bf16[64,2816]{1,0:T(8,128)(2,1)S(1)}, bf16[64,2816]{1,0:T(8,128)(2,1)S(1)}, u32[]{:S(2)}, u32[]{:S(2)}) collective-permute-start(bf16[64,2816]{1,0:T(8,128)(2,1)S(1)} %get-tuple-element.191), channel_id=1, source_target_pairs={{0,8},{8,0},{16,24},{24,16},{1,9},{9,1},{17,25},{25,17},{2,10},{10... | collective-permute-start | bytes 1081352 | tf_op jit(solution)/shard_map/ppermute | solution.py:35
  133.9 17.4 %collective-permute-start.37 = (bf16[64,2816]{1,0:T(8,128)(2,1)S(1)}, bf16[64,2816]{1,0:T(8,128)(2,1)S(1)}, u32[]{:S(2)}, u32[]{:S(2)}) collective-permute-start(bf16[64,2816]{1,0:T(8,128)(2,1)S(1)} %get-tuple-element.192), channel_id=1, source_target_pairs={{0,16},{8,24},{16,0},{24,8},{1,17},{9,25},{17,1},{25,9},{2,18},{10... | collective-permute-start | bytes 1081352 | tf_op jit(solution)/shard_map/ppermute | solution.py:35
  135.4 15.9 %collective-permute-start.38 = (bf16[64,2816]{1,0:T(8,128)(2,1)S(1)}, bf16[64,2816]{1,0:T(8,128)(2,1)S(1)}, u32[]{:S(2)}, u32[]{:S(2)}) collective-permute-start(bf16[64,2816]{1,0:T(8,128)(2,1)S(1)} %get-tuple-element.193), channel_id=1, source_target_pairs={{0,24},{8,16},{16,8},{24,0},{1,25},{9,17},{17,9},{25,1},{2,26},{10... | collective-permute-start | bytes 1081352 | tf_op jit(solution)/shard_map/ppermute | solution.py:35
  156.1 10.3 %collective-permute-start.40 = (bf16[1,64,512]{2,1,0:T(8,128)(2,1)S(1)}, bf16[1,64,512]{2,1,0:T(8,128)(2,1)S(1)}, u32[]{:S(2)}, u32[]{:S(2)}) collective-permute-start(bf16[1,64,512]{2,1,0:T(8,128)(2,1)S(1)} %get-tuple-element.228), channel_id=1, source_target_pairs={{0,2},{1,3},{2,0},{3,1},{4,6},{5,7},{6,4},{7,5},{8,10},{9,11},{10,... | collective-permute-start | bytes 196616 | tf_op jit(solution)/shard_map/ppermute | solution.py:35
  156.5 10.0 %collective-permute-start.42 = (bf16[1,64,512]{2,1,0:T(8,128)(2,1)S(1)}, bf16[1,64,512]{2,1,0:T(8,128)(2,1)S(1)}, u32[]{:S(2)}, u32[]{:S(2)}) collective-permute-start(bf16[1,64,512]{2,1,0:T(8,128)(2,1)S(1)} %get-tuple-element.229), channel_id=1, source_target_pairs={{0,6},{1,7},{2,4},{3,5},{4,2},{5,3},{6,0},{7,1},{8,14},{9,15},{10,... | collective-permute-start | bytes 196616 | tf_op jit(solution)/shard_map/ppermute | solution.py:35
  158.0 8.5 %collective-permute-start.41 = (bf16[1,64,512]{2,1,0:T(8,128)(2,1)S(1)}, bf16[1,64,512]{2,1,0:T(8,128)(2,1)S(1)}, u32[]{:S(2)}, u32[]{:S(2)}) collective-permute-start(bf16[1,64,512]{2,1,0:T(8,128)(2,1)S(1)} %get-tuple-element.230), channel_id=1, source_target_pairs={{0,4},{1,5},{2,6},{3,7},{4,0},{5,1},{6,2},{7,3},{8,12},{9,13},{10,... | collective-permute-start | bytes 196616 | tf_op jit(solution)/shard_map/ppermute | solution.py:35
  (27 other events, 234.7 us)

commit v5 on v4

--- a/solution.py
+++ b/solution.py
@@ -143,48 +143,58 @@
     return lax.optimization_barrier(arrays)
 
 
-def load(place, *arrays):
-    count = len(arrays)
-
-    def body(place_ref, *refs):
-        token, sems = refs[-2:]
-        copies = [
-            pltpu.make_async_copy(refs[i], refs[count + i], sems.at[i]) for i in range(count)
-        ]
-        for copy in copies:
+def row_copies(order_ref, wanted, sources, held_ref, sems):
+    depth = held_ref.shape[2]
+    groups = []
+    for n, j in enumerate(wanted):
+        at = pl.ds(pl.multiple_of(order_ref[j] * depth, depth), depth)
+        groups.append(
+            [
+                pltpu.make_async_copy(source.at[at], held_ref.at[k, n], sems.at[k, n])
+                for k, source in enumerate(sources)
+            ]
+        )
+    return groups
+
+
+def in_turn(groups, ahead):
+    for group in groups[:ahead]:
+        for copy in group:
             copy.start()
-        token[...] = jnp.zeros_like(token)
-        for copy in copies:
+    for n, group in enumerate(groups):
+        for copy in group:
             copy.wait()
-
-    outs = kernel_call(
-        body,
-        [in_smem] + [in_hbm] * count,
-        [pltpu.VMEM(a.shape, a.dtype) for a in arrays] + [shape_of((8, 128), jnp.float32)],
-        2,
-        [pltpu.SemaphoreType.DMA((count,))],
-    )(place, *[in_place(x) for x in arrays])
-    return [held(x) for x in outs[:count]] + [outs[count]]
-
-
-def forward_first(order, pieces, rows, gate_weight, up_weight):
-    parts, _, depth = pieces.shape
-    units = gate_weight.shape[1]
-
-    def body(order_ref, x_ref, gate_ref, up_ref, gate_out, up_out):
-        for out, weight in ((gate_out, gate_ref), (up_out, up_ref)):
-            total = jnp.zeros((rows, units), jnp.float32)
-            for i in range(parts):
-                at = pl.ds(pl.multiple_of(order_ref[i] * depth, depth), depth)
-                total = total + dot32(x_ref[i, :rows], weight[at, :])
-            out[...] = total
+        for copy in groups[n + ahead] if n + ahead < len(groups) else []:
+            copy.start()
+        yield n
+
+
+def forward_part(order, pieces, wanted, rows, gate_weight, up_weight, *totals):
+    depth, units = pieces.shape[2], gate_weight.shape[1]
+    begun = len(totals)
+
+    def body(order_ref, x_ref, gate_ref, up_ref, *refs):
+        starts, outs, (held_ref, sems) = refs[:begun], refs[begun:-2], refs[-2:]
+        copies = row_copies(order_ref, wanted, (gate_ref, up_ref), held_ref, sems)
+        for n in in_turn(copies, 3):
+            for k, out in enumerate(outs):
+                term = dot32(x_ref[wanted[n], :rows], held_ref[k, n])
+                if n:
+                    term = term + out[...]
+                elif begun:
+                    term = term + starts[k][...]
+                out[...] = term
 
     return kernel_call(
         body,
-        [in_smem, in_vmem, in_vmem, in_vmem],
+        [in_smem, in_vmem, in_hbm, in_hbm] + [in_vmem] * begun,
         [shape_of((rows, units), jnp.float32)] * 2,
-        6,
-    )(order, pieces, gate_weight, up_weight)
+        18,
+        [
+            pltpu.VMEM((2, len(wanted), depth, units), gate_weight.dtype),
+            pltpu.SemaphoreType.DMA((2, len(wanted))),
+        ],
+    )(order, pieces, in_place(gate_weight), in_place(up_weight), *totals)
 
 
 def forward_rest(
@@ -194,64 +204,57 @@
     rows, units = gate_part.shape
     width = down_weight.shape[1]
     chunk = width // 8
-    slots = 4
+    wanted = range(parts, 2 * parts)
 
     def body(
         order_ref, x_ref, gate_in, up_in, gate_ref, up_ref, down_ref, one_hot, extra_ref,
-        gate_out, up_out, own_out, other_out, held_ref, sems,
+        gate_out, up_out, own_out, other_out, held_ref, down_held, totals, sems, down_sems,
     ):
-        copies = [
-            pltpu.make_async_copy(
-                down_ref.at[:, pl.ds(i * chunk, chunk)], held_ref.at[i % slots], sems.at[i % slots]
+        copies = row_copies(order_ref, wanted, (gate_ref, up_ref), held_ref, sems)
+        for i in range(8):
+            at = pl.ds(i * chunk, chunk)
+            copies.append(
+                [pltpu.make_async_copy(down_ref.at[:, at], down_held.at[i], down_sems.at[i])]
             )
-            for i in range(8)
-        ]
-        for copy in copies[:slots]:
-            copy.start()
-        values = []
-        for start, weight in ((gate_in, gate_ref), (up_in, up_ref)):
-            total = start[...]
-            for i in range(parts):
-                at = pl.ds(pl.multiple_of(order_ref[parts + i] * depth, depth), depth)
-                total = total + dot32(x_ref[i, :rows], weight[at, :])
-            values.append(total)
-        gate, up = values
-        gate_out[:rows] = gate.astype(jnp.bfloat16)
-        gate_out[rows:] = extra_ref[...]
-        up_out[:rows] = up.astype(jnp.bfloat16)
-        up_out[rows:] = extra_ref[...]
-        hidden = (gate * sigmoid(gate) * up).astype(jnp.bfloat16)
-        hidden = dot32(one_hot[...], hidden).astype(jnp.bfloat16)
-        for i, copy in enumerate(copies):
-            copy.wait()
-            at = pl.ds(i * chunk, chunk)
-            total = dot32(hidden, held_ref[i % slots])
-            if i + slots < 8:
-                copies[i + slots].start()
+        hidden = None
+        for n in in_turn(copies, 4):
+            if n < parts:
+                for k, start in enumerate((gate_in, up_in)):
+                    term = dot32(x_ref[n, :rows], held_ref[k, n])
+                    totals[k] = term + (totals[k] if n else start[...])
+                continue
+            if hidden is None:
+                gate, up = totals[0], totals[1]
+                gate_out[:rows] = gate.astype(jnp.bfloat16)
+                gate_out[rows:] = extra_ref[...]
+                up_out[:rows] = up.astype(jnp.bfloat16)
+                up_out[rows:] = extra_ref[...]
+                hidden = (gate * sigmoid(gate) * up).astype(jnp.bfloat16)
+                hidden = dot32(one_hot[...], hidden).astype(jnp.bfloat16)
+            at = pl.ds((n - parts) * chunk, chunk)
+            total = dot32(hidden, down_held[n - parts])
             own_out[:, at] = total[: rows // 2].astype(jnp.bfloat16)
             other_out[:, at] = total[rows // 2 :].astype(jnp.bfloat16)
 
     return kernel_call(
         body,
-        [in_smem] + [in_vmem] * 5 + [in_hbm, in_vmem, in_vmem],
+        [in_smem] + [in_vmem] * 3 + [in_hbm] * 3 + [in_vmem] * 2,
+        [shape_of((rows + extra.shape[0], units))] * 2 + [shape_of((rows // 2, width))] * 2,
+        36,
         [
-            shape_of((rows + extra.shape[0], units)),
-            shape_of((rows + extra.shape[0], units)),
-            shape_of((rows // 2, width)),
-            shape_of((rows // 2, width)),
-        ],
-        13,
-        [
-            pltpu.VMEM((slots, units, chunk), down_weight.dtype),
-            pltpu.SemaphoreType.DMA((slots,)),
+            pltpu.VMEM((2, parts, depth, units), gate_weight.dtype),
+            pltpu.VMEM((8, units, chunk), down_weight.dtype),
+            pltpu.VMEM((2, rows, units), jnp.float32),
+            pltpu.SemaphoreType.DMA((2, parts)),
+            pltpu.SemaphoreType.DMA((8,)),
         ],
     )(
         order,
         pieces,
         gate_part,
         up_part,
-        gate_weight,
-        up_weight,
+        in_place(gate_weight),
+        in_place(up_weight),
         in_place(down_weight),
         to_relative,
         extra,
@@ -530,10 +533,12 @@
     slots = jnp.concatenate([negative_slots // slot_cap, negative_slots % slot_cap], axis=1)
     slots = jnp.pad(slots, ((0, 0), (0, mlp_input.shape[1] - 2 * negatives)))
     message = jnp.concatenate([mlp_input, slots.astype(jnp.bfloat16)], axis=0)
-    gate_held, up_held, loaded = load(place, gate_weight, up_weight)
-    first = gather_chips(message[None]) + loaded[0, 0].astype(jnp.bfloat16)
+    parts = forward_part(fsdp_order, message[None], (0,), group_rows, gate_weight, up_weight)
+    first, *parts = together(gather_chips(message[None]), *parts)
     second = swap_core(first)
-    gate_part, up_part = forward_first(fsdp_order, first, group_rows, gate_held, up_held)
+    gate_part, up_part = forward_part(
+        fsdp_order, first, tuple(range(1, chips)), group_rows, gate_weight, up_weight, *parts
+    )
     gate_part, up_part, second, span_later = together(gate_part, up_part, second, span_index)
     units = up_weight.shape[1]
     bands = units // (2 * negatives)
@@ -547,8 +552,8 @@
         second,
         gate_part,
         up_part,
-        gate_held,
-        up_held,
+        gate_weight,
+        up_weight,
         down_weight,
         to_relative,
         extra,
@@ -556,8 +561,8 @@
 
     near, far = 1, dp_count // 2
     own_part, other_part, other_index = together(own_part, other_part, other_index)
-    own_part, received, request_rows, request_counts, span_later = together(
-        own_part, swap_core(other_part), request_rows, request_counts, span_later
+    own_part, received, gate_act, up_act, request_rows, request_counts, span_later = together(
+        own_part, swap_core(other_part), gate_act, up_act, request_rows, request_counts, span_later
     )
     branch = add_up([own_part, received]).astype(jnp.bfloat16)
 
@@ -641,24 +646,29 @@
         inverse_temp * (pull - inner[:, None] * unit_rows) / row_norm[:, None]
     ).astype(jnp.bfloat16)
 
-    head_grad, gate_near, up_far = together(head_grad, gate_near, up_far)
-    own_rows, gate_last, up_last = together(
-        gather_chips(head_grad), swap(gate_near, "dp", far), swap(up_far, "dp", near)
-    )
+    own_rows, block_near, block_far, gate_near, up_far = together(
+        gather_chips(head_grad),
+        swap(blocks[near], "dp", near),
+        swap(blocks[far], "dp", far),
+        gate_near,
+        up_far,
+    )
+    gate_last, up_last = swap(gate_near, "dp", far), swap(up_far, "dp", near)
     other_rows = swap_core(own_rows)
+    own_gate_grad, own_up_grad, grads = backward_hidden(
+        dp_order, own_rows, other_rows, down_weight, gate_act, up_act, to_relative, dp_count
+    )
+    own_gate_grad, own_up_grad, gate_last, up_last, block_last, *grads = together(
+        own_gate_grad,
+        own_up_grad,
+        gate_last,
+        up_last,
+        swap(blocks[near + far], "dp", near + far),
+        *grads,
+    )
+    blocks = [blocks[0], block_near, block_far, block_last]
     gates = [gate_act, gate_near, gate_far, gate_last]
     ups = [up_act, up_near, up_far, up_last]
-    own_gate_grad, own_up_grad, grads = backward_hidden(
-        dp_order, own_rows, other_rows, down_weight, gate_act, up_act, to_relative, dp_count
-    )
-    own_gate_grad, own_up_grad, *rest = together(
-        own_gate_grad,
-        own_up_grad,
-        *grads,
-        blocks[0],
-        *[swap(blocks[k], "dp", k) for k in range(1, dp_count)],
-    )
-    grads, blocks = rest[:dp_count], rest[dp_count:]
     grads = [grads[0]] + [swap(grads[k], "dp", k) for k in range(1, dp_count)]
     own_blocks, other_blocks = backward_input(
         fsdp_order, own_gate_grad, own_up_grad, gate_weight, up_weight

time: 167 us -> 159 us (0.952)
  waiting for transfers between devices: 34.6 us -> 30.7 us
  starting transfers between devices: 48.7 us -> 51.4 us
  Pallas kernels: 61.1 us -> 58.5 us
  other arithmetic: 14 us -> 11.6 us
  local copies, waits for them, and re-layouts: 4.88 us -> 2.74 us
    ppermute x43, waiting for transfers between devices: 34.6 us -> 30.7 us  [swap(): return lax.ppermute(x, axis, pairs)]
    ppermute x43, starting transfers between devices: 48.7 us -> 51.4 us  [swap(): return lax.ppermute(x, axis, pairs)]
    pallas_call x3, Pallas kernels: 22.7 us -> 20.1 us  [the longest x1 10.9 us: forward_rest(): kernel_call(body, [in_smem] + [in_vmem] * 3 + [in_hbm] * 3 + [in_vmem] *...]
  transfers between devices with their start and end apart: 43 -> 43, of which waited for: 15 -> 16; matrix products, arithmetic and copies ran while one was open for 7% -> 7% of each run, Pallas kernels for 33% -> 33%
where the time goes in v5:
time: 159 us
  Pallas kernels  58.5 us (37%)
  starting transfers between devices  51.4 us (32%)
  waiting for transfers between devices  30.7 us (19%)
  other arithmetic  11.6 us (7%)
  local copies, waits for them, and re-layouts  2.74 us (2%)
  between operations  2.48 us (2%)
    ppermute x43, starting transfers between devices, swap(): return lax.ppermute(x, axis, pairs)  51.4 us
    ppermute x43, waiting for transfers between devices, swap(): return lax.ppermute(x, axis, pairs)  30.7 us
    pallas_call x1, Pallas kernels, backward_input(): kernel_call(body, [in_smem, in_vmem, in_vmem, in_hbm, in_hbm], [shape_of(...  12.7 us
    pallas_call x1, Pallas kernels, forward_rest(): kernel_call(body, [in_smem] + [in_vmem] * 3 + [in_hbm] * 3 + [in_vmem] *...  10.9 us
    pallas_call x2, Pallas kernels, forward_part(): kernel_call(body, [in_smem, in_vmem, in_hbm, in_hbm] + [in_vmem] * begun,...  9.21 us
    pallas_call x1, Pallas kernels, backward_hidden(): kernel_call(body, [in_smem, in_vmem, in_vmem, in_hbm, in_vmem, in_vmem, i...  7.46 us
    pallas_call x1, Pallas kernels, score_kernel(): kernel_call(body, [in_vmem] * pieces + [in_hbm] * 2 + [in_vmem] * 3, [sha...  6.68 us
    pallas_call x1, Pallas kernels, weight_grads(): pl.pallas_call(body, grid=(units // chunk,), in_specs=[in_vmem] * (4 * gr...  6.25 us
  transfers between devices with their start and end apart: 43, of which 16 were waited for; matrix products, arithmetic and copies ran while one was open for 7% of the time, Pallas kernels for 33%

profile of v5, /device:TPU:0, one launch (start us, length us, event | category | flops | bytes accessed | tf_op | source)
XLA Modules:
  0.0 158.8 jit_solution(9341083001053390584)
XLA Ops:
  2.3 3.0 %collective-permute-start = (bf16[1,72,512]{2,1,0:T(8,128)(2,1)S(1)}, bf16[1,72,512]{2,1,0:T(8,128)(2,1)S(1)}, u32[]{:S(2)}, u32[]{:S(2)}) collective-permute-start(bf16[1,72,512]{2,1,0:T(8,128)(2,1)S(1)} %maximum_bitcast_fusion.x_ref), channel_id=1, source_target_pairs={{0,2},{1,3},{2,0},{3,1},{4,6},{5,7},{6,4},{7,5},{8,10},{9,11},{10,... | collective-permute-start | bytes 221192 | tf_op jit(solution)/shard_map/ppermute | solution.py:35
  5.3 2.6 %collective-permute-start.1 = (bf16[1,72,512]{2,1,0:T(8,128)(2,1)S(1)}, bf16[1,72,512]{2,1,0:T(8,128)(2,1)S(1)}, u32[]{:S(2)}, u32[]{:S(2)}) collective-permute-start(bf16[1,72,512]{2,1,0:T(8,128)(2,1)S(1)} %maximum_bitcast_fusion.x_ref), channel_id=1, source_target_pairs={{0,4},{1,5},{2,6},{3,7},{4,0},{5,1},{6,2},{7,3},{8,12},{9,13},{10,... | collective-permute-start | bytes 221192 | tf_op jit(solution)/shard_map/ppermute | solution.py:35
  8.2 3.4 %shard_map.137 = (f32[64,1792]{1,0:T(8,128)S(1)}, f32[64,1792]{1,0:T(8,128)S(1)}) custom-call(s32[8]{0:T(128)S(1)} %fusion.40.order_ref, bf16[1,72,512]{2,1,0:T(8,128)(2,1)S(1)} %maximum_bitcast_fusion.x_ref, bf16[4096,1792]{1,0:T(8,128)(2,1)} %gate_ref.7, bf16[4096,1792]{1,0:T(8,128)(2,1)} %up_ref.7), custom_call_target="tpu_custom_call" | custom-call | tf_op jit(solution)/shard_map/pallas_call | solution.py:188
  14.3 5.8 %shard_map.138 = (f32[64,1792]{1,0:T(8,128)S(1)}, f32[64,1792]{1,0:T(8,128)S(1)}) custom-call(s32[8]{0:T(128)S(1)} %fusion.40.order_ref, bf16[4,72,512]{2,1,0:T(8,128)(2,1)S(1)} %pad_maximum_fusion.1.x_ref.first_ref, bf16[4096,1792]{1,0:T(8,128)(2,1)} %gate_ref.7, bf16[4096,1792]{1,0:T(8,128)(2,1)} %up_ref.7, f32[64,1792]{1,0:T(8,128)S(1)} %get-tuple-element.115.refs_0_, ...), custom_call_target="tpu_custom_call" | custom-call | tf_op jit(solution)/shard_map/pallas_call | solution.py:188
  20.4 10.9 %shard_map.139 = (bf16[72,1792]{1,0:T(8,128)(2,1)S(1)}, bf16[72,1792]{1,0:T(8,128)(2,1)S(1)}, bf16[32,4096]{1,0:T(8,128)(2,1)S(1)}, bf16[32,4096]{1,0:T(8,128)(2,1)S(1)}) custom-call(s32[8]{0:T(128)S(1)} %fusion.40.order_ref, bf16[4,72,512]{2,1,0:T(8,128)(2,1)S(1)} %collective-permute-done.3.x_ref.second_ref, f32[64,1792]{1,0:T(8,128)S(1)} %get-tuple-element.120.gate_in, ...), custom_call_target="tpu_custom_call" | custom-call | tf_op jit(solution)/shard_map/pallas_call | solution.py:239
  41.4 3.2 %collective-permute-done.7 = bf16[8,4096]{1,0:T(8,128)(2,1)S(1)} collective-permute-done((bf16[8,4096]{1,0:T(8,128)(2,1)S(1)}, bf16[8,4096]{1,0:T(8,128)(2,1)S(1)}, u32[]{:S(2)}, u32[]{:S(2)}) %collective-permute-start.7) | collective-permute-done | bytes 65568 | tf_op jit(solution)/shard_map/ppermute | solution.py:35
  44.6 2.4 %collective-permute-done.10.refs_10_.refs_14_ = bf16[72,1792]{1,0:T(8,128)(2,1)S(1)} collective-permute-done((bf16[72,1792]{1,0:T(8,128)(2,1)S(1)}, bf16[72,1792]{1,0:T(8,128)(2,1)S(1)}, u32[]{:S(2)}, u32[]{:S(2)}) %collective-permute-start.10) | collective-permute-done | bytes 258080 | tf_op jit(solution)/shard_map/ppermute | solution.py:35
  47.4 2.6 %collective-permute-start.13 = (bf16[8,4096]{1,0:T(8,128)(2,1)S(1)}, bf16[8,4096]{1,0:T(8,128)(2,1)S(1)}, u32[]{:S(2)}, u32[]{:S(2)}) collective-permute-start(bf16[8,4096]{1,0:T(8,128)(2,1)S(1)} %get-tuple-element.241), channel_id=1, source_target_pairs={{0,4},{1,5},{2,6},{3,7},{4,0},{5,1},{6,2},{7,3},{8,12},{9,13},{10,... | collective-permute-start | bytes 196616 | tf_op jit(solution)/shard_map/ppermute | solution.py:35
  53.1 3.1 %multiply_reduce_fusion = f32[512]{0:T(512)S(1)} fusion(bf16[512,4096]{1,0:T(8,128)(2,1)} %copy-done.2), kind=kLoop, calls=%fused_computation.1 | loop fusion | flops 6290944 | bytes 4196352 | tf_op jit(solution)/shard_map/reduce_sum | solution.py:30
  59.8 2.5 %collective-permute-start.18 = (bf16[32,4096]{1,0:T(8,128)(2,1)S(1)}, bf16[32,4096]{1,0:T(8,128)(2,1)S(1)}, u32[]{:S(2)}, u32[]{:S(2)}) collective-permute-start(bf16[32,4096]{1,0:T(8,128)(2,1)S(1)} %pad_maximum_fusion.2.refs_0_), channel_id=1, source_target_pairs={{0,24},{8,16},{16,8},{24,0},{1,25},{9,17},{17,9},{25,1},{2,26},{10... | collective-permute-start | bytes 786440 | tf_op jit(solution)/shard_map/ppermute | solution.py:35
  70.0 6.7 %shard_map.140 = (bf16[32,4224]{1,0:T(8,128)(2,1)S(1)}, bf16[32,4224]{1,0:T(8,128)(2,1)S(1)}, bf16[32,4224]{1,0:T(8,128)(2,1)S(1)}, bf16[32,4224]{1,0:T(8,128)(2,1)S(1)}) custom-call(bf16[32,4096]{1,0:T(8,128)(2,1)S(1)} %pad_maximum_fusion.2.refs_0_, bf16[32,4096]{1,0:T(8,128)(2,1)S(1)} %collective-permute-done.16.refs_1_, ...), custom_call_target="tpu_custom_call" | custom-call | tf_op jit(solution)/shard_map/pallas_call | solution.py:325
  80.5 3.2 %collective-permute-done.19 = bf16[32,4224]{1,0:T(8,128)(2,1)S(1)} collective-permute-done((bf16[32,4224]{1,0:T(8,128)(2,1)S(1)}, bf16[32,4224]{1,0:T(8,128)(2,1)S(1)}, u32[]{:S(2)}, u32[]{:S(2)}) %collective-permute-start.19) | collective-permute-done | bytes 270368 | tf_op jit(solution)/shard_map/ppermute | solution.py:35
  83.7 4.1 %collective-permute-done.20 = bf16[32,4224]{1,0:T(8,128)(2,1)S(1)} collective-permute-done((bf16[32,4224]{1,0:T(8,128)(2,1)S(1)}, bf16[32,4224]{1,0:T(8,128)(2,1)S(1)}, u32[]{:S(2)}, u32[]{:S(2)}) %collective-permute-start.20) | collective-permute-done | bytes 270368 | tf_op jit(solution)/shard_map/ppermute | solution.py:35
  88.0 2.7 %collective-permute-start.23 = (bf16[8,4224]{1,0:T(8,128)(2,1)S(1)}, bf16[8,4224]{1,0:T(8,128)(2,1)S(1)}, u32[]{:S(2)}, u32[]{:S(2)}) collective-permute-start(bf16[8,4224]{1,0:T(8,128)(2,1)S(1)} %get-tuple-element.231), channel_id=1, source_target_pairs={{0,4},{1,5},{2,6},{3,7},{4,0},{5,1},{6,2},{7,3},{8,12},{9,13},{10,... | collective-permute-start | bytes 202760 | tf_op jit(solution)/shard_map/ppermute | solution.py:35
  95.1 2.2 %collective-permute-done.24 = bf16[8,4224]{1,0:T(8,128)(2,1)S(1)} collective-permute-done((bf16[8,4224]{1,0:T(8,128)(2,1)S(1)}, bf16[8,4224]{1,0:T(8,128)(2,1)S(1)}, u32[]{:S(2)}, u32[]{:S(2)}) %collective-permute-start.24) | collective-permute-done | bytes 67616 | tf_op jit(solution)/shard_map/ppermute | solution.py:35
  100.9 2.8 %collective-permute-start.28 = (bf16[8,4096]{1,0:T(8,128)(2,1)S(1)}, bf16[8,4096]{1,0:T(8,128)(2,1)S(1)}, u32[]{:S(2)}, u32[]{:S(2)}) collective-permute-start(bf16[8,4096]{1,0:T(8,128)(2,1)S(1)} %divide_convert_fusion), channel_id=1, source_target_pairs={{0,4},{1,5},{2,6},{3,7},{4,0},{5,1},{6,2},{7,3},{8,12},{9,13},{10,... | collective-permute-start | bytes 196616 | tf_op jit(solution)/shard_map/ppermute | solution.py:35
  107.3 2.5 %collective-permute-done.29 = bf16[8,4096]{1,0:T(8,128)(2,1)S(1)} collective-permute-done((bf16[8,4096]{1,0:T(8,128)(2,1)S(1)}, bf16[8,4096]{1,0:T(8,128)(2,1)S(1)}, u32[]{:S(2)}, u32[]{:S(2)}) %collective-permute-start.29) | collective-permute-done | bytes 65568 | tf_op jit(solution)/shard_map/ppermute | solution.py:35
  112.2 1.7 %collective-permute-start.34 = (bf16[72,1792]{1,0:T(8,128)(2,1)S(1)}, bf16[72,1792]{1,0:T(8,128)(2,1)S(1)}, u32[]{:S(2)}, u32[]{:S(2)}) collective-permute-start(bf16[72,1792]{1,0:T(8,128)(2,1)S(1)} %collective-permute-done.10.refs_10_.refs_14_), channel_id=1, source_target_pairs={{0,8},{8,0},{16,24},{24,16},{1,9},{9,1},{17,25},{25,17},{2,10},{10... | collective-permute-start | bytes 774152 | tf_op jit(solution)/shard_map/ppermute | solution.py:35
  114.8 7.5 %shard_map.142 = (bf16[64,1792]{1,0:T(8,128)(2,1)S(1)}, bf16[64,1792]{1,0:T(8,128)(2,1)S(1)}, bf16[64,2816]{1,0:T(8,128)(2,1)S(1)}, bf16[64,2816]{1,0:T(8,128)(2...) custom-call(s32[4]{0:T(128)S(1)} %iota_xor_fusion.order_ref, ...), custom_call_target="tpu_custom_call" | custom-call | tf_op jit(solution)/shard_map/pallas_call | solution.py:373
  127.4 12.7 %shard_map.143 = (bf16[4,64,512]{2,1,0:T(8,128)(2,1)S(1)}, bf16[4,64,512]{2,1,0:T(8,128)(2,1)S(1)}) custom-call(s32[8]{0:T(128)S(1)} %fusion.40.order_ref, bf16[64,1792]{1,0:T(8,128)(2,1)S(1)} %get-tuple-element.190.gate_grad_ref, bf16[64,1792]{1,0:T(8,128)(2,1)S(1)} %get-tuple-element.191.up_grad_ref, bf16[4096,1792]{1,0:T(8,128)(2,1)} %gate_ref.7, ...), custom_call_target="tpu_custom_call" | custom-call | tf_op jit(solution)/shard_map/pallas_call | solution.py:419
  140.1 2.0 %collective-permute-done.37.refs_2_.refs_6_ = bf16[64,2816]{1,0:T(8,128)(2,1)S(1)} collective-permute-done((bf16[64,2816]{1,0:T(8,128)(2,1)S(1)}, bf16[64,2816]{1,0:T(8,128)(2,1)S(1)}, u32[]{:S(2)}, u32[]{:S(2)}) %collective-permute-start.37) | collective-permute-done | bytes 360480 | tf_op jit(solution)/shard_map/ppermute | solution.py:35
  142.1 4.7 %shard_map.144 = bf16[1792,1024]{1,0:T(8,128)(2,1)} custom-call(bf16[64,2816]{1,0:T(8,128)(2,1)S(1)} %get-tuple-element.200.refs_0_.refs_4_, bf16[64,2816]{1,0:T(8,128)(2,1)S(1)} %collective-permute-done.36.refs_1_.refs_5_, bf16[64,2816]{1,0:T(8,128)(2,1)S(1)} %collective-permute-done.37.refs_2_.refs_6_, ...), custom_call_target="tpu_custom_call" | custom-call | tf_op jit(solution)/shard_map/pallas_call | solution.py:488
  146.9 2.8 %collective-permute-start.41 = (bf16[1,64,512]{2,1,0:T(8,128)(2,1)S(1)}, bf16[1,64,512]{2,1,0:T(8,128)(2,1)S(1)}, u32[]{:S(2)}, u32[]{:S(2)}) collective-permute-start(bf16[1,64,512]{2,1,0:T(8,128)(2,1)S(1)} %get-tuple-element.234), channel_id=1, source_target_pairs={{0,4},{1,5},{2,6},{3,7},{4,0},{5,1},{6,2},{7,3},{8,12},{9,13},{10,... | collective-permute-start | bytes 196616 | tf_op jit(solution)/shard_map/ppermute | solution.py:35
  151.9 6.2 %shard_map.145 = (bf16[1024,1792]{1,0:T(8,128)(2,1)}, bf16[1024,1792]{1,0:T(8,128)(2,1)}) custom-call(bf16[64,1024]{1,0:T(8,128)(2,1)S(1)} %get-tuple-element.210.refs_0_, bf16[64,1024]{1,0:T(8,128)(2,1)S(1)} %collective-permute-done.30.refs_1_, bf16[64,1024]{1,0:T(8,128)(2,1)S(1)} %collective-permute-done.31.refs_2_, ...), custom_call_target="tpu_custom_call" | custom-call | tf_op jit(solution)/shard_map/pallas_call | solution.py:458
  (157 shorter events, 55.1 us)
Async XLA Ops:
  2.3 9.3 %collective-permute-start = (bf16[1,72,512]{2,1,0:T(8,128)(2,1)S(1)}, bf16[1,72,512]{2,1,0:T(8,128)(2,1)S(1)}, u32[]{:S(2)}, u32[]{:S(2)}) collective-permute-start(bf16[1,72,512]{2,1,0:T(8,128)(2,1)S(1)} %maximum_bitcast_fusion.x_ref), channel_id=1, source_target_pairs={{0,2},{1,3},{2,0},{3,1},{4,6},{5,7},{6,4},{7,5},{8,10},{9,11},{10,... | collective-permute-start | bytes 221192 | tf_op jit(solution)/shard_map/ppermute | solution.py:35
  5.3 7.8 %collective-permute-start.1 = (bf16[1,72,512]{2,1,0:T(8,128)(2,1)S(1)}, bf16[1,72,512]{2,1,0:T(8,128)(2,1)S(1)}, u32[]{:S(2)}, u32[]{:S(2)}) collective-permute-start(bf16[1,72,512]{2,1,0:T(8,128)(2,1)S(1)} %maximum_bitcast_fusion.x_ref), channel_id=1, source_target_pairs={{0,4},{1,5},{2,6},{3,7},{4,0},{5,1},{6,2},{7,3},{8,12},{9,13},{10,... | collective-permute-start | bytes 221192 | tf_op jit(solution)/shard_map/ppermute | solution.py:35
  20.1 11.2 %collective-permute-start.4 = (bf16[512,4096]{1,0:T(8,128)(2,1)S(1)}, bf16[512,4096]{1,0:T(8,128)(2,1)S(1)}, u32[]{:S(2)}, u32[]{:S(2)}) collective-permute-start(bf16[512,4096]{1,0:T(8,128)(2,1)S(1)} %copy-done), channel_id=1, source_target_pairs={{0,1},{1,0},{2,3},{3,2},{4,5},{5,4},{6,7},{7,6},{8,9},{9,8},{10,11... | collective-permute-start | bytes 12582920 | tf_op jit(solution)/shard_map/ppermute | solution.py:35
  33.9 13.2 %collective-permute-start.9 = (bf16[72,1792]{1,0:T(8,128)(2,1)S(1)}, bf16[72,1792]{1,0:T(8,128)(2,1)S(1)}, u32[]{:S(2)}, u32[]{:S(2)}) collective-permute-start(bf16[72,1792]{1,0:T(8,128)(2,1)S(1)} %get-tuple-element.167.gate_ref.refs_4_.refs_8_), channel_id=1, source_target_pairs={{0,8},{8,0},{16,24},{24,16},{1,9},{9,1},{17,25},{25,17},{2,10},{10... | collective-permute-start | bytes 774152 | tf_op jit(solution)/shard_map/ppermute | solution.py:35
  36.5 8.1 %collective-permute-start.7 = (bf16[8,4096]{1,0:T(8,128)(2,1)S(1)}, bf16[8,4096]{1,0:T(8,128)(2,1)S(1)}, u32[]{:S(2)}, u32[]{:S(2)}) collective-permute-start(bf16[8,4096]{1,0:T(8,128)(2,1)S(1)} %get-tuple-element.237), channel_id=1, source_target_pairs={{0,4},{1,5},{2,6},{3,7},{4,0},{5,1},{6,2},{7,3},{8,12},{9,13},{10,... | collective-permute-start | bytes 196616 | tf_op jit(solution)/shard_map/ppermute | solution.py:35
  39.8 7.2 %collective-permute-start.10 = (bf16[72,1792]{1,0:T(8,128)(2,1)S(1)}, bf16[72,1792]{1,0:T(8,128)(2,1)S(1)}, u32[]{:S(2)}, u32[]{:S(2)}) collective-permute-start(bf16[72,1792]{1,0:T(8,128)(2,1)S(1)} %get-tuple-element.168.up_ref.refs_8_.refs_12_), channel_id=1, source_target_pairs={{0,16},{8,24},{16,0},{24,8},{1,17},{9,25},{17,1},{25,9},{2,18},{10... | collective-permute-start | bytes 774152 | tf_op jit(solution)/shard_map/ppermute | solution.py:35
  47.2 10.0 %collective-permute-start.12 = (bf16[8,4096]{1,0:T(8,128)(2,1)S(1)}, bf16[8,4096]{1,0:T(8,128)(2,1)S(1)}, u32[]{:S(2)}, u32[]{:S(2)}) collective-permute-start(bf16[8,4096]{1,0:T(8,128)(2,1)S(1)} %get-tuple-element.241), channel_id=1, source_target_pairs={{0,2},{1,3},{2,0},{3,1},{4,6},{5,7},{6,4},{7,5},{8,10},{9,11},{10,... | collective-permute-start | bytes 196616 | tf_op jit(solution)/shard_map/ppermute | solution.py:35
  47.4 9.8 %collective-permute-start.13 = (bf16[8,4096]{1,0:T(8,128)(2,1)S(1)}, bf16[8,4096]{1,0:T(8,128)(2,1)S(1)}, u32[]{:S(2)}, u32[]{:S(2)}) collective-permute-start(bf16[8,4096]{1,0:T(8,128)(2,1)S(1)} %get-tuple-element.241), channel_id=1, source_target_pairs={{0,4},{1,5},{2,6},{3,7},{4,0},{5,1},{6,2},{7,3},{8,12},{9,13},{10,... | collective-permute-start | bytes 196616 | tf_op jit(solution)/shard_map/ppermute | solution.py:35
  50.0 7.2 %collective-permute-start.14 = (bf16[8,4096]{1,0:T(8,128)(2,1)S(1)}, bf16[8,4096]{1,0:T(8,128)(2,1)S(1)}, u32[]{:S(2)}, u32[]{:S(2)}) collective-permute-start(bf16[8,4096]{1,0:T(8,128)(2,1)S(1)} %get-tuple-element.241), channel_id=1, source_target_pairs={{0,6},{1,7},{2,4},{3,5},{4,2},{5,3},{6,0},{7,1},{8,14},{9,15},{10,... | collective-permute-start | bytes 196616 | tf_op jit(solution)/shard_map/ppermute | solution.py:35
  58.7 10.0 %collective-permute-start.16 = (bf16[32,4096]{1,0:T(8,128)(2,1)S(1)}, bf16[32,4096]{1,0:T(8,128)(2,1)S(1)}, u32[]{:S(2)}, u32[]{:S(2)}) collective-permute-start(bf16[32,4096]{1,0:T(8,128)(2,1)S(1)} %pad_maximum_fusion.2.refs_0_), channel_id=1, source_target_pairs={{0,8},{8,0},{16,24},{24,16},{1,9},{9,1},{17,25},{25,17},{2,10},{10... | collective-permute-start | bytes 786440 | tf_op jit(solution)/shard_map/ppermute | solution.py:35
  59.3 10.6 %collective-permute-start.17 = (bf16[32,4096]{1,0:T(8,128)(2,1)S(1)}, bf16[32,4096]{1,0:T(8,128)(2,1)S(1)}, u32[]{:S(2)}, u32[]{:S(2)}) collective-permute-start(bf16[32,4096]{1,0:T(8,128)(2,1)S(1)} %pad_maximum_fusion.2.refs_0_), channel_id=1, source_target_pairs={{0,16},{8,24},{16,0},{24,8},{1,17},{9,25},{17,1},{25,9},{2,18},{10... | collective-permute-start | bytes 786440 | tf_op jit(solution)/shard_map/ppermute | solution.py:35
  59.8 10.1 %collective-permute-start.18 = (bf16[32,4096]{1,0:T(8,128)(2,1)S(1)}, bf16[32,4096]{1,0:T(8,128)(2,1)S(1)}, u32[]{:S(2)}, u32[]{:S(2)}) collective-permute-start(bf16[32,4096]{1,0:T(8,128)(2,1)S(1)} %pad_maximum_fusion.2.refs_0_), channel_id=1, source_target_pairs={{0,24},{8,16},{16,8},{24,0},{1,25},{9,17},{17,9},{25,1},{2,26},{10... | collective-permute-start | bytes 786440 | tf_op jit(solution)/shard_map/ppermute | solution.py:35
  78.3 9.5 %collective-permute-start.20 = (bf16[32,4224]{1,0:T(8,128)(2,1)S(1)}, bf16[32,4224]{1,0:T(8,128)(2,1)S(1)}, u32[]{:S(2)}, u32[]{:S(2)}) collective-permute-start(bf16[32,4224]{1,0:T(8,128)(2,1)S(1)} %get-tuple-element.164), channel_id=1, source_target_pairs={{0,16},{8,24},{16,0},{24,8},{1,17},{9,25},{17,1},{25,9},{2,18},{10... | collective-permute-start | bytes 811016 | tf_op jit(solution)/shard_map/ppermute | solution.py:35
  78.8 9.0 %collective-permute-start.21 = (bf16[32,4224]{1,0:T(8,128)(2,1)S(1)}, bf16[32,4224]{1,0:T(8,128)(2,1)S(1)}, u32[]{:S(2)}, u32[]{:S(2)}) collective-permute-start(bf16[32,4224]{1,0:T(8,128)(2,1)S(1)} %get-tuple-element.165), channel_id=1, source_target_pairs={{0,24},{8,16},{16,8},{24,0},{1,25},{9,17},{17,9},{25,1},{2,26},{10... | collective-permute-start | bytes 811016 | tf_op jit(solution)/shard_map/ppermute | solution.py:35
  93.0 7.3 %collective-permute-start.26 = (bf16[72,1792]{1,0:T(8,128)(2,1)S(1)}, bf16[72,1792]{1,0:T(8,128)(2,1)S(1)}, u32[]{:S(2)}, u32[]{:S(2)}) collective-permute-start(bf16[72,1792]{1,0:T(8,128)(2,1)S(1)} %get-tuple-element.168.up_ref.refs_8_.refs_12_), channel_id=1, source_target_pairs={{0,8},{8,0},{16,24},{24,16},{1,9},{9,1},{17,25},{25,17},{2,10},{10... | collective-permute-start | bytes 774152 | tf_op jit(solution)/shard_map/ppermute | solution.py:35
  111.3 12.6 %collective-permute-start.33 = (bf16[72,1792]{1,0:T(8,128)(2,1)S(1)}, bf16[72,1792]{1,0:T(8,128)(2,1)S(1)}, u32[]{:S(2)}, u32[]{:S(2)}) collective-permute-start(bf16[72,1792]{1,0:T(8,128)(2,1)S(1)} %collective-permute-done.9.refs_5_.refs_9_), channel_id=1, source_target_pairs={{0,16},{8,24},{16,0},{24,8},{1,17},{9,25},{17,1},{25,9},{2,18},{10... | collective-permute-start | bytes 774152 | tf_op jit(solution)/shard_map/ppermute | solution.py:35
  112.2 11.7 %collective-permute-start.34 = (bf16[72,1792]{1,0:T(8,128)(2,1)S(1)}, bf16[72,1792]{1,0:T(8,128)(2,1)S(1)}, u32[]{:S(2)}, u32[]{:S(2)}) collective-permute-start(bf16[72,1792]{1,0:T(8,128)(2,1)S(1)} %collective-permute-done.10.refs_10_.refs_14_), channel_id=1, source_target_pairs={{0,8},{8,0},{16,24},{24,16},{1,9},{9,1},{17,25},{25,17},{2,10},{10... | collective-permute-start | bytes 774152 | tf_op jit(solution)/shard_map/ppermute | solution.py:35
  114.0 9.9 %collective-permute-start.35 = (bf16[64,1024]{1,0:T(8,128)(2,1)S(1)}, bf16[64,1024]{1,0:T(8,128)(2,1)S(1)}, u32[]{:S(2)}, u32[]{:S(2)}) collective-permute-start(bf16[64,1024]{1,0:T(8,128)(2,1)S(1)} %get-tuple-element.185), channel_id=1, source_target_pairs={{0,24},{8,16},{16,8},{24,0},{1,25},{9,17},{17,9},{25,1},{2,26},{10... | collective-permute-start | bytes 393224 | tf_op jit(solution)/shard_map/ppermute | solution.py:35
  123.9 16.2 %collective-permute-start.36 = (bf16[64,2816]{1,0:T(8,128)(2,1)S(1)}, bf16[64,2816]{1,0:T(8,128)(2,1)S(1)}, u32[]{:S(2)}, u32[]{:S(2)}) collective-permute-start(bf16[64,2816]{1,0:T(8,128)(2,1)S(1)} %get-tuple-element.195), channel_id=1, source_target_pairs={{0,8},{8,0},{16,24},{24,16},{1,9},{9,1},{17,25},{25,17},{2,10},{10... | collective-permute-start | bytes 1081352 | tf_op jit(solution)/shard_map/ppermute | solution.py:35
  124.9 17.2 %collective-permute-start.37 = (bf16[64,2816]{1,0:T(8,128)(2,1)S(1)}, bf16[64,2816]{1,0:T(8,128)(2,1)S(1)}, u32[]{:S(2)}, u32[]{:S(2)}) collective-permute-start(bf16[64,2816]{1,0:T(8,128)(2,1)S(1)} %get-tuple-element.196), channel_id=1, source_target_pairs={{0,16},{8,24},{16,0},{24,8},{1,17},{9,25},{17,1},{25,9},{2,18},{10... | collective-permute-start | bytes 1081352 | tf_op jit(solution)/shard_map/ppermute | solution.py:35
  126.6 15.5 %collective-permute-start.38 = (bf16[64,2816]{1,0:T(8,128)(2,1)S(1)}, bf16[64,2816]{1,0:T(8,128)(2,1)S(1)}, u32[]{:S(2)}, u32[]{:S(2)}) collective-permute-start(bf16[64,2816]{1,0:T(8,128)(2,1)S(1)} %get-tuple-element.197), channel_id=1, source_target_pairs={{0,24},{8,16},{16,8},{24,0},{1,25},{9,17},{17,9},{25,1},{2,26},{10... | collective-permute-start | bytes 1081352 | tf_op jit(solution)/shard_map/ppermute | solution.py:35
  146.9 11.2 %collective-permute-start.40 = (bf16[1,64,512]{2,1,0:T(8,128)(2,1)S(1)}, bf16[1,64,512]{2,1,0:T(8,128)(2,1)S(1)}, u32[]{:S(2)}, u32[]{:S(2)}) collective-permute-start(bf16[1,64,512]{2,1,0:T(8,128)(2,1)S(1)} %get-tuple-element.232), channel_id=1, source_target_pairs={{0,2},{1,3},{2,0},{3,1},{4,6},{5,7},{6,4},{7,5},{8,10},{9,11},{10,... | collective-permute-start | bytes 196616 | tf_op jit(solution)/shard_map/ppermute | solution.py:35
  146.9 11.2 %collective-permute-start.41 = (bf16[1,64,512]{2,1,0:T(8,128)(2,1)S(1)}, bf16[1,64,512]{2,1,0:T(8,128)(2,1)S(1)}, u32[]{:S(2)}, u32[]{:S(2)}) collective-permute-start(bf16[1,64,512]{2,1,0:T(8,128)(2,1)S(1)} %get-tuple-element.234), channel_id=1, source_target_pairs={{0,4},{1,5},{2,6},{3,7},{4,0},{5,1},{6,2},{7,3},{8,12},{9,13},{10,... | collective-permute-start | bytes 196616 | tf_op jit(solution)/shard_map/ppermute | solution.py:35
  149.8 8.4 %collective-permute-start.42 = (bf16[1,64,512]{2,1,0:T(8,128)(2,1)S(1)}, bf16[1,64,512]{2,1,0:T(8,128)(2,1)S(1)}, u32[]{:S(2)}, u32[]{:S(2)}) collective-permute-start(bf16[1,64,512]{2,1,0:T(8,128)(2,1)S(1)} %get-tuple-element.233), channel_id=1, source_target_pairs={{0,6},{1,7},{2,4},{3,5},{4,2},{5,3},{6,0},{7,1},{8,14},{9,15},{10,... | collective-permute-start | bytes 196616 | tf_op jit(solution)/shard_map/ppermute | solution.py:35
  (26 other events, 205.2 us)

commit v6 on v5

--- a/solution.py
+++ b/solution.py
@@ -433,36 +433,42 @@
     rows, units = grads[0].shape[0], gate_acts[0].shape[1]
     width = input_columns[0].shape[1]
     chunk = 256 if units % 256 == 0 else units
+    chunks = units // chunk
 
     def body(*refs):
-        columns, refs, turned = refs[:groups], refs[groups:-1], refs[-1]
-
-        @pl.when(pl.program_id(0) == 0)
-        def _():
-            turned[...] = jnp.concatenate([r[...] for r in columns], axis=0).T
-
-        at = pl.ds(0, units)
-        if chunk < units:
-            at = pl.ds(pl.multiple_of(pl.program_id(0) * chunk, chunk), chunk)
-        hidden_grad, gate, up = (
-            jnp.concatenate([r[:rows, at] for r in refs[k * groups : (k + 1) * groups]], axis=0)
-            for k in range(3)
-        )
-        gate_out, up_out = refs[3 * groups :]
-        gate_grad, up_grad = activation_grads(
-            hidden_grad.astype(jnp.float32), gate.astype(jnp.float32), up.astype(jnp.float32)
-        )
-        gate_out[...] = dot32(turned[...], gate_grad).astype(jnp.bfloat16)
-        up_out[...] = dot32(turned[...], up_grad).astype(jnp.bfloat16)
+        columns, refs = refs[:groups], refs[groups:]
+        (gate_out, up_out, turned, made, sems), refs = refs[3 * groups :], refs[: 3 * groups]
+        turned[...] = jnp.concatenate([r[...] for r in columns], axis=0).T
+        copies = []
+        for i in range(chunks):
+            at = pl.ds(i * chunk, chunk)
+            hidden_grad, gate, up = (
+                jnp.concatenate([r[:rows, at] for r in refs[k * groups : (k + 1) * groups]], axis=0)
+                for k in range(3)
+            )
+            both = activation_grads(
+                hidden_grad.astype(jnp.float32), gate.astype(jnp.float32), up.astype(jnp.float32)
+            )
+            for k, out in enumerate((gate_out, up_out)):
+                made[k, i] = dot32(turned[...], both[k]).astype(jnp.bfloat16)
+                copies.append(
+                    pltpu.make_async_copy(made.at[k, i], out.at[:, at], sems.at[k, i])
+                )
+                copies[-1].start()
+        for copy in copies:
+            copy.wait()
 
     return pl.pallas_call(
         body,
-        grid=(units // chunk,),
         in_specs=[in_vmem] * (4 * groups),
-        out_specs=[pl.BlockSpec((width, chunk), lambda i: (0, i))] * 2,
+        out_specs=[pl.BlockSpec(memory_space=pl.ANY)] * 2,
         out_shape=[shape_of((width, units))] * 2,
-        scratch_shapes=[pltpu.VMEM((width, groups * rows), jnp.bfloat16)],
-        compiler_params=pltpu.CompilerParams(vmem_limit_bytes=14 * mib),
+        scratch_shapes=[
+            pltpu.VMEM((width, groups * rows), jnp.bfloat16),
+            pltpu.VMEM((2, chunks, width, chunk), jnp.bfloat16),
+            pltpu.SemaphoreType.DMA((2, chunks)),
+        ],
+        compiler_params=pltpu.CompilerParams(vmem_limit_bytes=18 * mib),
     )(*input_columns, *grads, *gate_acts, *up_acts)
 
 
@@ -471,26 +477,35 @@
     rows, units = grads[0].shape[0], gate_acts[0].shape[1]
     width = grads[0].shape[1] - units
     chunk = 256 if units % 256 == 0 else units
+    chunks = units // chunk
 
     def body(*refs):
-        at = pl.ds(0, units)
-        if chunk < units:
-            at = pl.ds(pl.multiple_of(pl.program_id(0) * chunk, chunk), chunk)
-        gate, up = (
-            jnp.concatenate([r[:rows, at] for r in refs[k * groups : (k + 1) * groups]], axis=0)
-            for k in (1, 2)
-        )
-        gate, up = gate.astype(jnp.float32), up.astype(jnp.float32)
-        hidden = (gate * sigmoid(gate) * up).astype(jnp.bfloat16)
+        (out, made, sems), refs = refs[3 * groups :], refs[: 3 * groups]
         head_grad = jnp.concatenate([r[:, units:] for r in refs[:groups]], axis=0)
-        refs[-1][...] = dot32(hidden, head_grad, contract_first).astype(jnp.bfloat16)
+        copies = []
+        for i in range(chunks):
+            at = pl.ds(i * chunk, chunk)
+            gate, up = (
+                jnp.concatenate([r[:rows, at] for r in refs[k * groups : (k + 1) * groups]], axis=0)
+                for k in (1, 2)
+            )
+            gate, up = gate.astype(jnp.float32), up.astype(jnp.float32)
+            hidden = (gate * sigmoid(gate) * up).astype(jnp.bfloat16)
+            made[i] = dot32(hidden, head_grad, contract_first).astype(jnp.bfloat16)
+            copies.append(pltpu.make_async_copy(made.at[i], out.at[at], sems.at[i]))
+            copies[-1].start()
+        for copy in copies:
+            copy.wait()
 
     return pl.pallas_call(
         body,
-        grid=(units // chunk,),
         in_specs=[in_vmem] * (3 * groups),
-        out_specs=pl.BlockSpec((chunk, width), lambda i: (i, 0)),
+        out_specs=pl.BlockSpec(memory_space=pl.ANY),
         out_shape=shape_of((units, width)),
+        scratch_shapes=[
+            pltpu.VMEM((chunks, chunk, width), jnp.bfloat16),
+            pltpu.SemaphoreType.DMA((chunks,)),
+        ],
         compiler_params=pltpu.CompilerParams(vmem_limit_bytes=14 * mib),
     )(*grads, *gate_acts, *up_acts)
 
@@ -539,7 +554,10 @@
     gate_part, up_part = forward_part(
         fsdp_order, first, tuple(range(1, chips)), group_rows, gate_weight, up_weight, *parts
     )
-    gate_part, up_part, second, span_later = together(gate_part, up_part, second, span_index)
+    tables = jnp.concatenate([request_rows[:, 0, :], request_counts], axis=1)[None]
+    gate_part, up_part, second, span_later, tables = together(
+        gate_part, up_part, second, span_index, gather_core(tables)
+    )
     units = up_weight.shape[1]
     bands = units // (2 * negatives)
     extra = [first[c, group_rows:, : 2 * negatives] for c in range(chips)]
@@ -561,17 +579,17 @@
 
     near, far = 1, dp_count // 2
     own_part, other_part, other_index = together(own_part, other_part, other_index)
-    own_part, received, gate_act, up_act, request_rows, request_counts, span_later = together(
-        own_part, swap_core(other_part), gate_act, up_act, request_rows, request_counts, span_later
+    own_part, received, gate_act, up_act, span_later, tables = together(
+        own_part, swap_core(other_part), gate_act, up_act, span_later, tables
     )
     branch = add_up([own_part, received]).astype(jnp.bfloat16)
 
-    tables = jnp.concatenate([request_rows[:, 0, :], request_counts], axis=1)[None]
-    tables = gather_core(tables)
-    top_state, gate_near, up_far, span_later, other_index, tables = together(
+    tables = jnp.take(tables, asker, axis=1)
+    top_state, gate_near, up_far, own_norm, span_later, other_index, tables = together(
         sum_chips(branch) + residual_in.astype(jnp.float32),
         swap(gate_act, "dp", near),
         swap(up_act, "dp", far),
+        norm_of(span_later.astype(jnp.float32)),
         span_later,
         other_index,
         tables,
@@ -579,16 +597,14 @@
     row_norm = norm_of(top_state)
     unit_rows = top_state / row_norm[:, None]
 
-    states, last_slots, own_norm, other_norm, span_later, other_index, tables, positive_keys, asker, both = together(
+    states, last_slots, other_norm, span_later, other_index, tables, positive_keys, both = together(
         gather_chips(top_state.astype(jnp.bfloat16)),
         swap(gate_near[group_rows:], "dp", far),
-        norm_of(span_later.astype(jnp.float32)),
-        norm_of(other_index.astype(jnp.float32)),
+        swap_core(own_norm),
         span_later,
         other_index,
         tables,
         positive_keys,
-        asker,
         both,
     )
     index_norm = jnp.concatenate([own_norm, other_norm], axis=0)
@@ -604,7 +620,6 @@
     ]
     slots = jnp.stack(slots, axis=1).reshape(dp_count * chips, own_queries, 2 * negatives)
     slots = slots[..., :negatives] * slot_cap + slots[..., negatives:]
-    tables = jnp.take(tables, asker, axis=1)
     counts, dead = [], 0.0
     for k in range(2):
         shard_counts, shard_dead = use_counts(

time: 159 us -> 156 us (0.981)
  waiting for transfers between devices: 30.7 us -> 36.1 us
  Pallas kernels: 58.5 us -> 53.7 us
  other arithmetic: 11.6 us -> 8.29 us
    ppermute x43 -> x44, waiting for transfers between devices: 30.7 us -> 36.1 us  [swap(): return lax.ppermute(x, axis, pairs)]
    pallas_call x2, Pallas kernels: 10.9 us -> 6 us  [the longest x1 3.72 us: weight_grads(): pl.pallas_call(body, in_specs=[in_vmem] * (4 * groups), out_specs=[pl.Blo...]
    reduce_sum x4 -> x3, other arithmetic: 4.27 us -> 1.18 us  [norm_of(): return jnp.sqrt(jnp.sum(rows * rows, axis=-1) + eps)]
    ppermute x43 -> x44, starting transfers between devices: 51.4 us -> 51.5 us  [swap(): return lax.ppermute(x, axis, pairs)]
  transfers between devices with their start and end apart: 43 -> 44, of which waited for: 16 -> 19; matrix products, arithmetic and copies ran while one was open for 7% -> 5% of each run, Pallas kernels for 33% -> 30%
where the time goes in v6:
time: 156 us
  Pallas kernels  53.7 us (34%)
  starting transfers between devices  51.5 us (33%)
  waiting for transfers between devices  36.1 us (23%)
  other arithmetic  8.29 us (5%)
  between operations  2.5 us (2%)
  local copies, waits for them, and re-layouts  2.4 us (2%)
    ppermute x44, starting transfers between devices, swap(): return lax.ppermute(x, axis, pairs)  51.5 us
    ppermute x44, waiting for transfers between devices, swap(): return lax.ppermute(x, axis, pairs)  36.1 us
    pallas_call x1, Pallas kernels, backward_input(): kernel_call(body, [in_smem, in_vmem, in_vmem, in_hbm, in_hbm], [shape_of(...  12.7 us
    pallas_call x1, Pallas kernels, forward_rest(): kernel_call(body, [in_smem] + [in_vmem] * 3 + [in_hbm] * 3 + [in_vmem] *...  10.9 us
    pallas_call x2, Pallas kernels, forward_part(): kernel_call(body, [in_smem, in_vmem, in_hbm, in_hbm] + [in_vmem] * begun,...  9.18 us
    pallas_call x1, Pallas kernels, backward_hidden(): kernel_call(body, [in_smem, in_vmem, in_vmem, in_hbm, in_vmem, in_vmem, i...  7.45 us
    pallas_call x1, Pallas kernels, score_kernel(): kernel_call(body, [in_vmem] * pieces + [in_hbm] * 2 + [in_vmem] * 3, [sha...  6.86 us
    pallas_call x1, Pallas kernels, weight_grads(): pl.pallas_call(body, in_specs=[in_vmem] * (4 * groups), out_specs=[pl.Blo...  3.72 us
  transfers between devices with their start and end apart: 44, of which 19 were waited for; matrix products, arithmetic and copies ran while one was open for 5% of the time, Pallas kernels for 30%

profile of v6, /device:TPU:0, one launch (start us, length us, event | category | flops | bytes accessed | tf_op | source)
XLA Modules:
  0.0 155.8 jit_solution(2381638659734874732)
XLA Ops:
  2.3 3.0 %collective-permute-start = (bf16[1,72,512]{2,1,0:T(8,128)(2,1)S(1)}, bf16[1,72,512]{2,1,0:T(8,128)(2,1)S(1)}, u32[]{:S(2)}, u32[]{:S(2)}) collective-permute-start(bf16[1,72,512]{2,1,0:T(8,128)(2,1)S(1)} %maximum_bitcast_fusion.x_ref), channel_id=1, source_target_pairs={{0,2},{1,3},{2,0},{3,1},{4,6},{5,7},{6,4},{7,5},{8,10},{9,11},{10,... | collective-permute-start | bytes 221192 | tf_op jit(solution)/shard_map/ppermute | solution.py:35
  5.3 2.6 %collective-permute-start.1 = (bf16[1,72,512]{2,1,0:T(8,128)(2,1)S(1)}, bf16[1,72,512]{2,1,0:T(8,128)(2,1)S(1)}, u32[]{:S(2)}, u32[]{:S(2)}) collective-permute-start(bf16[1,72,512]{2,1,0:T(8,128)(2,1)S(1)} %maximum_bitcast_fusion.x_ref), channel_id=1, source_target_pairs={{0,4},{1,5},{2,6},{3,7},{4,0},{5,1},{6,2},{7,3},{8,12},{9,13},{10,... | collective-permute-start | bytes 221192 | tf_op jit(solution)/shard_map/ppermute | solution.py:35
  8.2 3.4 %shard_map.137 = (f32[64,1792]{1,0:T(8,128)S(1)}, f32[64,1792]{1,0:T(8,128)S(1)}) custom-call(s32[8]{0:T(128)S(1)} %fusion.40.order_ref, bf16[1,72,512]{2,1,0:T(8,128)(2,1)S(1)} %maximum_bitcast_fusion.x_ref, bf16[4096,1792]{1,0:T(8,128)(2,1)} %gate_ref.7, bf16[4096,1792]{1,0:T(8,128)(2,1)} %up_ref.7), custom_call_target="tpu_custom_call" | custom-call | tf_op jit(solution)/shard_map/pallas_call | solution.py:188
  15.9 5.8 %shard_map.138 = (f32[64,1792]{1,0:T(8,128)S(1)}, f32[64,1792]{1,0:T(8,128)S(1)}) custom-call(s32[8]{0:T(128)S(1)} %fusion.40.order_ref, bf16[4,72,512]{2,1,0:T(8,128)(2,1)S(1)} %pad_maximum_fusion.1.x_ref.first_ref, bf16[4096,1792]{1,0:T(8,128)(2,1)} %gate_ref.7, bf16[4096,1792]{1,0:T(8,128)(2,1)} %up_ref.7, f32[64,1792]{1,0:T(8,128)S(1)} %get-tuple-element.114.refs_0_, ...), custom_call_target="tpu_custom_call" | custom-call | tf_op jit(solution)/shard_map/pallas_call | solution.py:188
  22.1 10.9 %shard_map.139 = (bf16[72,1792]{1,0:T(8,128)(2,1)S(1)}, bf16[72,1792]{1,0:T(8,128)(2,1)S(1)}, bf16[32,4096]{1,0:T(8,128)(2,1)S(1)}, bf16[32,4096]{1,0:T(8,128)(2,1)S(1)}) custom-call(s32[8]{0:T(128)S(1)} %fusion.40.order_ref, bf16[4,72,512]{2,1,0:T(8,128)(2,1)S(1)} %collective-permute-done.3.x_ref.second_ref, f32[64,1792]{1,0:T(8,128)S(1)} %get-tuple-element.119.gate_in, ...), custom_call_target="tpu_custom_call" | custom-call | tf_op jit(solution)/shard_map/pallas_call | solution.py:239
  37.3 1.7 %collective-permute-start.8 = (bf16[8,4096]{1,0:T(8,128)(2,1)S(1)}, bf16[8,4096]{1,0:T(8,128)(2,1)S(1)}, u32[]{:S(2)}, u32[]{:S(2)}) collective-permute-start(bf16[8,4096]{1,0:T(8,128)(2,1)S(1)} %get-tuple-element.235), channel_id=1, source_target_pairs={{0,4},{1,5},{2,6},{3,7},{4,0},{5,1},{6,2},{7,3},{8,12},{9,13},{10,... | collective-permute-start | bytes 196616 | tf_op jit(solution)/shard_map/ppermute | solution.py:35
  43.7 1.7 %collective-permute-done.8 = bf16[8,4096]{1,0:T(8,128)(2,1)S(1)} collective-permute-done((bf16[8,4096]{1,0:T(8,128)(2,1)S(1)}, bf16[8,4096]{1,0:T(8,128)(2,1)S(1)}, u32[]{:S(2)}, u32[]{:S(2)}) %collective-permute-start.8) | collective-permute-done | bytes 65568 | tf_op jit(solution)/shard_map/ppermute | solution.py:35
  45.5 2.4 %collective-permute-done.11.refs_10_.refs_14_ = bf16[72,1792]{1,0:T(8,128)(2,1)S(1)} collective-permute-done((bf16[72,1792]{1,0:T(8,128)(2,1)S(1)}, bf16[72,1792]{1,0:T(8,128)(2,1)S(1)}, u32[]{:S(2)}, u32[]{:S(2)}) %collective-permute-start.11) | collective-permute-done | bytes 258080 | tf_op jit(solution)/shard_map/ppermute | solution.py:35
  48.3 2.6 %collective-permute-start.13 = (bf16[8,4096]{1,0:T(8,128)(2,1)S(1)}, bf16[8,4096]{1,0:T(8,128)(2,1)S(1)}, u32[]{:S(2)}, u32[]{:S(2)}) collective-permute-start(bf16[8,4096]{1,0:T(8,128)(2,1)S(1)} %get-tuple-element.239), channel_id=1, source_target_pairs={{0,4},{1,5},{2,6},{3,7},{4,0},{5,1},{6,2},{7,3},{8,12},{9,13},{10,... | collective-permute-start | bytes 196616 | tf_op jit(solution)/shard_map/ppermute | solution.py:35
  54.8 2.1 %collective-permute-done.14 = bf16[8,4096]{1,0:T(8,128)(2,1)S(1)} collective-permute-done((bf16[8,4096]{1,0:T(8,128)(2,1)S(1)}, bf16[8,4096]{1,0:T(8,128)(2,1)S(1)}, u32[]{:S(2)}, u32[]{:S(2)}) %collective-permute-start.14) | collective-permute-done | bytes 65568 | tf_op jit(solution)/shard_map/ppermute | solution.py:35
  67.6 2.7 %collective-permute-done.18.refs_2_ = bf16[32,4096]{1,0:T(8,128)(2,1)S(1)} collective-permute-done((bf16[32,4096]{1,0:T(8,128)(2,1)S(1)}, bf16[32,4096]{1,0:T(8,128)(2,1)S(1)}, u32[]{:S(2)}, u32[]{:S(2)}) %collective-permute-start.18) | collective-permute-done | bytes 262176 | tf_op jit(solution)/shard_map/ppermute | solution.py:35
  70.4 6.9 %shard_map.140 = (bf16[32,4224]{1,0:T(8,128)(2,1)S(1)}, bf16[32,4224]{1,0:T(8,128)(2,1)S(1)}, bf16[32,4224]{1,0:T(8,128)(2,1)S(1)}, bf16[32,4224]{1,0:T(8,128)(2,1)S(1)}) custom-call(bf16[32,4096]{1,0:T(8,128)(2,1)S(1)} %pad_maximum_fusion.2.refs_0_, bf16[32,4096]{1,0:T(8,128)(2,1)S(1)} %collective-permute-done.17.refs_1_, ...), custom_call_target="tpu_custom_call" | custom-call | tf_op jit(solution)/shard_map/pallas_call | solution.py:325
  81.0 3.4 %collective-permute-done.20 = bf16[32,4224]{1,0:T(8,128)(2,1)S(1)} collective-permute-done((bf16[32,4224]{1,0:T(8,128)(2,1)S(1)}, bf16[32,4224]{1,0:T(8,128)(2,1)S(1)}, u32[]{:S(2)}, u32[]{:S(2)}) %collective-permute-start.20) | collective-permute-done | bytes 270368 | tf_op jit(solution)/shard_map/ppermute | solution.py:35
  84.4 5.4 %collective-permute-done.21 = bf16[32,4224]{1,0:T(8,128)(2,1)S(1)} collective-permute-done((bf16[32,4224]{1,0:T(8,128)(2,1)S(1)}, bf16[32,4224]{1,0:T(8,128)(2,1)S(1)}, u32[]{:S(2)}, u32[]{:S(2)}) %collective-permute-start.21) | collective-permute-done | bytes 270368 | tf_op jit(solution)/shard_map/ppermute | solution.py:35
  90.1 3.5 %collective-permute-start.24 = (bf16[8,4224]{1,0:T(8,128)(2,1)S(1)}, bf16[8,4224]{1,0:T(8,128)(2,1)S(1)}, u32[]{:S(2)}, u32[]{:S(2)}) collective-permute-start(bf16[8,4224]{1,0:T(8,128)(2,1)S(1)} %get-tuple-element.229), channel_id=1, source_target_pairs={{0,4},{1,5},{2,6},{3,7},{4,0},{5,1},{6,2},{7,3},{8,12},{9,13},{10,... | collective-permute-start | bytes 202760 | tf_op jit(solution)/shard_map/ppermute | solution.py:35
  97.3 2.4 %collective-permute-done.25 = bf16[8,4224]{1,0:T(8,128)(2,1)S(1)} collective-permute-done((bf16[8,4224]{1,0:T(8,128)(2,1)S(1)}, bf16[8,4224]{1,0:T(8,128)(2,1)S(1)}, u32[]{:S(2)}, u32[]{:S(2)}) %collective-permute-start.25) | collective-permute-done | bytes 67616 | tf_op jit(solution)/shard_map/ppermute | solution.py:35
  102.0 3.4 %collective-permute-start.29 = (bf16[8,4096]{1,0:T(8,128)(2,1)S(1)}, bf16[8,4096]{1,0:T(8,128)(2,1)S(1)}, u32[]{:S(2)}, u32[]{:S(2)}) collective-permute-start(bf16[8,4096]{1,0:T(8,128)(2,1)S(1)} %divide_convert_fusion), channel_id=1, source_target_pairs={{0,4},{1,5},{2,6},{3,7},{4,0},{5,1},{6,2},{7,3},{8,12},{9,13},{10,... | collective-permute-start | bytes 196616 | tf_op jit(solution)/shard_map/ppermute | solution.py:35
  108.2 3.3 %collective-permute-done.30 = bf16[8,4096]{1,0:T(8,128)(2,1)S(1)} collective-permute-done((bf16[8,4096]{1,0:T(8,128)(2,1)S(1)}, bf16[8,4096]{1,0:T(8,128)(2,1)S(1)}, u32[]{:S(2)}, u32[]{:S(2)}) %collective-permute-start.30) | collective-permute-done | bytes 65568 | tf_op jit(solution)/shard_map/ppermute | solution.py:35
  116.3 7.5 %shard_map.142 = (bf16[64,1792]{1,0:T(8,128)(2,1)S(1)}, bf16[64,1792]{1,0:T(8,128)(2,1)S(1)}, bf16[64,2816]{1,0:T(8,128)(2,1)S(1)}, bf16[64,2816]{1,0:T(8,128)(2...) custom-call(s32[4]{0:T(128)S(1)} %iota_xor_fusion.order_ref, ...), custom_call_target="tpu_custom_call" | custom-call | tf_op jit(solution)/shard_map/pallas_call | solution.py:373
  123.8 1.7 %collective-permute-done.36.refs_3_ = bf16[64,1024]{1,0:T(8,128)(2,1)S(1)} collective-permute-done((bf16[64,1024]{1,0:T(8,128)(2,1)S(1)}, bf16[64,1024]{1,0:T(8,128)(2,1)S(1)}, u32[]{:S(2)}, u32[]{:S(2)}) %collective-permute-start.36) | collective-permute-done | bytes 131104 | tf_op jit(solution)/shard_map/ppermute | solution.py:35
  129.0 12.7 %shard_map.143 = (bf16[4,64,512]{2,1,0:T(8,128)(2,1)S(1)}, bf16[4,64,512]{2,1,0:T(8,128)(2,1)S(1)}) custom-call(s32[8]{0:T(128)S(1)} %fusion.40.order_ref, bf16[64,1792]{1,0:T(8,128)(2,1)S(1)} %get-tuple-element.188.gate_grad_ref, bf16[64,1792]{1,0:T(8,128)(2,1)S(1)} %get-tuple-element.189.up_grad_ref, bf16[4096,1792]{1,0:T(8,128)(2,1)} %gate_ref.7, ...), custom_call_target="tpu_custom_call" | custom-call | tf_op jit(solution)/shard_map/pallas_call | solution.py:419
  143.2 2.3 %shard_map.144 = bf16[1792,1024]{1,0:T(8,128)(2,1)} custom-call(bf16[64,2816]{1,0:T(8,128)(2,1)S(1)} %get-tuple-element.198.refs_0_.refs_4_, bf16[64,2816]{1,0:T(8,128)(2,1)S(1)} %collective-permute-done.37.refs_1_.refs_5_, bf16[64,2816]{1,0:T(8,128)(2,1)S(1)} %collective-permute-done.38.refs_2_.refs_6_, ...), custom_call_target="tpu_custom_call" | custom-call | tf_op jit(solution)/shard_map/pallas_call | solution.py:500
  145.7 3.4 %collective-permute-start.42 = (bf16[1,64,512]{2,1,0:T(8,128)(2,1)S(1)}, bf16[1,64,512]{2,1,0:T(8,128)(2,1)S(1)}, u32[]{:S(2)}, u32[]{:S(2)}) collective-permute-start(bf16[1,64,512]{2,1,0:T(8,128)(2,1)S(1)} %get-tuple-element.232), channel_id=1, source_target_pairs={{0,4},{1,5},{2,6},{3,7},{4,0},{5,1},{6,2},{7,3},{8,12},{9,13},{10,... | collective-permute-start | bytes 196616 | tf_op jit(solution)/shard_map/ppermute | solution.py:35
  150.6 3.7 %shard_map.145 = (bf16[1024,1792]{1,0:T(8,128)(2,1)}, bf16[1024,1792]{1,0:T(8,128)(2,1)}) custom-call(bf16[64,1024]{1,0:T(8,128)(2,1)S(1)} %get-tuple-element.208.refs_0_, bf16[64,1024]{1,0:T(8,128)(2,1)S(1)} %collective-permute-done.31.refs_1_, bf16[64,1024]{1,0:T(8,128)(2,1)S(1)} %collective-permute-done.32.refs_2_, ...), custom_call_target="tpu_custom_call" | custom-call | tf_op jit(solution)/shard_map/pallas_call | solution.py:461
  (155 shorter events, 55.2 us)
Async XLA Ops:
  2.3 9.3 %collective-permute-start = (bf16[1,72,512]{2,1,0:T(8,128)(2,1)S(1)}, bf16[1,72,512]{2,1,0:T(8,128)(2,1)S(1)}, u32[]{:S(2)}, u32[]{:S(2)}) collective-permute-start(bf16[1,72,512]{2,1,0:T(8,128)(2,1)S(1)} %maximum_bitcast_fusion.x_ref), channel_id=1, source_target_pairs={{0,2},{1,3},{2,0},{3,1},{4,6},{5,7},{6,4},{7,5},{8,10},{9,11},{10,... | collective-permute-start | bytes 221192 | tf_op jit(solution)/shard_map/ppermute | solution.py:35
  5.3 7.8 %collective-permute-start.1 = (bf16[1,72,512]{2,1,0:T(8,128)(2,1)S(1)}, bf16[1,72,512]{2,1,0:T(8,128)(2,1)S(1)}, u32[]{:S(2)}, u32[]{:S(2)}) collective-permute-start(bf16[1,72,512]{2,1,0:T(8,128)(2,1)S(1)} %maximum_bitcast_fusion.x_ref), channel_id=1, source_target_pairs={{0,4},{1,5},{2,6},{3,7},{4,0},{5,1},{6,2},{7,3},{8,12},{9,13},{10,... | collective-permute-start | bytes 221192 | tf_op jit(solution)/shard_map/ppermute | solution.py:35
  14.2 7.5 %collective-permute-start.3 = (bf16[4,72,512]{2,1,0:T(8,128)(2,1)S(1)}, bf16[4,72,512]{2,1,0:T(8,128)(2,1)S(1)}, u32[]{:S(2)}, u32[]{:S(2)}) collective-permute-start(bf16[4,72,512]{2,1,0:T(8,128)(2,1)S(1)} %pad_maximum_fusion.1.x_ref.first_ref), channel_id=1, source_target_pairs={{0,1},{1,0},{2,3},{3,2},{4,5},{5,4},{6,7},{7,6},{8,9},{9,8},{10,11... | collective-permute-start | bytes 884744 | tf_op jit(solution)/shard_map/ppermute | solution.py:35
  21.7 11.2 %collective-permute-start.5 = (bf16[512,4096]{1,0:T(8,128)(2,1)S(1)}, bf16[512,4096]{1,0:T(8,128)(2,1)S(1)}, u32[]{:S(2)}, u32[]{:S(2)}) collective-permute-start(bf16[512,4096]{1,0:T(8,128)(2,1)S(1)} %copy-done), channel_id=1, source_target_pairs={{0,1},{1,0},{2,3},{3,2},{4,5},{5,4},{6,7},{7,6},{8,9},{9,8},{10,11... | collective-permute-start | bytes 12582920 | tf_op jit(solution)/shard_map/ppermute | solution.py:35
  34.6 10.9 %collective-permute-start.10 = (bf16[72,1792]{1,0:T(8,128)(2,1)S(1)}, bf16[72,1792]{1,0:T(8,128)(2,1)S(1)}, u32[]{:S(2)}, u32[]{:S(2)}) collective-permute-start(bf16[72,1792]{1,0:T(8,128)(2,1)S(1)} %get-tuple-element.165.gate_ref.refs_4_.refs_8_), channel_id=1, source_target_pairs={{0,8},{8,0},{16,24},{24,16},{1,9},{9,1},{17,25},{25,17},{2,10},{10... | collective-permute-start | bytes 774152 | tf_op jit(solution)/shard_map/ppermute | solution.py:35
  36.2 7.6 %collective-permute-start.7 = (bf16[8,4096]{1,0:T(8,128)(2,1)S(1)}, bf16[8,4096]{1,0:T(8,128)(2,1)S(1)}, u32[]{:S(2)}, u32[]{:S(2)}) collective-permute-start(bf16[8,4096]{1,0:T(8,128)(2,1)S(1)} %get-tuple-element.233), channel_id=1, source_target_pairs={{0,2},{1,3},{2,0},{3,1},{4,6},{5,7},{6,4},{7,5},{8,10},{9,11},{10,... | collective-permute-start | bytes 196616 | tf_op jit(solution)/shard_map/ppermute | solution.py:35
  37.3 8.1 %collective-permute-start.8 = (bf16[8,4096]{1,0:T(8,128)(2,1)S(1)}, bf16[8,4096]{1,0:T(8,128)(2,1)S(1)}, u32[]{:S(2)}, u32[]{:S(2)}) collective-permute-start(bf16[8,4096]{1,0:T(8,128)(2,1)S(1)} %get-tuple-element.235), channel_id=1, source_target_pairs={{0,4},{1,5},{2,6},{3,7},{4,0},{5,1},{6,2},{7,3},{8,12},{9,13},{10,... | collective-permute-start | bytes 196616 | tf_op jit(solution)/shard_map/ppermute | solution.py:35
  40.6 7.3 %collective-permute-start.11 = (bf16[72,1792]{1,0:T(8,128)(2,1)S(1)}, bf16[72,1792]{1,0:T(8,128)(2,1)S(1)}, u32[]{:S(2)}, u32[]{:S(2)}) collective-permute-start(bf16[72,1792]{1,0:T(8,128)(2,1)S(1)} %get-tuple-element.166.up_ref.refs_8_.refs_12_), channel_id=1, source_target_pairs={{0,16},{8,24},{16,0},{24,8},{1,17},{9,25},{17,1},{25,9},{2,18},{10... | collective-permute-start | bytes 774152 | tf_op jit(solution)/shard_map/ppermute | solution.py:35
  57.7 9.8 %collective-permute-start.17 = (bf16[32,4096]{1,0:T(8,128)(2,1)S(1)}, bf16[32,4096]{1,0:T(8,128)(2,1)S(1)}, u32[]{:S(2)}, u32[]{:S(2)}) collective-permute-start(bf16[32,4096]{1,0:T(8,128)(2,1)S(1)} %pad_maximum_fusion.2.refs_0_), channel_id=1, source_target_pairs={{0,8},{8,0},{16,24},{24,16},{1,9},{9,1},{17,25},{25,17},{2,10},{10... | collective-permute-start | bytes 786440 | tf_op jit(solution)/shard_map/ppermute | solution.py:35
  58.3 11.9 %collective-permute-start.18 = (bf16[32,4096]{1,0:T(8,128)(2,1)S(1)}, bf16[32,4096]{1,0:T(8,128)(2,1)S(1)}, u32[]{:S(2)}, u32[]{:S(2)}) collective-permute-start(bf16[32,4096]{1,0:T(8,128)(2,1)S(1)} %pad_maximum_fusion.2.refs_0_), channel_id=1, source_target_pairs={{0,16},{8,24},{16,0},{24,8},{1,17},{9,25},{17,1},{25,9},{2,18},{10... | collective-permute-start | bytes 786440 | tf_op jit(solution)/shard_map/ppermute | solution.py:35
  59.9 10.4 %collective-permute-start.19 = (bf16[32,4096]{1,0:T(8,128)(2,1)S(1)}, bf16[32,4096]{1,0:T(8,128)(2,1)S(1)}, u32[]{:S(2)}, u32[]{:S(2)}) collective-permute-start(bf16[32,4096]{1,0:T(8,128)(2,1)S(1)} %pad_maximum_fusion.2.refs_0_), channel_id=1, source_target_pairs={{0,24},{8,16},{16,8},{24,0},{1,25},{9,17},{17,9},{25,1},{2,26},{10... | collective-permute-start | bytes 786440 | tf_op jit(solution)/shard_map/ppermute | solution.py:35
  77.2 7.2 %collective-permute-start.20 = (bf16[32,4224]{1,0:T(8,128)(2,1)S(1)}, bf16[32,4224]{1,0:T(8,128)(2,1)S(1)}, u32[]{:S(2)}, u32[]{:S(2)}) collective-permute-start(bf16[32,4224]{1,0:T(8,128)(2,1)S(1)} %get-tuple-element.161), channel_id=1, source_target_pairs={{0,8},{8,0},{16,24},{24,16},{1,9},{9,1},{17,25},{25,17},{2,10},{10... | collective-permute-start | bytes 811016 | tf_op jit(solution)/shard_map/ppermute | solution.py:35
  78.8 11.0 %collective-permute-start.21 = (bf16[32,4224]{1,0:T(8,128)(2,1)S(1)}, bf16[32,4224]{1,0:T(8,128)(2,1)S(1)}, u32[]{:S(2)}, u32[]{:S(2)}) collective-permute-start(bf16[32,4224]{1,0:T(8,128)(2,1)S(1)} %get-tuple-element.162), channel_id=1, source_target_pairs={{0,16},{8,24},{16,0},{24,8},{1,17},{9,25},{17,1},{25,9},{2,18},{10... | collective-permute-start | bytes 811016 | tf_op jit(solution)/shard_map/ppermute | solution.py:35
  79.8 10.0 %collective-permute-start.22 = (bf16[32,4224]{1,0:T(8,128)(2,1)S(1)}, bf16[32,4224]{1,0:T(8,128)(2,1)S(1)}, u32[]{:S(2)}, u32[]{:S(2)}) collective-permute-start(bf16[32,4224]{1,0:T(8,128)(2,1)S(1)} %get-tuple-element.163), channel_id=1, source_target_pairs={{0,24},{8,16},{16,8},{24,0},{1,25},{9,17},{17,9},{25,1},{2,26},{10... | collective-permute-start | bytes 811016 | tf_op jit(solution)/shard_map/ppermute | solution.py:35
  90.0 7.3 %collective-permute-start.23 = (bf16[8,4224]{1,0:T(8,128)(2,1)S(1)}, bf16[8,4224]{1,0:T(8,128)(2,1)S(1)}, u32[]{:S(2)}, u32[]{:S(2)}) collective-permute-start(bf16[8,4224]{1,0:T(8,128)(2,1)S(1)} %get-tuple-element.227), channel_id=1, source_target_pairs={{0,2},{1,3},{2,0},{3,1},{4,6},{5,7},{6,4},{7,5},{8,10},{9,11},{10,... | collective-permute-start | bytes 202760 | tf_op jit(solution)/shard_map/ppermute | solution.py:35
  90.1 7.2 %collective-permute-start.24 = (bf16[8,4224]{1,0:T(8,128)(2,1)S(1)}, bf16[8,4224]{1,0:T(8,128)(2,1)S(1)}, u32[]{:S(2)}, u32[]{:S(2)}) collective-permute-start(bf16[8,4224]{1,0:T(8,128)(2,1)S(1)} %get-tuple-element.229), channel_id=1, source_target_pairs={{0,4},{1,5},{2,6},{3,7},{4,0},{5,1},{6,2},{7,3},{8,12},{9,13},{10,... | collective-permute-start | bytes 202760 | tf_op jit(solution)/shard_map/ppermute | solution.py:35
  112.8 12.6 %collective-permute-start.34 = (bf16[72,1792]{1,0:T(8,128)(2,1)S(1)}, bf16[72,1792]{1,0:T(8,128)(2,1)S(1)}, u32[]{:S(2)}, u32[]{:S(2)}) collective-permute-start(bf16[72,1792]{1,0:T(8,128)(2,1)S(1)} %collective-permute-done.10.refs_5_.refs_9_), channel_id=1, source_target_pairs={{0,16},{8,24},{16,0},{24,8},{1,17},{9,25},{17,1},{25,9},{2,18},{10... | collective-permute-start | bytes 774152 | tf_op jit(solution)/shard_map/ppermute | solution.py:35
  113.2 12.3 %collective-permute-start.35 = (bf16[72,1792]{1,0:T(8,128)(2,1)S(1)}, bf16[72,1792]{1,0:T(8,128)(2,1)S(1)}, u32[]{:S(2)}, u32[]{:S(2)}) collective-permute-start(bf16[72,1792]{1,0:T(8,128)(2,1)S(1)} %collective-permute-done.11.refs_10_.refs_14_), channel_id=1, source_target_pairs={{0,8},{8,0},{16,24},{24,16},{1,9},{9,1},{17,25},{25,17},{2,10},{10... | collective-permute-start | bytes 774152 | tf_op jit(solution)/shard_map/ppermute | solution.py:35
  114.8 10.6 %collective-permute-start.36 = (bf16[64,1024]{1,0:T(8,128)(2,1)S(1)}, bf16[64,1024]{1,0:T(8,128)(2,1)S(1)}, u32[]{:S(2)}, u32[]{:S(2)}) collective-permute-start(bf16[64,1024]{1,0:T(8,128)(2,1)S(1)} %get-tuple-element.183), channel_id=1, source_target_pairs={{0,24},{8,16},{16,8},{24,0},{1,25},{9,17},{17,9},{25,1},{2,26},{10... | collective-permute-start | bytes 393224 | tf_op jit(solution)/shard_map/ppermute | solution.py:35
  125.5 16.2 %collective-permute-start.37 = (bf16[64,2816]{1,0:T(8,128)(2,1)S(1)}, bf16[64,2816]{1,0:T(8,128)(2,1)S(1)}, u32[]{:S(2)}, u32[]{:S(2)}) collective-permute-start(bf16[64,2816]{1,0:T(8,128)(2,1)S(1)} %get-tuple-element.193), channel_id=1, source_target_pairs={{0,8},{8,0},{16,24},{24,16},{1,9},{9,1},{17,25},{25,17},{2,10},{10... | collective-permute-start | bytes 1081352 | tf_op jit(solution)/shard_map/ppermute | solution.py:35
  126.0 17.2 %collective-permute-start.38 = (bf16[64,2816]{1,0:T(8,128)(2,1)S(1)}, bf16[64,2816]{1,0:T(8,128)(2,1)S(1)}, u32[]{:S(2)}, u32[]{:S(2)}) collective-permute-start(bf16[64,2816]{1,0:T(8,128)(2,1)S(1)} %get-tuple-element.194), channel_id=1, source_target_pairs={{0,16},{8,24},{16,0},{24,8},{1,17},{9,25},{17,1},{25,9},{2,18},{10... | collective-permute-start | bytes 1081352 | tf_op jit(solution)/shard_map/ppermute | solution.py:35
  127.5 15.7 %collective-permute-start.39 = (bf16[64,2816]{1,0:T(8,128)(2,1)S(1)}, bf16[64,2816]{1,0:T(8,128)(2,1)S(1)}, u32[]{:S(2)}, u32[]{:S(2)}) collective-permute-start(bf16[64,2816]{1,0:T(8,128)(2,1)S(1)} %get-tuple-element.195), channel_id=1, source_target_pairs={{0,24},{8,16},{16,8},{24,0},{1,25},{9,17},{17,9},{25,1},{2,26},{10... | collective-permute-start | bytes 1081352 | tf_op jit(solution)/shard_map/ppermute | solution.py:35
  145.6 8.7 %collective-permute-start.41 = (bf16[1,64,512]{2,1,0:T(8,128)(2,1)S(1)}, bf16[1,64,512]{2,1,0:T(8,128)(2,1)S(1)}, u32[]{:S(2)}, u32[]{:S(2)}) collective-permute-start(bf16[1,64,512]{2,1,0:T(8,128)(2,1)S(1)} %get-tuple-element.230), channel_id=1, source_target_pairs={{0,2},{1,3},{2,0},{3,1},{4,6},{5,7},{6,4},{7,5},{8,10},{9,11},{10,... | collective-permute-start | bytes 196616 | tf_op jit(solution)/shard_map/ppermute | solution.py:35
  145.7 8.6 %collective-permute-start.42 = (bf16[1,64,512]{2,1,0:T(8,128)(2,1)S(1)}, bf16[1,64,512]{2,1,0:T(8,128)(2,1)S(1)}, u32[]{:S(2)}, u32[]{:S(2)}) collective-permute-start(bf16[1,64,512]{2,1,0:T(8,128)(2,1)S(1)} %get-tuple-element.232), channel_id=1, source_target_pairs={{0,4},{1,5},{2,6},{3,7},{4,0},{5,1},{6,2},{7,3},{8,12},{9,13},{10,... | collective-permute-start | bytes 196616 | tf_op jit(solution)/shard_map/ppermute | solution.py:35
  (26 other events, 170.5 us)

commit v7 on v6

--- a/solution.py
+++ b/solution.py
@@ -94,7 +94,7 @@
     slot_cap = row_table.shape[1]
     slot = lax.broadcasted_iota(jnp.int32, (1, 1, 1, slot_cap), 3) + shard[:, None, None, None] * slot_cap
     asked = jnp.sum((slots[..., None] == slot).astype(jnp.float32), axis=2)
-    live = lax.broadcasted_iota(jnp.int32, (devices, 1, slot_cap), 2) < count_table[:, None, None]
+    live = lax.broadcasted_iota(jnp.int32, (devices, 1, slot_cap), 2) < count_table[:, :, None]
     used = jnp.where(live, asked, 0.0)
     dead = jnp.sum(asked - used, axis=-1).reshape(devices * queries)
     row = lax.broadcasted_iota(jnp.int32, (1, 1, shard_rows), 2)
@@ -585,25 +585,28 @@
     branch = add_up([own_part, received]).astype(jnp.bfloat16)
 
     tables = jnp.take(tables, asker, axis=1)
-    top_state, gate_near, up_far, own_norm, span_later, other_index, tables = together(
+    row_tables, count_tables = tables[..., :-1], tables[..., -1:]
+    top_state, gate_near, up_far, own_norm, span_later, other_index, row_tables, count_tables = together(
         sum_chips(branch) + residual_in.astype(jnp.float32),
         swap(gate_act, "dp", near),
         swap(up_act, "dp", far),
         norm_of(span_later.astype(jnp.float32)),
         span_later,
         other_index,
-        tables,
+        row_tables,
+        count_tables,
     )
     row_norm = norm_of(top_state)
     unit_rows = top_state / row_norm[:, None]
 
-    states, last_slots, other_norm, span_later, other_index, tables, positive_keys, both = together(
+    states, last_slots, other_norm, span_later, other_index, row_tables, count_tables, positive_keys, both = together(
         gather_chips(top_state.astype(jnp.bfloat16)),
         swap(gate_near[group_rows:], "dp", far),
         swap_core(own_norm),
         span_later,
         other_index,
-        tables,
+        row_tables,
+        count_tables,
         positive_keys,
         both,
     )
@@ -624,8 +627,8 @@
     for k in range(2):
         shard_counts, shard_dead = use_counts(
             slots,
-            tables[k, :, :-1],
-            tables[k, :, -1],
+            row_tables[k],
+            count_tables[k],
             both[k : k + 1],
             span_index.shape[0],
         )

time: 156 us -> 155 us (level)
  transfers between devices with their start and end apart: 44 -> 44, of which waited for: 19 -> 19; matrix products, arithmetic and copies ran while one was open for 5% -> 6% of each run, Pallas kernels for 30% -> 30%
where the time goes in v7:
time: 155 us
  Pallas kernels  53.7 us (35%)
  starting transfers between devices  51.5 us (33%)
  waiting for transfers between devices  35.2 us (23%)
  other arithmetic  8.28 us (5%)
  between operations  2.5 us (2%)
  local copies, waits for them, and re-layouts  2.41 us (2%)
    ppermute x44, starting transfers between devices, swap(): return lax.ppermute(x, axis, pairs)  51.5 us
    ppermute x44, waiting for transfers between devices, swap(): return lax.ppermute(x, axis, pairs)  35.2 us
    pallas_call x1, Pallas kernels, backward_input(): kernel_call(body, [in_smem, in_vmem, in_vmem, in_hbm, in_hbm], [shape_of(...  12.7 us
    pallas_call x1, Pallas kernels, forward_rest(): kernel_call(body, [in_smem] + [in_vmem] * 3 + [in_hbm] * 3 + [in_vmem] *...  10.9 us
    pallas_call x2, Pallas kernels, forward_part(): kernel_call(body, [in_smem, in_vmem, in_hbm, in_hbm] + [in_vmem] * begun,...  9.18 us
    pallas_call x1, Pallas kernels, backward_hidden(): kernel_call(body, [in_smem, in_vmem, in_vmem, in_hbm, in_vmem, in_vmem, i...  7.45 us
    pallas_call x1, Pallas kernels, score_kernel(): kernel_call(body, [in_vmem] * pieces + [in_hbm] * 2 + [in_vmem] * 3, [sha...  6.85 us
    pallas_call x1, Pallas kernels, weight_grads(): pl.pallas_call(body, in_specs=[in_vmem] * (4 * groups), out_specs=[pl.Blo...  3.72 us
  transfers between devices with their start and end apart: 44, of which 19 were waited for; matrix products, arithmetic and copies ran while one was open for 6% of the time, Pallas kernels for 30%

profile of v7, /device:TPU:0, one launch (start us, length us, event | category | flops | bytes accessed | tf_op | source)
XLA Modules:
  0.0 155.0 jit_solution(5114298804121361675)
XLA Ops:
  2.3 3.0 %collective-permute-start = (bf16[1,72,512]{2,1,0:T(8,128)(2,1)S(1)}, bf16[1,72,512]{2,1,0:T(8,128)(2,1)S(1)}, u32[]{:S(2)}, u32[]{:S(2)}) collective-permute-start(bf16[1,72,512]{2,1,0:T(8,128)(2,1)S(1)} %maximum_bitcast_fusion.x_ref), channel_id=1, source_target_pairs={{0,2},{1,3},{2,0},{3,1},{4,6},{5,7},{6,4},{7,5},{8,10},{9,11},{10,... | collective-permute-start | bytes 221192 | tf_op jit(solution)/shard_map/ppermute | solution.py:35
  5.3 2.6 %collective-permute-start.1 = (bf16[1,72,512]{2,1,0:T(8,128)(2,1)S(1)}, bf16[1,72,512]{2,1,0:T(8,128)(2,1)S(1)}, u32[]{:S(2)}, u32[]{:S(2)}) collective-permute-start(bf16[1,72,512]{2,1,0:T(8,128)(2,1)S(1)} %maximum_bitcast_fusion.x_ref), channel_id=1, source_target_pairs={{0,4},{1,5},{2,6},{3,7},{4,0},{5,1},{6,2},{7,3},{8,12},{9,13},{10,... | collective-permute-start | bytes 221192 | tf_op jit(solution)/shard_map/ppermute | solution.py:35
  8.2 3.4 %shard_map.137 = (f32[64,1792]{1,0:T(8,128)S(1)}, f32[64,1792]{1,0:T(8,128)S(1)}) custom-call(s32[8]{0:T(128)S(1)} %fusion.40.order_ref, bf16[1,72,512]{2,1,0:T(8,128)(2,1)S(1)} %maximum_bitcast_fusion.x_ref, bf16[4096,1792]{1,0:T(8,128)(2,1)} %gate_ref.7, bf16[4096,1792]{1,0:T(8,128)(2,1)} %up_ref.7), custom_call_target="tpu_custom_call" | custom-call | tf_op jit(solution)/shard_map/pallas_call | solution.py:188
  15.9 5.8 %shard_map.138 = (f32[64,1792]{1,0:T(8,128)S(1)}, f32[64,1792]{1,0:T(8,128)S(1)}) custom-call(s32[8]{0:T(128)S(1)} %fusion.40.order_ref, bf16[4,72,512]{2,1,0:T(8,128)(2,1)S(1)} %pad_maximum_fusion.1.x_ref.first_ref, bf16[4096,1792]{1,0:T(8,128)(2,1)} %gate_ref.7, bf16[4096,1792]{1,0:T(8,128)(2,1)} %up_ref.7, f32[64,1792]{1,0:T(8,128)S(1)} %get-tuple-element.116.refs_0_, ...), custom_call_target="tpu_custom_call" | custom-call | tf_op jit(solution)/shard_map/pallas_call | solution.py:188
  22.1 10.9 %shard_map.139 = (bf16[72,1792]{1,0:T(8,128)(2,1)S(1)}, bf16[72,1792]{1,0:T(8,128)(2,1)S(1)}, bf16[32,4096]{1,0:T(8,128)(2,1)S(1)}, bf16[32,4096]{1,0:T(8,128)(2,1)S(1)}) custom-call(s32[8]{0:T(128)S(1)} %fusion.40.order_ref, bf16[4,72,512]{2,1,0:T(8,128)(2,1)S(1)} %collective-permute-done.3.x_ref.second_ref, f32[64,1792]{1,0:T(8,128)S(1)} %get-tuple-element.121.gate_in, ...), custom_call_target="tpu_custom_call" | custom-call | tf_op jit(solution)/shard_map/pallas_call | solution.py:239
  37.3 1.7 %collective-permute-start.8 = (bf16[8,4096]{1,0:T(8,128)(2,1)S(1)}, bf16[8,4096]{1,0:T(8,128)(2,1)S(1)}, u32[]{:S(2)}, u32[]{:S(2)}) collective-permute-start(bf16[8,4096]{1,0:T(8,128)(2,1)S(1)} %get-tuple-element.239), channel_id=1, source_target_pairs={{0,4},{1,5},{2,6},{3,7},{4,0},{5,1},{6,2},{7,3},{8,12},{9,13},{10,... | collective-permute-start | bytes 196616 | tf_op jit(solution)/shard_map/ppermute | solution.py:35
  45.5 2.4 %collective-permute-done.11.refs_10_.refs_14_ = bf16[72,1792]{1,0:T(8,128)(2,1)S(1)} collective-permute-done((bf16[72,1792]{1,0:T(8,128)(2,1)S(1)}, bf16[72,1792]{1,0:T(8,128)(2,1)S(1)}, u32[]{:S(2)}, u32[]{:S(2)}) %collective-permute-start.11) | collective-permute-done | bytes 258080 | tf_op jit(solution)/shard_map/ppermute | solution.py:35
  48.3 2.6 %collective-permute-start.13 = (bf16[8,4096]{1,0:T(8,128)(2,1)S(1)}, bf16[8,4096]{1,0:T(8,128)(2,1)S(1)}, u32[]{:S(2)}, u32[]{:S(2)}) collective-permute-start(bf16[8,4096]{1,0:T(8,128)(2,1)S(1)} %get-tuple-element.243), channel_id=1, source_target_pairs={{0,4},{1,5},{2,6},{3,7},{4,0},{5,1},{6,2},{7,3},{8,12},{9,13},{10,... | collective-permute-start | bytes 196616 | tf_op jit(solution)/shard_map/ppermute | solution.py:35
  54.8 2.1 %collective-permute-done.14 = bf16[8,4096]{1,0:T(8,128)(2,1)S(1)} collective-permute-done((bf16[8,4096]{1,0:T(8,128)(2,1)S(1)}, bf16[8,4096]{1,0:T(8,128)(2,1)S(1)}, u32[]{:S(2)}, u32[]{:S(2)}) %collective-permute-start.14) | collective-permute-done | bytes 65568 | tf_op jit(solution)/shard_map/ppermute | solution.py:35
  67.5 1.9 %collective-permute-done.18.refs_2_ = bf16[32,4096]{1,0:T(8,128)(2,1)S(1)} collective-permute-done((bf16[32,4096]{1,0:T(8,128)(2,1)S(1)}, bf16[32,4096]{1,0:T(8,128)(2,1)S(1)}, u32[]{:S(2)}, u32[]{:S(2)}) %collective-permute-start.18) | collective-permute-done | bytes 262176 | tf_op jit(solution)/shard_map/ppermute | solution.py:35
  69.5 6.9 %shard_map.140 = (bf16[32,4224]{1,0:T(8,128)(2,1)S(1)}, bf16[32,4224]{1,0:T(8,128)(2,1)S(1)}, bf16[32,4224]{1,0:T(8,128)(2,1)S(1)}, bf16[32,4224]{1,0:T(8,128)(2,1)S(1)}) custom-call(bf16[32,4096]{1,0:T(8,128)(2,1)S(1)} %pad_maximum_fusion.2.refs_0_, bf16[32,4096]{1,0:T(8,128)(2,1)S(1)} %collective-permute-done.17.refs_1_, ...), custom_call_target="tpu_custom_call" | custom-call | tf_op jit(solution)/shard_map/pallas_call | solution.py:325
  80.2 3.4 %collective-permute-done.20 = bf16[32,4224]{1,0:T(8,128)(2,1)S(1)} collective-permute-done((bf16[32,4224]{1,0:T(8,128)(2,1)S(1)}, bf16[32,4224]{1,0:T(8,128)(2,1)S(1)}, u32[]{:S(2)}, u32[]{:S(2)}) %collective-permute-start.20) | collective-permute-done | bytes 270368 | tf_op jit(solution)/shard_map/ppermute | solution.py:35
  83.6 5.4 %collective-permute-done.21 = bf16[32,4224]{1,0:T(8,128)(2,1)S(1)} collective-permute-done((bf16[32,4224]{1,0:T(8,128)(2,1)S(1)}, bf16[32,4224]{1,0:T(8,128)(2,1)S(1)}, u32[]{:S(2)}, u32[]{:S(2)}) %collective-permute-start.21) | collective-permute-done | bytes 270368 | tf_op jit(solution)/shard_map/ppermute | solution.py:35
  89.2 3.5 %collective-permute-start.24 = (bf16[8,4224]{1,0:T(8,128)(2,1)S(1)}, bf16[8,4224]{1,0:T(8,128)(2,1)S(1)}, u32[]{:S(2)}, u32[]{:S(2)}) collective-permute-start(bf16[8,4224]{1,0:T(8,128)(2,1)S(1)} %get-tuple-element.233), channel_id=1, source_target_pairs={{0,4},{1,5},{2,6},{3,7},{4,0},{5,1},{6,2},{7,3},{8,12},{9,13},{10,... | collective-permute-start | bytes 202760 | tf_op jit(solution)/shard_map/ppermute | solution.py:35
  96.4 2.4 %collective-permute-done.25 = bf16[8,4224]{1,0:T(8,128)(2,1)S(1)} collective-permute-done((bf16[8,4224]{1,0:T(8,128)(2,1)S(1)}, bf16[8,4224]{1,0:T(8,128)(2,1)S(1)}, u32[]{:S(2)}, u32[]{:S(2)}) %collective-permute-start.25) | collective-permute-done | bytes 67616 | tf_op jit(solution)/shard_map/ppermute | solution.py:35
  101.1 3.4 %collective-permute-start.29 = (bf16[8,4096]{1,0:T(8,128)(2,1)S(1)}, bf16[8,4096]{1,0:T(8,128)(2,1)S(1)}, u32[]{:S(2)}, u32[]{:S(2)}) collective-permute-start(bf16[8,4096]{1,0:T(8,128)(2,1)S(1)} %divide_convert_fusion), channel_id=1, source_target_pairs={{0,4},{1,5},{2,6},{3,7},{4,0},{5,1},{6,2},{7,3},{8,12},{9,13},{10,... | collective-permute-start | bytes 196616 | tf_op jit(solution)/shard_map/ppermute | solution.py:35
  107.3 3.3 %collective-permute-done.30 = bf16[8,4096]{1,0:T(8,128)(2,1)S(1)} collective-permute-done((bf16[8,4096]{1,0:T(8,128)(2,1)S(1)}, bf16[8,4096]{1,0:T(8,128)(2,1)S(1)}, u32[]{:S(2)}, u32[]{:S(2)}) %collective-permute-start.30) | collective-permute-done | bytes 65568 | tf_op jit(solution)/shard_map/ppermute | solution.py:35
  112.3 1.6 %collective-permute-start.35 = (bf16[72,1792]{1,0:T(8,128)(2,1)S(1)}, bf16[72,1792]{1,0:T(8,128)(2,1)S(1)}, u32[]{:S(2)}, u32[]{:S(2)}) collective-permute-start(bf16[72,1792]{1,0:T(8,128)(2,1)S(1)} %collective-permute-done.11.refs_10_.refs_14_), channel_id=1, source_target_pairs={{0,8},{8,0},{16,24},{24,16},{1,9},{9,1},{17,25},{25,17},{2,10},{10... | collective-permute-start | bytes 774152 | tf_op jit(solution)/shard_map/ppermute | solution.py:35
  115.4 7.5 %shard_map.142 = (bf16[64,1792]{1,0:T(8,128)(2,1)S(1)}, bf16[64,1792]{1,0:T(8,128)(2,1)S(1)}, bf16[64,2816]{1,0:T(8,128)(2,1)S(1)}, bf16[64,2816]{1,0:T(8,128)(2...) custom-call(s32[4]{0:T(128)S(1)} %iota_xor_fusion.order_ref, ...), custom_call_target="tpu_custom_call" | custom-call | tf_op jit(solution)/shard_map/pallas_call | solution.py:373
  122.9 1.7 %collective-permute-done.36.refs_3_ = bf16[64,1024]{1,0:T(8,128)(2,1)S(1)} collective-permute-done((bf16[64,1024]{1,0:T(8,128)(2,1)S(1)}, bf16[64,1024]{1,0:T(8,128)(2,1)S(1)}, u32[]{:S(2)}, u32[]{:S(2)}) %collective-permute-start.36) | collective-permute-done | bytes 131104 | tf_op jit(solution)/shard_map/ppermute | solution.py:35
  128.1 12.7 %shard_map.143 = (bf16[4,64,512]{2,1,0:T(8,128)(2,1)S(1)}, bf16[4,64,512]{2,1,0:T(8,128)(2,1)S(1)}) custom-call(s32[8]{0:T(128)S(1)} %fusion.40.order_ref, bf16[64,1792]{1,0:T(8,128)(2,1)S(1)} %get-tuple-element.192.gate_grad_ref, bf16[64,1792]{1,0:T(8,128)(2,1)S(1)} %get-tuple-element.193.up_grad_ref, bf16[4096,1792]{1,0:T(8,128)(2,1)} %gate_ref.7, ...), custom_call_target="tpu_custom_call" | custom-call | tf_op jit(solution)/shard_map/pallas_call | solution.py:419
  142.3 2.3 %shard_map.144 = bf16[1792,1024]{1,0:T(8,128)(2,1)} custom-call(bf16[64,2816]{1,0:T(8,128)(2,1)S(1)} %get-tuple-element.202.refs_0_.refs_4_, bf16[64,2816]{1,0:T(8,128)(2,1)S(1)} %collective-permute-done.37.refs_1_.refs_5_, bf16[64,2816]{1,0:T(8,128)(2,1)S(1)} %collective-permute-done.38.refs_2_.refs_6_, ...), custom_call_target="tpu_custom_call" | custom-call | tf_op jit(solution)/shard_map/pallas_call | solution.py:500
  144.8 3.4 %collective-permute-start.42 = (bf16[1,64,512]{2,1,0:T(8,128)(2,1)S(1)}, bf16[1,64,512]{2,1,0:T(8,128)(2,1)S(1)}, u32[]{:S(2)}, u32[]{:S(2)}) collective-permute-start(bf16[1,64,512]{2,1,0:T(8,128)(2,1)S(1)} %get-tuple-element.236), channel_id=1, source_target_pairs={{0,4},{1,5},{2,6},{3,7},{4,0},{5,1},{6,2},{7,3},{8,12},{9,13},{10,... | collective-permute-start | bytes 196616 | tf_op jit(solution)/shard_map/ppermute | solution.py:35
  149.7 3.7 %shard_map.145 = (bf16[1024,1792]{1,0:T(8,128)(2,1)}, bf16[1024,1792]{1,0:T(8,128)(2,1)}) custom-call(bf16[64,1024]{1,0:T(8,128)(2,1)S(1)} %get-tuple-element.212.refs_0_, bf16[64,1024]{1,0:T(8,128)(2,1)S(1)} %collective-permute-done.31.refs_1_, bf16[64,1024]{1,0:T(8,128)(2,1)S(1)} %collective-permute-done.32.refs_2_, ...), custom_call_target="tpu_custom_call" | custom-call | tf_op jit(solution)/shard_map/pallas_call | solution.py:461
  (156 shorter events, 55.1 us)
Async XLA Ops:
  2.3 9.3 %collective-permute-start = (bf16[1,72,512]{2,1,0:T(8,128)(2,1)S(1)}, bf16[1,72,512]{2,1,0:T(8,128)(2,1)S(1)}, u32[]{:S(2)}, u32[]{:S(2)}) collective-permute-start(bf16[1,72,512]{2,1,0:T(8,128)(2,1)S(1)} %maximum_bitcast_fusion.x_ref), channel_id=1, source_target_pairs={{0,2},{1,3},{2,0},{3,1},{4,6},{5,7},{6,4},{7,5},{8,10},{9,11},{10,... | collective-permute-start | bytes 221192 | tf_op jit(solution)/shard_map/ppermute | solution.py:35
  5.3 7.8 %collective-permute-start.1 = (bf16[1,72,512]{2,1,0:T(8,128)(2,1)S(1)}, bf16[1,72,512]{2,1,0:T(8,128)(2,1)S(1)}, u32[]{:S(2)}, u32[]{:S(2)}) collective-permute-start(bf16[1,72,512]{2,1,0:T(8,128)(2,1)S(1)} %maximum_bitcast_fusion.x_ref), channel_id=1, source_target_pairs={{0,4},{1,5},{2,6},{3,7},{4,0},{5,1},{6,2},{7,3},{8,12},{9,13},{10,... | collective-permute-start | bytes 221192 | tf_op jit(solution)/shard_map/ppermute | solution.py:35
  14.2 7.5 %collective-permute-start.3 = (bf16[4,72,512]{2,1,0:T(8,128)(2,1)S(1)}, bf16[4,72,512]{2,1,0:T(8,128)(2,1)S(1)}, u32[]{:S(2)}, u32[]{:S(2)}) collective-permute-start(bf16[4,72,512]{2,1,0:T(8,128)(2,1)S(1)} %pad_maximum_fusion.1.x_ref.first_ref), channel_id=1, source_target_pairs={{0,1},{1,0},{2,3},{3,2},{4,5},{5,4},{6,7},{7,6},{8,9},{9,8},{10,11... | collective-permute-start | bytes 884744 | tf_op jit(solution)/shard_map/ppermute | solution.py:35
  21.7 11.2 %collective-permute-start.5 = (bf16[512,4096]{1,0:T(8,128)(2,1)S(1)}, bf16[512,4096]{1,0:T(8,128)(2,1)S(1)}, u32[]{:S(2)}, u32[]{:S(2)}) collective-permute-start(bf16[512,4096]{1,0:T(8,128)(2,1)S(1)} %copy-done), channel_id=1, source_target_pairs={{0,1},{1,0},{2,3},{3,2},{4,5},{5,4},{6,7},{7,6},{8,9},{9,8},{10,11... | collective-permute-start | bytes 12582920 | tf_op jit(solution)/shard_map/ppermute | solution.py:35
  34.6 10.9 %collective-permute-start.10 = (bf16[72,1792]{1,0:T(8,128)(2,1)S(1)}, bf16[72,1792]{1,0:T(8,128)(2,1)S(1)}, u32[]{:S(2)}, u32[]{:S(2)}) collective-permute-start(bf16[72,1792]{1,0:T(8,128)(2,1)S(1)} %get-tuple-element.169.gate_ref.refs_4_.refs_8_), channel_id=1, source_target_pairs={{0,8},{8,0},{16,24},{24,16},{1,9},{9,1},{17,25},{25,17},{2,10},{10... | collective-permute-start | bytes 774152 | tf_op jit(solution)/shard_map/ppermute | solution.py:35
  36.2 7.6 %collective-permute-start.7 = (bf16[8,4096]{1,0:T(8,128)(2,1)S(1)}, bf16[8,4096]{1,0:T(8,128)(2,1)S(1)}, u32[]{:S(2)}, u32[]{:S(2)}) collective-permute-start(bf16[8,4096]{1,0:T(8,128)(2,1)S(1)} %get-tuple-element.237), channel_id=1, source_target_pairs={{0,2},{1,3},{2,0},{3,1},{4,6},{5,7},{6,4},{7,5},{8,10},{9,11},{10,... | collective-permute-start | bytes 196616 | tf_op jit(solution)/shard_map/ppermute | solution.py:35
  37.3 8.1 %collective-permute-start.8 = (bf16[8,4096]{1,0:T(8,128)(2,1)S(1)}, bf16[8,4096]{1,0:T(8,128)(2,1)S(1)}, u32[]{:S(2)}, u32[]{:S(2)}) collective-permute-start(bf16[8,4096]{1,0:T(8,128)(2,1)S(1)} %get-tuple-element.239), channel_id=1, source_target_pairs={{0,4},{1,5},{2,6},{3,7},{4,0},{5,1},{6,2},{7,3},{8,12},{9,13},{10,... | collective-permute-start | bytes 196616 | tf_op jit(solution)/shard_map/ppermute | solution.py:35
  40.6 7.3 %collective-permute-start.11 = (bf16[72,1792]{1,0:T(8,128)(2,1)S(1)}, bf16[72,1792]{1,0:T(8,128)(2,1)S(1)}, u32[]{:S(2)}, u32[]{:S(2)}) collective-permute-start(bf16[72,1792]{1,0:T(8,128)(2,1)S(1)} %get-tuple-element.170.up_ref.refs_8_.refs_12_), channel_id=1, source_target_pairs={{0,16},{8,24},{16,0},{24,8},{1,17},{9,25},{17,1},{25,9},{2,18},{10... | collective-permute-start | bytes 774152 | tf_op jit(solution)/shard_map/ppermute | solution.py:35
  57.0 10.5 %collective-permute-start.17 = (bf16[32,4096]{1,0:T(8,128)(2,1)S(1)}, bf16[32,4096]{1,0:T(8,128)(2,1)S(1)}, u32[]{:S(2)}, u32[]{:S(2)}) collective-permute-start(bf16[32,4096]{1,0:T(8,128)(2,1)S(1)} %pad_maximum_fusion.2.refs_0_), channel_id=1, source_target_pairs={{0,8},{8,0},{16,24},{24,16},{1,9},{9,1},{17,25},{25,17},{2,10},{10... | collective-permute-start | bytes 786440 | tf_op jit(solution)/shard_map/ppermute | solution.py:35
  57.6 11.9 %collective-permute-start.18 = (bf16[32,4096]{1,0:T(8,128)(2,1)S(1)}, bf16[32,4096]{1,0:T(8,128)(2,1)S(1)}, u32[]{:S(2)}, u32[]{:S(2)}) collective-permute-start(bf16[32,4096]{1,0:T(8,128)(2,1)S(1)} %pad_maximum_fusion.2.refs_0_), channel_id=1, source_target_pairs={{0,16},{8,24},{16,0},{24,8},{1,17},{9,25},{17,1},{25,9},{2,18},{10... | collective-permute-start | bytes 786440 | tf_op jit(solution)/shard_map/ppermute | solution.py:35
  59.1 10.3 %collective-permute-start.19 = (bf16[32,4096]{1,0:T(8,128)(2,1)S(1)}, bf16[32,4096]{1,0:T(8,128)(2,1)S(1)}, u32[]{:S(2)}, u32[]{:S(2)}) collective-permute-start(bf16[32,4096]{1,0:T(8,128)(2,1)S(1)} %pad_maximum_fusion.2.refs_0_), channel_id=1, source_target_pairs={{0,24},{8,16},{16,8},{24,0},{1,25},{9,17},{17,9},{25,1},{2,26},{10... | collective-permute-start | bytes 786440 | tf_op jit(solution)/shard_map/ppermute | solution.py:35
  76.4 7.2 %collective-permute-start.20 = (bf16[32,4224]{1,0:T(8,128)(2,1)S(1)}, bf16[32,4224]{1,0:T(8,128)(2,1)S(1)}, u32[]{:S(2)}, u32[]{:S(2)}) collective-permute-start(bf16[32,4224]{1,0:T(8,128)(2,1)S(1)} %get-tuple-element.165), channel_id=1, source_target_pairs={{0,8},{8,0},{16,24},{24,16},{1,9},{9,1},{17,25},{25,17},{2,10},{10... | collective-permute-start | bytes 811016 | tf_op jit(solution)/shard_map/ppermute | solution.py:35
  78.0 11.0 %collective-permute-start.21 = (bf16[32,4224]{1,0:T(8,128)(2,1)S(1)}, bf16[32,4224]{1,0:T(8,128)(2,1)S(1)}, u32[]{:S(2)}, u32[]{:S(2)}) collective-permute-start(bf16[32,4224]{1,0:T(8,128)(2,1)S(1)} %get-tuple-element.166), channel_id=1, source_target_pairs={{0,16},{8,24},{16,0},{24,8},{1,17},{9,25},{17,1},{25,9},{2,18},{10... | collective-permute-start | bytes 811016 | tf_op jit(solution)/shard_map/ppermute | solution.py:35
  78.9 10.0 %collective-permute-start.22 = (bf16[32,4224]{1,0:T(8,128)(2,1)S(1)}, bf16[32,4224]{1,0:T(8,128)(2,1)S(1)}, u32[]{:S(2)}, u32[]{:S(2)}) collective-permute-start(bf16[32,4224]{1,0:T(8,128)(2,1)S(1)} %get-tuple-element.167), channel_id=1, source_target_pairs={{0,24},{8,16},{16,8},{24,0},{1,25},{9,17},{17,9},{25,1},{2,26},{10... | collective-permute-start | bytes 811016 | tf_op jit(solution)/shard_map/ppermute | solution.py:35
  89.1 7.3 %collective-permute-start.23 = (bf16[8,4224]{1,0:T(8,128)(2,1)S(1)}, bf16[8,4224]{1,0:T(8,128)(2,1)S(1)}, u32[]{:S(2)}, u32[]{:S(2)}) collective-permute-start(bf16[8,4224]{1,0:T(8,128)(2,1)S(1)} %get-tuple-element.231), channel_id=1, source_target_pairs={{0,2},{1,3},{2,0},{3,1},{4,6},{5,7},{6,4},{7,5},{8,10},{9,11},{10,... | collective-permute-start | bytes 202760 | tf_op jit(solution)/shard_map/ppermute | solution.py:35
  89.2 7.2 %collective-permute-start.24 = (bf16[8,4224]{1,0:T(8,128)(2,1)S(1)}, bf16[8,4224]{1,0:T(8,128)(2,1)S(1)}, u32[]{:S(2)}, u32[]{:S(2)}) collective-permute-start(bf16[8,4224]{1,0:T(8,128)(2,1)S(1)} %get-tuple-element.233), channel_id=1, source_target_pairs={{0,4},{1,5},{2,6},{3,7},{4,0},{5,1},{6,2},{7,3},{8,12},{9,13},{10,... | collective-permute-start | bytes 202760 | tf_op jit(solution)/shard_map/ppermute | solution.py:35
  111.9 12.6 %collective-permute-start.34 = (bf16[72,1792]{1,0:T(8,128)(2,1)S(1)}, bf16[72,1792]{1,0:T(8,128)(2,1)S(1)}, u32[]{:S(2)}, u32[]{:S(2)}) collective-permute-start(bf16[72,1792]{1,0:T(8,128)(2,1)S(1)} %collective-permute-done.10.refs_5_.refs_9_), channel_id=1, source_target_pairs={{0,16},{8,24},{16,0},{24,8},{1,17},{9,25},{17,1},{25,9},{2,18},{10... | collective-permute-start | bytes 774152 | tf_op jit(solution)/shard_map/ppermute | solution.py:35
  112.3 12.3 %collective-permute-start.35 = (bf16[72,1792]{1,0:T(8,128)(2,1)S(1)}, bf16[72,1792]{1,0:T(8,128)(2,1)S(1)}, u32[]{:S(2)}, u32[]{:S(2)}) collective-permute-start(bf16[72,1792]{1,0:T(8,128)(2,1)S(1)} %collective-permute-done.11.refs_10_.refs_14_), channel_id=1, source_target_pairs={{0,8},{8,0},{16,24},{24,16},{1,9},{9,1},{17,25},{25,17},{2,10},{10... | collective-permute-start | bytes 774152 | tf_op jit(solution)/shard_map/ppermute | solution.py:35
  113.9 10.6 %collective-permute-start.36 = (bf16[64,1024]{1,0:T(8,128)(2,1)S(1)}, bf16[64,1024]{1,0:T(8,128)(2,1)S(1)}, u32[]{:S(2)}, u32[]{:S(2)}) collective-permute-start(bf16[64,1024]{1,0:T(8,128)(2,1)S(1)} %get-tuple-element.187), channel_id=1, source_target_pairs={{0,24},{8,16},{16,8},{24,0},{1,25},{9,17},{17,9},{25,1},{2,26},{10... | collective-permute-start | bytes 393224 | tf_op jit(solution)/shard_map/ppermute | solution.py:35
  124.6 16.2 %collective-permute-start.37 = (bf16[64,2816]{1,0:T(8,128)(2,1)S(1)}, bf16[64,2816]{1,0:T(8,128)(2,1)S(1)}, u32[]{:S(2)}, u32[]{:S(2)}) collective-permute-start(bf16[64,2816]{1,0:T(8,128)(2,1)S(1)} %get-tuple-element.197), channel_id=1, source_target_pairs={{0,8},{8,0},{16,24},{24,16},{1,9},{9,1},{17,25},{25,17},{2,10},{10... | collective-permute-start | bytes 1081352 | tf_op jit(solution)/shard_map/ppermute | solution.py:35
  125.1 17.2 %collective-permute-start.38 = (bf16[64,2816]{1,0:T(8,128)(2,1)S(1)}, bf16[64,2816]{1,0:T(8,128)(2,1)S(1)}, u32[]{:S(2)}, u32[]{:S(2)}) collective-permute-start(bf16[64,2816]{1,0:T(8,128)(2,1)S(1)} %get-tuple-element.198), channel_id=1, source_target_pairs={{0,16},{8,24},{16,0},{24,8},{1,17},{9,25},{17,1},{25,9},{2,18},{10... | collective-permute-start | bytes 1081352 | tf_op jit(solution)/shard_map/ppermute | solution.py:35
  126.6 15.7 %collective-permute-start.39 = (bf16[64,2816]{1,0:T(8,128)(2,1)S(1)}, bf16[64,2816]{1,0:T(8,128)(2,1)S(1)}, u32[]{:S(2)}, u32[]{:S(2)}) collective-permute-start(bf16[64,2816]{1,0:T(8,128)(2,1)S(1)} %get-tuple-element.199), channel_id=1, source_target_pairs={{0,24},{8,16},{16,8},{24,0},{1,25},{9,17},{17,9},{25,1},{2,26},{10... | collective-permute-start | bytes 1081352 | tf_op jit(solution)/shard_map/ppermute | solution.py:35
  144.7 8.7 %collective-permute-start.41 = (bf16[1,64,512]{2,1,0:T(8,128)(2,1)S(1)}, bf16[1,64,512]{2,1,0:T(8,128)(2,1)S(1)}, u32[]{:S(2)}, u32[]{:S(2)}) collective-permute-start(bf16[1,64,512]{2,1,0:T(8,128)(2,1)S(1)} %get-tuple-element.234), channel_id=1, source_target_pairs={{0,2},{1,3},{2,0},{3,1},{4,6},{5,7},{6,4},{7,5},{8,10},{9,11},{10,... | collective-permute-start | bytes 196616 | tf_op jit(solution)/shard_map/ppermute | solution.py:35
  144.8 8.6 %collective-permute-start.42 = (bf16[1,64,512]{2,1,0:T(8,128)(2,1)S(1)}, bf16[1,64,512]{2,1,0:T(8,128)(2,1)S(1)}, u32[]{:S(2)}, u32[]{:S(2)}) collective-permute-start(bf16[1,64,512]{2,1,0:T(8,128)(2,1)S(1)} %get-tuple-element.236), channel_id=1, source_target_pairs={{0,4},{1,5},{2,6},{3,7},{4,0},{5,1},{6,2},{7,3},{8,12},{9,13},{10,... | collective-permute-start | bytes 196616 | tf_op jit(solution)/shard_map/ppermute | solution.py:35
  (26 other events, 170.5 us)

commit v8 on v7

--- a/solution.py
+++ b/solution.py
@@ -217,7 +217,7 @@
                 [pltpu.make_async_copy(down_ref.at[:, at], down_held.at[i], down_sems.at[i])]
             )
         hidden = None
-        for n in in_turn(copies, 4):
+        for n in in_turn(copies, 7):
             if n < parts:
                 for k, start in enumerate((gate_in, up_in)):
                     term = dot32(x_ref[n, :rows], held_ref[k, n])

time: 155 us -> 156 us (level)
  transfers between devices with their start and end apart: 44 -> 44, of which waited for: 19 -> 19; matrix products, arithmetic and copies ran while one was open for 6% -> 6% of each run, Pallas kernels for 30% -> 31%
where the time goes in v8:
time: 156 us
  Pallas kernels  54.8 us (35%)
  starting transfers between devices  51.5 us (33%)
  waiting for transfers between devices  35.2 us (23%)
  other arithmetic  8.28 us (5%)
  between operations  2.5 us (2%)
  local copies, waits for them, and re-layouts  2.41 us (2%)
    ppermute x44, starting transfers between devices, swap(): return lax.ppermute(x, axis, pairs)  51.5 us
    ppermute x44, waiting for transfers between devices, swap(): return lax.ppermute(x, axis, pairs)  35.2 us
    pallas_call x1, Pallas kernels, backward_input(): kernel_call(body, [in_smem, in_vmem, in_vmem, in_hbm, in_hbm], [shape_of(...  12.7 us
    pallas_call x1, Pallas kernels, forward_rest(): kernel_call(body, [in_smem] + [in_vmem] * 3 + [in_hbm] * 3 + [in_vmem] *...  12 us
    pallas_call x2, Pallas kernels, forward_part(): kernel_call(body, [in_smem, in_vmem, in_hbm, in_hbm] + [in_vmem] * begun,...  9.18 us
    pallas_call x1, Pallas kernels, backward_hidden(): kernel_call(body, [in_smem, in_vmem, in_vmem, in_hbm, in_vmem, in_vmem, i...  7.46 us
    pallas_call x1, Pallas kernels, score_kernel(): kernel_call(body, [in_vmem] * pieces + [in_hbm] * 2 + [in_vmem] * 3, [sha...  6.85 us
    pallas_call x1, Pallas kernels, weight_grads(): pl.pallas_call(body, in_specs=[in_vmem] * (4 * groups), out_specs=[pl.Blo...  3.72 us
  transfers between devices with their start and end apart: 44, of which 19 were waited for; matrix products, arithmetic and copies ran while one was open for 6% of the time, Pallas kernels for 31%

profile of v8, /device:TPU:0, one launch (start us, length us, event | category | flops | bytes accessed | tf_op | source)
XLA Modules:
  0.0 156.1 jit_solution(1861234106261422115)
XLA Ops:
  2.3 3.0 %collective-permute-start = (bf16[1,72,512]{2,1,0:T(8,128)(2,1)S(1)}, bf16[1,72,512]{2,1,0:T(8,128)(2,1)S(1)}, u32[]{:S(2)}, u32[]{:S(2)}) collective-permute-start(bf16[1,72,512]{2,1,0:T(8,128)(2,1)S(1)} %maximum_bitcast_fusion.x_ref), channel_id=1, source_target_pairs={{0,2},{1,3},{2,0},{3,1},{4,6},{5,7},{6,4},{7,5},{8,10},{9,11},{10,... | collective-permute-start | bytes 221192 | tf_op jit(solution)/shard_map/ppermute | solution.py:35
  5.3 2.6 %collective-permute-start.1 = (bf16[1,72,512]{2,1,0:T(8,128)(2,1)S(1)}, bf16[1,72,512]{2,1,0:T(8,128)(2,1)S(1)}, u32[]{:S(2)}, u32[]{:S(2)}) collective-permute-start(bf16[1,72,512]{2,1,0:T(8,128)(2,1)S(1)} %maximum_bitcast_fusion.x_ref), channel_id=1, source_target_pairs={{0,4},{1,5},{2,6},{3,7},{4,0},{5,1},{6,2},{7,3},{8,12},{9,13},{10,... | collective-permute-start | bytes 221192 | tf_op jit(solution)/shard_map/ppermute | solution.py:35
  8.2 3.4 %shard_map.137 = (f32[64,1792]{1,0:T(8,128)S(1)}, f32[64,1792]{1,0:T(8,128)S(1)}) custom-call(s32[8]{0:T(128)S(1)} %fusion.40.order_ref, bf16[1,72,512]{2,1,0:T(8,128)(2,1)S(1)} %maximum_bitcast_fusion.x_ref, bf16[4096,1792]{1,0:T(8,128)(2,1)} %gate_ref.7, bf16[4096,1792]{1,0:T(8,128)(2,1)} %up_ref.7), custom_call_target="tpu_custom_call" | custom-call | tf_op jit(solution)/shard_map/pallas_call | solution.py:188
  15.9 5.8 %shard_map.138 = (f32[64,1792]{1,0:T(8,128)S(1)}, f32[64,1792]{1,0:T(8,128)S(1)}) custom-call(s32[8]{0:T(128)S(1)} %fusion.40.order_ref, bf16[4,72,512]{2,1,0:T(8,128)(2,1)S(1)} %pad_maximum_fusion.1.x_ref.first_ref, bf16[4096,1792]{1,0:T(8,128)(2,1)} %gate_ref.7, bf16[4096,1792]{1,0:T(8,128)(2,1)} %up_ref.7, f32[64,1792]{1,0:T(8,128)S(1)} %get-tuple-element.116.refs_0_, ...), custom_call_target="tpu_custom_call" | custom-call | tf_op jit(solution)/shard_map/pallas_call | solution.py:188
  22.1 12.0 %shard_map.139 = (bf16[72,1792]{1,0:T(8,128)(2,1)S(1)}, bf16[72,1792]{1,0:T(8,128)(2,1)S(1)}, bf16[32,4096]{1,0:T(8,128)(2,1)S(1)}, bf16[32,4096]{1,0:T(8,128)(2,1)S(1)}) custom-call(s32[8]{0:T(128)S(1)} %fusion.40.order_ref, bf16[4,72,512]{2,1,0:T(8,128)(2,1)S(1)} %collective-permute-done.3.x_ref.second_ref, f32[64,1792]{1,0:T(8,128)S(1)} %get-tuple-element.121.gate_in, ...), custom_call_target="tpu_custom_call" | custom-call | tf_op jit(solution)/shard_map/pallas_call | solution.py:239
  38.5 1.7 %collective-permute-start.8 = (bf16[8,4096]{1,0:T(8,128)(2,1)S(1)}, bf16[8,4096]{1,0:T(8,128)(2,1)S(1)}, u32[]{:S(2)}, u32[]{:S(2)}) collective-permute-start(bf16[8,4096]{1,0:T(8,128)(2,1)S(1)} %get-tuple-element.239), channel_id=1, source_target_pairs={{0,4},{1,5},{2,6},{3,7},{4,0},{5,1},{6,2},{7,3},{8,12},{9,13},{10,... | collective-permute-start | bytes 196616 | tf_op jit(solution)/shard_map/ppermute | solution.py:35
  45.0 1.7 %collective-permute-done.8 = bf16[8,4096]{1,0:T(8,128)(2,1)S(1)} collective-permute-done((bf16[8,4096]{1,0:T(8,128)(2,1)S(1)}, bf16[8,4096]{1,0:T(8,128)(2,1)S(1)}, u32[]{:S(2)}, u32[]{:S(2)}) %collective-permute-start.8) | collective-permute-done | bytes 65568 | tf_op jit(solution)/shard_map/ppermute | solution.py:35
  46.7 2.3 %collective-permute-done.11.refs_10_.refs_14_ = bf16[72,1792]{1,0:T(8,128)(2,1)S(1)} collective-permute-done((bf16[72,1792]{1,0:T(8,128)(2,1)S(1)}, bf16[72,1792]{1,0:T(8,128)(2,1)S(1)}, u32[]{:S(2)}, u32[]{:S(2)}) %collective-permute-start.11) | collective-permute-done | bytes 258080 | tf_op jit(solution)/shard_map/ppermute | solution.py:35
  49.4 2.6 %collective-permute-start.13 = (bf16[8,4096]{1,0:T(8,128)(2,1)S(1)}, bf16[8,4096]{1,0:T(8,128)(2,1)S(1)}, u32[]{:S(2)}, u32[]{:S(2)}) collective-permute-start(bf16[8,4096]{1,0:T(8,128)(2,1)S(1)} %get-tuple-element.243), channel_id=1, source_target_pairs={{0,4},{1,5},{2,6},{3,7},{4,0},{5,1},{6,2},{7,3},{8,12},{9,13},{10,... | collective-permute-start | bytes 196616 | tf_op jit(solution)/shard_map/ppermute | solution.py:35
  56.0 2.1 %collective-permute-done.14 = bf16[8,4096]{1,0:T(8,128)(2,1)S(1)} collective-permute-done((bf16[8,4096]{1,0:T(8,128)(2,1)S(1)}, bf16[8,4096]{1,0:T(8,128)(2,1)S(1)}, u32[]{:S(2)}, u32[]{:S(2)}) %collective-permute-start.14) | collective-permute-done | bytes 65568 | tf_op jit(solution)/shard_map/ppermute | solution.py:35
  68.6 1.9 %collective-permute-done.18.refs_2_ = bf16[32,4096]{1,0:T(8,128)(2,1)S(1)} collective-permute-done((bf16[32,4096]{1,0:T(8,128)(2,1)S(1)}, bf16[32,4096]{1,0:T(8,128)(2,1)S(1)}, u32[]{:S(2)}, u32[]{:S(2)}) %collective-permute-start.18) | collective-permute-done | bytes 262176 | tf_op jit(solution)/shard_map/ppermute | solution.py:35
  70.7 6.9 %shard_map.140 = (bf16[32,4224]{1,0:T(8,128)(2,1)S(1)}, bf16[32,4224]{1,0:T(8,128)(2,1)S(1)}, bf16[32,4224]{1,0:T(8,128)(2,1)S(1)}, bf16[32,4224]{1,0:T(8,128)(2,1)S(1)}) custom-call(bf16[32,4096]{1,0:T(8,128)(2,1)S(1)} %pad_maximum_fusion.2.refs_0_, bf16[32,4096]{1,0:T(8,128)(2,1)S(1)} %collective-permute-done.17.refs_1_, ...), custom_call_target="tpu_custom_call" | custom-call | tf_op jit(solution)/shard_map/pallas_call | solution.py:325
  81.3 3.4 %collective-permute-done.20 = bf16[32,4224]{1,0:T(8,128)(2,1)S(1)} collective-permute-done((bf16[32,4224]{1,0:T(8,128)(2,1)S(1)}, bf16[32,4224]{1,0:T(8,128)(2,1)S(1)}, u32[]{:S(2)}, u32[]{:S(2)}) %collective-permute-start.20) | collective-permute-done | bytes 270368 | tf_op jit(solution)/shard_map/ppermute | solution.py:35
  84.7 5.4 %collective-permute-done.21 = bf16[32,4224]{1,0:T(8,128)(2,1)S(1)} collective-permute-done((bf16[32,4224]{1,0:T(8,128)(2,1)S(1)}, bf16[32,4224]{1,0:T(8,128)(2,1)S(1)}, u32[]{:S(2)}, u32[]{:S(2)}) %collective-permute-start.21) | collective-permute-done | bytes 270368 | tf_op jit(solution)/shard_map/ppermute | solution.py:35
  90.3 3.5 %collective-permute-start.24 = (bf16[8,4224]{1,0:T(8,128)(2,1)S(1)}, bf16[8,4224]{1,0:T(8,128)(2,1)S(1)}, u32[]{:S(2)}, u32[]{:S(2)}) collective-permute-start(bf16[8,4224]{1,0:T(8,128)(2,1)S(1)} %get-tuple-element.233), channel_id=1, source_target_pairs={{0,4},{1,5},{2,6},{3,7},{4,0},{5,1},{6,2},{7,3},{8,12},{9,13},{10,... | collective-permute-start | bytes 202760 | tf_op jit(solution)/shard_map/ppermute | solution.py:35
  97.5 2.4 %collective-permute-done.25 = bf16[8,4224]{1,0:T(8,128)(2,1)S(1)} collective-permute-done((bf16[8,4224]{1,0:T(8,128)(2,1)S(1)}, bf16[8,4224]{1,0:T(8,128)(2,1)S(1)}, u32[]{:S(2)}, u32[]{:S(2)}) %collective-permute-start.25) | collective-permute-done | bytes 67616 | tf_op jit(solution)/shard_map/ppermute | solution.py:35
  102.2 3.4 %collective-permute-start.29 = (bf16[8,4096]{1,0:T(8,128)(2,1)S(1)}, bf16[8,4096]{1,0:T(8,128)(2,1)S(1)}, u32[]{:S(2)}, u32[]{:S(2)}) collective-permute-start(bf16[8,4096]{1,0:T(8,128)(2,1)S(1)} %divide_convert_fusion), channel_id=1, source_target_pairs={{0,4},{1,5},{2,6},{3,7},{4,0},{5,1},{6,2},{7,3},{8,12},{9,13},{10,... | collective-permute-start | bytes 196616 | tf_op jit(solution)/shard_map/ppermute | solution.py:35
  108.4 3.3 %collective-permute-done.30 = bf16[8,4096]{1,0:T(8,128)(2,1)S(1)} collective-permute-done((bf16[8,4096]{1,0:T(8,128)(2,1)S(1)}, bf16[8,4096]{1,0:T(8,128)(2,1)S(1)}, u32[]{:S(2)}, u32[]{:S(2)}) %collective-permute-start.30) | collective-permute-done | bytes 65568 | tf_op jit(solution)/shard_map/ppermute | solution.py:35
  116.6 7.5 %shard_map.142 = (bf16[64,1792]{1,0:T(8,128)(2,1)S(1)}, bf16[64,1792]{1,0:T(8,128)(2,1)S(1)}, bf16[64,2816]{1,0:T(8,128)(2,1)S(1)}, bf16[64,2816]{1,0:T(8,128)(2...) custom-call(s32[4]{0:T(128)S(1)} %iota_xor_fusion.order_ref, ...), custom_call_target="tpu_custom_call" | custom-call | tf_op jit(solution)/shard_map/pallas_call | solution.py:373
  124.0 1.7 %collective-permute-done.36.refs_3_ = bf16[64,1024]{1,0:T(8,128)(2,1)S(1)} collective-permute-done((bf16[64,1024]{1,0:T(8,128)(2,1)S(1)}, bf16[64,1024]{1,0:T(8,128)(2,1)S(1)}, u32[]{:S(2)}, u32[]{:S(2)}) %collective-permute-start.36) | collective-permute-done | bytes 131104 | tf_op jit(solution)/shard_map/ppermute | solution.py:35
  129.2 12.7 %shard_map.143 = (bf16[4,64,512]{2,1,0:T(8,128)(2,1)S(1)}, bf16[4,64,512]{2,1,0:T(8,128)(2,1)S(1)}) custom-call(s32[8]{0:T(128)S(1)} %fusion.40.order_ref, bf16[64,1792]{1,0:T(8,128)(2,1)S(1)} %get-tuple-element.192.gate_grad_ref, bf16[64,1792]{1,0:T(8,128)(2,1)S(1)} %get-tuple-element.193.up_grad_ref, bf16[4096,1792]{1,0:T(8,128)(2,1)} %gate_ref.7, ...), custom_call_target="tpu_custom_call" | custom-call | tf_op jit(solution)/shard_map/pallas_call | solution.py:419
  143.4 2.3 %shard_map.144 = bf16[1792,1024]{1,0:T(8,128)(2,1)} custom-call(bf16[64,2816]{1,0:T(8,128)(2,1)S(1)} %get-tuple-element.202.refs_0_.refs_4_, bf16[64,2816]{1,0:T(8,128)(2,1)S(1)} %collective-permute-done.37.refs_1_.refs_5_, bf16[64,2816]{1,0:T(8,128)(2,1)S(1)} %collective-permute-done.38.refs_2_.refs_6_, ...), custom_call_target="tpu_custom_call" | custom-call | tf_op jit(solution)/shard_map/pallas_call | solution.py:500
  145.9 3.4 %collective-permute-start.42 = (bf16[1,64,512]{2,1,0:T(8,128)(2,1)S(1)}, bf16[1,64,512]{2,1,0:T(8,128)(2,1)S(1)}, u32[]{:S(2)}, u32[]{:S(2)}) collective-permute-start(bf16[1,64,512]{2,1,0:T(8,128)(2,1)S(1)} %get-tuple-element.236), channel_id=1, source_target_pairs={{0,4},{1,5},{2,6},{3,7},{4,0},{5,1},{6,2},{7,3},{8,12},{9,13},{10,... | collective-permute-start | bytes 196616 | tf_op jit(solution)/shard_map/ppermute | solution.py:35
  150.8 3.7 %shard_map.145 = (bf16[1024,1792]{1,0:T(8,128)(2,1)}, bf16[1024,1792]{1,0:T(8,128)(2,1)}) custom-call(bf16[64,1024]{1,0:T(8,128)(2,1)S(1)} %get-tuple-element.212.refs_0_, bf16[64,1024]{1,0:T(8,128)(2,1)S(1)} %collective-permute-done.31.refs_1_, bf16[64,1024]{1,0:T(8,128)(2,1)S(1)} %collective-permute-done.32.refs_2_, ...), custom_call_target="tpu_custom_call" | custom-call | tf_op jit(solution)/shard_map/pallas_call | solution.py:461
  (156 shorter events, 55.1 us)
Async XLA Ops:
  2.3 9.3 %collective-permute-start = (bf16[1,72,512]{2,1,0:T(8,128)(2,1)S(1)}, bf16[1,72,512]{2,1,0:T(8,128)(2,1)S(1)}, u32[]{:S(2)}, u32[]{:S(2)}) collective-permute-start(bf16[1,72,512]{2,1,0:T(8,128)(2,1)S(1)} %maximum_bitcast_fusion.x_ref), channel_id=1, source_target_pairs={{0,2},{1,3},{2,0},{3,1},{4,6},{5,7},{6,4},{7,5},{8,10},{9,11},{10,... | collective-permute-start | bytes 221192 | tf_op jit(solution)/shard_map/ppermute | solution.py:35
  5.3 7.8 %collective-permute-start.1 = (bf16[1,72,512]{2,1,0:T(8,128)(2,1)S(1)}, bf16[1,72,512]{2,1,0:T(8,128)(2,1)S(1)}, u32[]{:S(2)}, u32[]{:S(2)}) collective-permute-start(bf16[1,72,512]{2,1,0:T(8,128)(2,1)S(1)} %maximum_bitcast_fusion.x_ref), channel_id=1, source_target_pairs={{0,4},{1,5},{2,6},{3,7},{4,0},{5,1},{6,2},{7,3},{8,12},{9,13},{10,... | collective-permute-start | bytes 221192 | tf_op jit(solution)/shard_map/ppermute | solution.py:35
  14.2 7.5 %collective-permute-start.3 = (bf16[4,72,512]{2,1,0:T(8,128)(2,1)S(1)}, bf16[4,72,512]{2,1,0:T(8,128)(2,1)S(1)}, u32[]{:S(2)}, u32[]{:S(2)}) collective-permute-start(bf16[4,72,512]{2,1,0:T(8,128)(2,1)S(1)} %pad_maximum_fusion.1.x_ref.first_ref), channel_id=1, source_target_pairs={{0,1},{1,0},{2,3},{3,2},{4,5},{5,4},{6,7},{7,6},{8,9},{9,8},{10,11... | collective-permute-start | bytes 884744 | tf_op jit(solution)/shard_map/ppermute | solution.py:35
  21.7 12.4 %collective-permute-start.5 = (bf16[512,4096]{1,0:T(8,128)(2,1)S(1)}, bf16[512,4096]{1,0:T(8,128)(2,1)S(1)}, u32[]{:S(2)}, u32[]{:S(2)}) collective-permute-start(bf16[512,4096]{1,0:T(8,128)(2,1)S(1)} %copy-done), channel_id=1, source_target_pairs={{0,1},{1,0},{2,3},{3,2},{4,5},{5,4},{6,7},{7,6},{8,9},{9,8},{10,11... | collective-permute-start | bytes 12582920 | tf_op jit(solution)/shard_map/ppermute | solution.py:35
  35.7 10.9 %collective-permute-start.10 = (bf16[72,1792]{1,0:T(8,128)(2,1)S(1)}, bf16[72,1792]{1,0:T(8,128)(2,1)S(1)}, u32[]{:S(2)}, u32[]{:S(2)}) collective-permute-start(bf16[72,1792]{1,0:T(8,128)(2,1)S(1)} %get-tuple-element.169.gate_ref.refs_4_.refs_8_), channel_id=1, source_target_pairs={{0,8},{8,0},{16,24},{24,16},{1,9},{9,1},{17,25},{25,17},{2,10},{10... | collective-permute-start | bytes 774152 | tf_op jit(solution)/shard_map/ppermute | solution.py:35
  37.3 7.6 %collective-permute-start.7 = (bf16[8,4096]{1,0:T(8,128)(2,1)S(1)}, bf16[8,4096]{1,0:T(8,128)(2,1)S(1)}, u32[]{:S(2)}, u32[]{:S(2)}) collective-permute-start(bf16[8,4096]{1,0:T(8,128)(2,1)S(1)} %get-tuple-element.237), channel_id=1, source_target_pairs={{0,2},{1,3},{2,0},{3,1},{4,6},{5,7},{6,4},{7,5},{8,10},{9,11},{10,... | collective-permute-start | bytes 196616 | tf_op jit(solution)/shard_map/ppermute | solution.py:35
  38.5 8.1 %collective-permute-start.8 = (bf16[8,4096]{1,0:T(8,128)(2,1)S(1)}, bf16[8,4096]{1,0:T(8,128)(2,1)S(1)}, u32[]{:S(2)}, u32[]{:S(2)}) collective-permute-start(bf16[8,4096]{1,0:T(8,128)(2,1)S(1)} %get-tuple-element.239), channel_id=1, source_target_pairs={{0,4},{1,5},{2,6},{3,7},{4,0},{5,1},{6,2},{7,3},{8,12},{9,13},{10,... | collective-permute-start | bytes 196616 | tf_op jit(solution)/shard_map/ppermute | solution.py:35
  41.8 7.3 %collective-permute-start.11 = (bf16[72,1792]{1,0:T(8,128)(2,1)S(1)}, bf16[72,1792]{1,0:T(8,128)(2,1)S(1)}, u32[]{:S(2)}, u32[]{:S(2)}) collective-permute-start(bf16[72,1792]{1,0:T(8,128)(2,1)S(1)} %get-tuple-element.170.up_ref.refs_8_.refs_12_), channel_id=1, source_target_pairs={{0,16},{8,24},{16,0},{24,8},{1,17},{9,25},{17,1},{25,9},{2,18},{10... | collective-permute-start | bytes 774152 | tf_op jit(solution)/shard_map/ppermute | solution.py:35
  58.1 10.5 %collective-permute-start.17 = (bf16[32,4096]{1,0:T(8,128)(2,1)S(1)}, bf16[32,4096]{1,0:T(8,128)(2,1)S(1)}, u32[]{:S(2)}, u32[]{:S(2)}) collective-permute-start(bf16[32,4096]{1,0:T(8,128)(2,1)S(1)} %pad_maximum_fusion.2.refs_0_), channel_id=1, source_target_pairs={{0,8},{8,0},{16,24},{24,16},{1,9},{9,1},{17,25},{25,17},{2,10},{10... | collective-permute-start | bytes 786440 | tf_op jit(solution)/shard_map/ppermute | solution.py:35
  58.7 11.9 %collective-permute-start.18 = (bf16[32,4096]{1,0:T(8,128)(2,1)S(1)}, bf16[32,4096]{1,0:T(8,128)(2,1)S(1)}, u32[]{:S(2)}, u32[]{:S(2)}) collective-permute-start(bf16[32,4096]{1,0:T(8,128)(2,1)S(1)} %pad_maximum_fusion.2.refs_0_), channel_id=1, source_target_pairs={{0,16},{8,24},{16,0},{24,8},{1,17},{9,25},{17,1},{25,9},{2,18},{10... | collective-permute-start | bytes 786440 | tf_op jit(solution)/shard_map/ppermute | solution.py:35
  60.2 10.3 %collective-permute-start.19 = (bf16[32,4096]{1,0:T(8,128)(2,1)S(1)}, bf16[32,4096]{1,0:T(8,128)(2,1)S(1)}, u32[]{:S(2)}, u32[]{:S(2)}) collective-permute-start(bf16[32,4096]{1,0:T(8,128)(2,1)S(1)} %pad_maximum_fusion.2.refs_0_), channel_id=1, source_target_pairs={{0,24},{8,16},{16,8},{24,0},{1,25},{9,17},{17,9},{25,1},{2,26},{10... | collective-permute-start | bytes 786440 | tf_op jit(solution)/shard_map/ppermute | solution.py:35
  77.5 7.2 %collective-permute-start.20 = (bf16[32,4224]{1,0:T(8,128)(2,1)S(1)}, bf16[32,4224]{1,0:T(8,128)(2,1)S(1)}, u32[]{:S(2)}, u32[]{:S(2)}) collective-permute-start(bf16[32,4224]{1,0:T(8,128)(2,1)S(1)} %get-tuple-element.165), channel_id=1, source_target_pairs={{0,8},{8,0},{16,24},{24,16},{1,9},{9,1},{17,25},{25,17},{2,10},{10... | collective-permute-start | bytes 811016 | tf_op jit(solution)/shard_map/ppermute | solution.py:35
  79.1 11.0 %collective-permute-start.21 = (bf16[32,4224]{1,0:T(8,128)(2,1)S(1)}, bf16[32,4224]{1,0:T(8,128)(2,1)S(1)}, u32[]{:S(2)}, u32[]{:S(2)}) collective-permute-start(bf16[32,4224]{1,0:T(8,128)(2,1)S(1)} %get-tuple-element.166), channel_id=1, source_target_pairs={{0,16},{8,24},{16,0},{24,8},{1,17},{9,25},{17,1},{25,9},{2,18},{10... | collective-permute-start | bytes 811016 | tf_op jit(solution)/shard_map/ppermute | solution.py:35
  80.1 10.0 %collective-permute-start.22 = (bf16[32,4224]{1,0:T(8,128)(2,1)S(1)}, bf16[32,4224]{1,0:T(8,128)(2,1)S(1)}, u32[]{:S(2)}, u32[]{:S(2)}) collective-permute-start(bf16[32,4224]{1,0:T(8,128)(2,1)S(1)} %get-tuple-element.167), channel_id=1, source_target_pairs={{0,24},{8,16},{16,8},{24,0},{1,25},{9,17},{17,9},{25,1},{2,26},{10... | collective-permute-start | bytes 811016 | tf_op jit(solution)/shard_map/ppermute | solution.py:35
  90.2 7.3 %collective-permute-start.23 = (bf16[8,4224]{1,0:T(8,128)(2,1)S(1)}, bf16[8,4224]{1,0:T(8,128)(2,1)S(1)}, u32[]{:S(2)}, u32[]{:S(2)}) collective-permute-start(bf16[8,4224]{1,0:T(8,128)(2,1)S(1)} %get-tuple-element.231), channel_id=1, source_target_pairs={{0,2},{1,3},{2,0},{3,1},{4,6},{5,7},{6,4},{7,5},{8,10},{9,11},{10,... | collective-permute-start | bytes 202760 | tf_op jit(solution)/shard_map/ppermute | solution.py:35
  90.3 7.2 %collective-permute-start.24 = (bf16[8,4224]{1,0:T(8,128)(2,1)S(1)}, bf16[8,4224]{1,0:T(8,128)(2,1)S(1)}, u32[]{:S(2)}, u32[]{:S(2)}) collective-permute-start(bf16[8,4224]{1,0:T(8,128)(2,1)S(1)} %get-tuple-element.233), channel_id=1, source_target_pairs={{0,4},{1,5},{2,6},{3,7},{4,0},{5,1},{6,2},{7,3},{8,12},{9,13},{10,... | collective-permute-start | bytes 202760 | tf_op jit(solution)/shard_map/ppermute | solution.py:35
  113.1 12.6 %collective-permute-start.34 = (bf16[72,1792]{1,0:T(8,128)(2,1)S(1)}, bf16[72,1792]{1,0:T(8,128)(2,1)S(1)}, u32[]{:S(2)}, u32[]{:S(2)}) collective-permute-start(bf16[72,1792]{1,0:T(8,128)(2,1)S(1)} %collective-permute-done.10.refs_5_.refs_9_), channel_id=1, source_target_pairs={{0,16},{8,24},{16,0},{24,8},{1,17},{9,25},{17,1},{25,9},{2,18},{10... | collective-permute-start | bytes 774152 | tf_op jit(solution)/shard_map/ppermute | solution.py:35
  113.5 12.2 %collective-permute-start.35 = (bf16[72,1792]{1,0:T(8,128)(2,1)S(1)}, bf16[72,1792]{1,0:T(8,128)(2,1)S(1)}, u32[]{:S(2)}, u32[]{:S(2)}) collective-permute-start(bf16[72,1792]{1,0:T(8,128)(2,1)S(1)} %collective-permute-done.11.refs_10_.refs_14_), channel_id=1, source_target_pairs={{0,8},{8,0},{16,24},{24,16},{1,9},{9,1},{17,25},{25,17},{2,10},{10... | collective-permute-start | bytes 774152 | tf_op jit(solution)/shard_map/ppermute | solution.py:35
  115.1 10.6 %collective-permute-start.36 = (bf16[64,1024]{1,0:T(8,128)(2,1)S(1)}, bf16[64,1024]{1,0:T(8,128)(2,1)S(1)}, u32[]{:S(2)}, u32[]{:S(2)}) collective-permute-start(bf16[64,1024]{1,0:T(8,128)(2,1)S(1)} %get-tuple-element.187), channel_id=1, source_target_pairs={{0,24},{8,16},{16,8},{24,0},{1,25},{9,17},{17,9},{25,1},{2,26},{10... | collective-permute-start | bytes 393224 | tf_op jit(solution)/shard_map/ppermute | solution.py:35
  125.7 16.2 %collective-permute-start.37 = (bf16[64,2816]{1,0:T(8,128)(2,1)S(1)}, bf16[64,2816]{1,0:T(8,128)(2,1)S(1)}, u32[]{:S(2)}, u32[]{:S(2)}) collective-permute-start(bf16[64,2816]{1,0:T(8,128)(2,1)S(1)} %get-tuple-element.197), channel_id=1, source_target_pairs={{0,8},{8,0},{16,24},{24,16},{1,9},{9,1},{17,25},{25,17},{2,10},{10... | collective-permute-start | bytes 1081352 | tf_op jit(solution)/shard_map/ppermute | solution.py:35
  126.2 17.2 %collective-permute-start.38 = (bf16[64,2816]{1,0:T(8,128)(2,1)S(1)}, bf16[64,2816]{1,0:T(8,128)(2,1)S(1)}, u32[]{:S(2)}, u32[]{:S(2)}) collective-permute-start(bf16[64,2816]{1,0:T(8,128)(2,1)S(1)} %get-tuple-element.198), channel_id=1, source_target_pairs={{0,16},{8,24},{16,0},{24,8},{1,17},{9,25},{17,1},{25,9},{2,18},{10... | collective-permute-start | bytes 1081352 | tf_op jit(solution)/shard_map/ppermute | solution.py:35
  127.7 15.7 %collective-permute-start.39 = (bf16[64,2816]{1,0:T(8,128)(2,1)S(1)}, bf16[64,2816]{1,0:T(8,128)(2,1)S(1)}, u32[]{:S(2)}, u32[]{:S(2)}) collective-permute-start(bf16[64,2816]{1,0:T(8,128)(2,1)S(1)} %get-tuple-element.199), channel_id=1, source_target_pairs={{0,24},{8,16},{16,8},{24,0},{1,25},{9,17},{17,9},{25,1},{2,26},{10... | collective-permute-start | bytes 1081352 | tf_op jit(solution)/shard_map/ppermute | solution.py:35
  145.8 8.7 %collective-permute-start.41 = (bf16[1,64,512]{2,1,0:T(8,128)(2,1)S(1)}, bf16[1,64,512]{2,1,0:T(8,128)(2,1)S(1)}, u32[]{:S(2)}, u32[]{:S(2)}) collective-permute-start(bf16[1,64,512]{2,1,0:T(8,128)(2,1)S(1)} %get-tuple-element.234), channel_id=1, source_target_pairs={{0,2},{1,3},{2,0},{3,1},{4,6},{5,7},{6,4},{7,5},{8,10},{9,11},{10,... | collective-permute-start | bytes 196616 | tf_op jit(solution)/shard_map/ppermute | solution.py:35
  145.9 8.6 %collective-permute-start.42 = (bf16[1,64,512]{2,1,0:T(8,128)(2,1)S(1)}, bf16[1,64,512]{2,1,0:T(8,128)(2,1)S(1)}, u32[]{:S(2)}, u32[]{:S(2)}) collective-permute-start(bf16[1,64,512]{2,1,0:T(8,128)(2,1)S(1)} %get-tuple-element.236), channel_id=1, source_target_pairs={{0,4},{1,5},{2,6},{3,7},{4,0},{5,1},{6,2},{7,3},{8,12},{9,13},{10,... | collective-permute-start | bytes 196616 | tf_op jit(solution)/shard_map/ppermute | solution.py:35
  (26 other events, 170.5 us)
